TPU v7x, 128 devices: a whole 4x4x4 slice. The times are simulated.
128 devices in a mesh: dp: 4 (over x), expert: 2 (over core), mp: 16 (over z, y).
Axes of the slice: x: 4, y: 4, z: 4, core: 2. Of those that a mesh axis runs over, the one named last changes fastest.
Arguments:
- block_input: bfloat16 [16384, 1024], P(('dp', 'expert', 'mp')), may hold values from -6 to 6
- attn_gain: float32 [1024], replicated, may hold values from 0.5 to 1.5
- qkv_weight: float32 [1024, 3072], replicated, may hold values from -0.1875 to 0.1875
- out_weight: float32 [1024, 1024], replicated, may hold values from -3 to 3
- moe_gain: float32 [1024], replicated, may hold values from 0.5 to 1.5
- router_weight: float32 [1024, 8], replicated, may hold values from -0.125 to 0.125
- gate_weight: float32 [8, 1024, 2816], P('expert', 'dp', 'mp'), may hold values from -0.1875 to 0.1875
- up_weight: float32 [8, 1024, 2816], P('expert', 'dp', 'mp'), may hold values from -0.1875 to 0.1875
- down_weight: float32 [8, 2816, 1024], P('expert', 'mp', 'dp'), may hold values from -0.15625 to 0.15625
- routes: int32 [16384, 2], P(('dp', 'expert', 'mp')), may hold values from 0 to 7, as said below
- slot_index: int32 [16384, 2], P(('dp', 'expert', 'mp')), may hold values from 0 to 127, as said below
- cotangent: bfloat16 [16384, 1024], P(('dp', 'expert', 'mp')), may hold values from -6 to 6
Outputs:
- block_output: bfloat16 [16384, 1024], P(('dp', 'expert', 'mp'))
- input_grad: float32 [16384, 1024], P(('dp', 'expert', 'mp'))
- attn_gain_grad: float32 [1024], replicated
- qkv_grad: float32 [1024, 3072], replicated
- out_grad: float32 [1024, 1024], replicated
- moe_gain_grad: float32 [1024], replicated
- router_grad: float32 [1024, 8], replicated
- gate_grad: float32 [8, 1024, 2816], P('expert', 'dp', 'mp')
- up_grad: float32 [8, 1024, 2816], P('expert', 'dp', 'mp')
- down_grad: float32 [8, 2816, 1024], P('expert', 'mp', 'dp')
Inputs may be any that keep to these rules, and one draw needn't show every extreme that they name: routes[t, 0] and routes[t, 1] differ; in one aligned block of 128 rows, chosen at random, every token names one common expert; in the other blocks the routes vary. slot_index[t, j] is the number of pairs (t2, j2) in the same aligned block of 128 rows, with t2 < t, or t2 = t and j2 < j, whose expert equals routes[t, j].
All inputs are finite; a program needn't handle non-finite values.
Results may differ from a plain program's by a relative error of at most 0.019.
Values may be sent and summed in bfloat16 or wider, within the bound.
A program may use at most 256 MiB of HBM per device.

v0:
```python
from functools import partial

import jax
import jax.numpy as jnp
from jax import lax
from jax.sharding import PartitionSpec as P

HEADS = 16


EPSILON = 1e-06
HIGHEST = lax.Precision.HIGHEST


def gather_turned(arrays, axis, dims):
    turned = [jnp.moveaxis(a, dim, 0) for a, dim in zip(arrays, dims)]
    both = jnp.concatenate([t.reshape(len(t), -1) for t in turned], axis=1)
    filled, at, outs = (lax.all_gather(both, axis, axis=0, tiled=True), 0, [])
    for t, dim in zip(turned, dims):
        share = filled[:, at : at + t[0].size].reshape(-1, *t.shape[1:])
        outs.append(jnp.moveaxis(share, 0, dim))
        at += t[0].size
    return tuple(outs)


def sent_together(arrays, axis, dim, along):
    ends, at = ([], 0)
    for a in arrays[:-1]:
        at += a.shape[along]
        ends.append(at)
    both = jnp.concatenate(arrays, axis=along)
    return tuple(
        jnp.split(lax.psum_scatter(both, axis, scatter_dimension=dim, tiled=True), ends, axis=along)
    )


def rms_norm(values, gain):
    return values * lax.rsqrt(jnp.mean(values * values, axis=-1, keepdims=True) + EPSILON) * gain


def gating(moe_in, router_weight, routes):
    logits = jnp.dot(moe_in, router_weight, precision=HIGHEST, preferred_element_type=jnp.float32)
    probs = jax.nn.softmax(logits, axis=-1)
    chosen = jnp.take_along_axis(probs, routes, axis=1)
    return chosen / jnp.sum(chosen, axis=1, keepdims=True)


def geglu(gate_pre, up_pre):
    return jax.nn.gelu(gate_pre, approximate=True) * up_pre


def fetch_experts(gate_weight, up_weight, down_weight):
    return gather_turned(
        (
            gate_weight.astype(jnp.bfloat16),
            up_weight.astype(jnp.bfloat16),
            down_weight.astype(jnp.bfloat16),
        ),
        "dp",
        (1, 1, 2),
    )


def to_heads(rows):
    return lax.all_to_all(rows, "mp", split_axis=2, concat_axis=0, tiled=True)


def to_tokens(rows):
    return lax.all_to_all(rows, "mp", split_axis=0, concat_axis=2, tiled=True)


def attention_forward(queries, key_heads, value_heads):
    router_scores = (
        jnp.einsum("qhd,khd->hqk", queries, key_heads, preferred_element_type=jnp.float32) * 0.125
    )
    log_total = jax.nn.logsumexp(router_scores, axis=-1, keepdims=True)
    probs_low = jnp.exp(router_scores - log_total).astype(jnp.bfloat16)
    context = jnp.einsum("hqk,khd->qhd", probs_low, value_heads, preferred_element_type=jnp.float32)
    return (context.astype(jnp.bfloat16), log_total)


def attention_backward(queries, key_heads, value_heads, log_total, context_cot):
    scores_again = (
        jnp.einsum("qhd,khd->hqk", queries, key_heads, preferred_element_type=jnp.float32) * 0.125
    )
    probs_full = jnp.exp(scores_again - log_total)
    probs_again = probs_full.astype(jnp.bfloat16)
    probs_cot = jnp.einsum(
        "qhd,khd->hqk", context_cot, value_heads, preferred_element_type=jnp.float32
    )
    inner = jnp.sum(probs_full * probs_cot, axis=-1, keepdims=True)
    score_cot = (probs_full * (probs_cot - inner)).astype(jnp.bfloat16)
    query_cot = (
        jnp.einsum("hqk,khd->qhd", score_cot, key_heads, preferred_element_type=jnp.float32) * 0.125
    )
    key_part = (
        jnp.einsum("hqk,qhd->khd", score_cot, queries, preferred_element_type=jnp.float32) * 0.125
    )
    value_part = jnp.einsum(
        "hqk,qhd->khd", probs_again, context_cot, preferred_element_type=jnp.float32
    )
    return (query_cot, key_part, value_part)


def body(
    block_input,
    attn_gain,
    qkv_weight,
    out_weight,
    moe_gain,
    router_weight,
    gate_weight,
    up_weight,
    down_weight,
    routes,
    slot_index,
    cotangent,
):
    tok_rows, width = block_input.shape
    head_count = HEADS
    head_size = width // head_count
    group_count = lax.axis_size("expert")
    local_experts = gate_weight.shape[0]
    all_experts = local_experts * group_count
    capacity = max(2, (10 * tok_rows + 4 * all_experts - 1) // (4 * all_experts))
    inputs = block_input.astype(jnp.float32)
    qkv_low = qkv_weight.astype(jnp.bfloat16)
    out_low = out_weight.astype(jnp.bfloat16)
    normed, norm_back = jax.vjp(rms_norm, inputs, attn_gain)
    normed_low = normed.astype(jnp.bfloat16)
    packed = jnp.dot(normed_low, qkv_low, preferred_element_type=jnp.float32).astype(jnp.bfloat16)
    by_head = to_heads(packed.reshape(tok_rows, 3, head_count, head_size))
    queries = by_head[:, 0]
    key_heads = by_head[:, 1]
    value_heads = by_head[:, 2]
    context_here, log_total = attention_forward(queries, key_heads, value_heads)
    context = to_tokens(context_here[:, None]).reshape(tok_rows, width)
    branch = jnp.dot(context, out_low, preferred_element_type=jnp.float32)
    middle = inputs + branch
    moe_in, moe_back = jax.vjp(rms_norm, middle, moe_gain)
    gates, gate_back = jax.vjp(partial(gating, routes=routes), moe_in, router_weight)
    valid = slot_index < capacity
    target = jnp.where(valid, routes * capacity + slot_index, all_experts * capacity).reshape(-1)
    fetch_at = jnp.where(valid, routes * capacity + slot_index, 0)
    keep_mask = valid.astype(jnp.float32)
    moe_low = moe_in.astype(jnp.bfloat16)
    pair_rows = jnp.repeat(moe_low, 2, axis=0)
    send_rows = (
        jnp.zeros((all_experts * capacity, width), jnp.bfloat16)
        .at[target]
        .set(pair_rows, mode="drop")
    )
    arrived = lax.all_to_all(
        send_rows.reshape(group_count, local_experts, capacity, width),
        "expert",
        split_axis=0,
        concat_axis=0,
        tiled=True,
    )
    expert_rows = lax.all_gather(arrived, "mp", axis=0, tiled=True)
    weights_now = fetch_experts(gate_weight, up_weight, down_weight)
    gate_pre = jnp.einsum(
        "secd,edf->secf", expert_rows, weights_now[0], preferred_element_type=jnp.float32
    )
    up_pre = jnp.einsum(
        "secd,edf->secf", expert_rows, weights_now[1], preferred_element_type=jnp.float32
    )
    hidden, geglu_back = jax.vjp(geglu, gate_pre, up_pre)
    hidden_low = hidden.astype(jnp.bfloat16)
    partial_out = jnp.einsum(
        "secf,efd->secd", hidden_low, weights_now[2], preferred_element_type=jnp.float32
    )
    summed = lax.psum_scatter(
        partial_out.astype(jnp.bfloat16), "mp", scatter_dimension=0, tiled=True
    )
    returned = lax.all_to_all(summed, "expert", split_axis=0, concat_axis=0, tiled=True)
    returned = returned.reshape(all_experts * capacity, width)
    fetched = jnp.take(returned, fetch_at, axis=0).astype(jnp.float32) * keep_mask[:, :, None]
    mixture = jnp.sum(gates[:, :, None] * fetched, axis=1)
    block_output = (middle + mixture).astype(jnp.bfloat16)
    upstream = cotangent.astype(jnp.float32)
    gate_cot = jnp.sum(upstream[:, None, :] * fetched, axis=2)
    row_cot = (
        (gates[:, :, None] * upstream[:, None, :]).astype(jnp.bfloat16).reshape(2 * tok_rows, width)
    )
    send_cot = (
        jnp.zeros((all_experts * capacity, width), jnp.bfloat16)
        .at[target]
        .set(row_cot, mode="drop")
    )
    cot_arrived = lax.all_to_all(
        send_cot.reshape(group_count, local_experts, capacity, width),
        "expert",
        split_axis=0,
        concat_axis=0,
        tiled=True,
    )
    cot_rows = lax.all_gather(cot_arrived, "mp", axis=0, tiled=True)
    weights_back = fetch_experts(gate_weight, up_weight, down_weight)
    hidden_cot = jnp.einsum(
        "secd,efd->secf", cot_rows, weights_back[2], preferred_element_type=jnp.float32
    )
    down_term = jnp.einsum(
        "secf,secd->efd", hidden_low, cot_rows, preferred_element_type=jnp.float32
    )
    gate_cot_pre, up_cot_pre = geglu_back(hidden_cot)
    gate_cot_low = gate_cot_pre.astype(jnp.bfloat16)
    up_cot_low = up_cot_pre.astype(jnp.bfloat16)
    gate_term = jnp.einsum(
        "secd,secf->edf", expert_rows, gate_cot_low, preferred_element_type=jnp.float32
    )
    up_term = jnp.einsum(
        "secd,secf->edf", expert_rows, up_cot_low, preferred_element_type=jnp.float32
    )
    rows_cot = jnp.einsum(
        "secf,edf->secd", gate_cot_low, weights_back[0], preferred_element_type=jnp.float32
    )
    rows_cot = rows_cot + jnp.einsum(
        "secf,edf->secd", up_cot_low, weights_back[1], preferred_element_type=jnp.float32
    )
    rows_summed = lax.psum_scatter(
        rows_cot.astype(jnp.bfloat16), "mp", scatter_dimension=0, tiled=True
    )
    rows_back = lax.all_to_all(rows_summed, "expert", split_axis=0, concat_axis=0, tiled=True)
    rows_back = rows_back.reshape(all_experts * capacity, width)
    moe_cot = jnp.sum(
        jnp.take(rows_back, fetch_at, axis=0).astype(jnp.float32) * keep_mask[:, :, None], axis=1
    )
    router_in_cot, router_term = gate_back(gate_cot)
    middle_norm_cot, moe_gain_term = moe_back(moe_cot + router_in_cot)
    middle_cot = upstream + middle_norm_cot
    branch_cot = middle_cot.astype(jnp.bfloat16)
    out_term = jnp.einsum("td,tf->df", context, branch_cot, preferred_element_type=jnp.float32)
    context_cot = jnp.einsum("tf,df->td", branch_cot, out_low, preferred_element_type=jnp.float32)
    context_cot = context_cot.astype(jnp.bfloat16).reshape(tok_rows, head_count, head_size)
    cot_heads = to_heads(context_cot[:, None])[:, 0]
    query_cot, key_part, value_part = attention_backward(
        queries, key_heads, value_heads, log_total, cot_heads
    )
    stacked = jnp.stack(
        [
            query_cot.astype(jnp.bfloat16),
            key_part.astype(jnp.bfloat16),
            value_part.astype(jnp.bfloat16),
        ],
        axis=1,
    )
    packed_cot = to_tokens(stacked).reshape(tok_rows, 3 * width)
    qkv_term = jnp.einsum("td,tf->df", normed_low, packed_cot, preferred_element_type=jnp.float32)
    normed_cot = jnp.einsum("tf,df->td", packed_cot, qkv_low, preferred_element_type=jnp.float32)
    input_norm_cot, attn_gain_term = norm_back(normed_cot)
    input_grad = middle_cot + input_norm_cot
    shared = lax.psum(
        (attn_gain_term, qkv_term, out_term, moe_gain_term, router_term), ("dp", "expert", "mp")
    )
    expert_sums = (
        *tuple(
            (
                part.astype(jnp.float32)
                for part in sent_together(
                    (gate_term.astype(jnp.bfloat16), up_term.astype(jnp.bfloat16)), "dp", 1, 0
                )
            )
        ),
        lax.psum_scatter(
            down_term.astype(jnp.bfloat16), "dp", scatter_dimension=2, tiled=True
        ).astype(jnp.float32),
    )
    return (
        block_output,
        input_grad,
        shared[0],
        shared[1],
        shared[2],
        shared[3],
        shared[4],
        expert_sums[0],
        expert_sums[1],
        expert_sums[2],
    )


def solution(mesh):
    placed = (
        P(("dp", "expert", "mp"), None),
        P(),
        P(),
        P(),
        P(),
        P(),
        P("expert", "dp", "mp"),
        P("expert", "dp", "mp"),
        P("expert", "mp", "dp"),
        P(("dp", "expert", "mp"), None),
        P(("dp", "expert", "mp"), None),
        P(("dp", "expert", "mp"), None),
    )
    return jax.shard_map(
        body,
        mesh=mesh,
        in_specs=placed,
        out_specs=(
            P(("dp", "expert", "mp"), None),
            P(("dp", "expert", "mp"), None),
            P(),
            P(),
            P(),
            P(),
            P(),
            P("expert", "dp", "mp"),
            P("expert", "dp", "mp"),
            P("expert", "mp", "dp"),
        ),
        check_vma=False,
    )
```

profile of v0, /device:TPU:1, one launch (start us, length us, event | category | flops | bytes accessed | tf_op | source)
XLA Modules:
  0.0 921.8 jit_solution(6296135521882199452)
XLA Ops:
  12.0 5.6 convolution_convert_fusion
  18.1 21.9 %all_to_all.83 = bf16[128,3,16,64]{0,3,1,2:T(8,128)(2,1)S(1)} all-to-all(bf16[128,3,16,64]{0,3,1,2:T(8,128)(2,1)S(1)} %copy.157), channel_id=1, replica_groups=mesh['dp'=4,'expert'=2,'mp'=16] {'mp'}, dimensions={2} | all-to-all | bytes 1572864 | tf_op jit(solution)/shard_map/all_to_all | solution.py:65
  40.1 8.2 multiply_reduce_fusion.1
  48.4 8.6 exponential_reduce_fusion
  57.0 7.6 fusion.20
  67.3 3.6 all-to-all-start.1
  71.5 7.0 all-to-all-done.1
  79.9 2.8 multiply_reduce_fusion.7
  85.2 6.6 all_to_all.84
  99.2 4.3 all_to_all.85
  104.8 4.0 fusion.68
  108.8 61.8 %all-gather.6.cloned.1.call-done = bf16[32,4,40,1024]{3,2,0,1:T(8,128)(2,1)} async-done(((bf16[2,4,40,1024]{3,2,0,1:T(8,128)(2,1)}), bf16[32,4,40,1024]{3,2,0,1:T(8,128)(2,1)}) %all-gather.6.cloned.1.call-update) | async-done | bytes 10485776 | tf_op jit(solution)/shard_map/all_gather | solution.py:160
  170.6 8.1 fusion.71
  178.7 5.0 fusion.70
  183.7 69.7 %all-gather.8.cloned.1.call-done = bf16[32,4,40,1024]{3,2,0,1:T(8,128)(2,1)} async-done(((bf16[2,4,40,1024]{3,2,0,1:T(8,128)(2,1)}), bf16[32,4,40,1024]{3,2,0,1:T(8,128)(2,1)}) %all-gather.8.cloned.1.call-update) | async-done | bytes 10485776 | tf_op jit(solution)/shard_map/all_gather | solution.py:198
  253.4 12.4 %fusion.9 = (bf16[32,4,40,176]{3,2,0,1:T(8,128)(2,1)S(1)}, bf16[32,4,40,176]{3,2,0,1:T(8,128)(2,1)S(1)}, bf16[32,4,40,176]{3,2,0,1:T(8,128)(2,1)}) fusion(f32[4,176,32,40]{1,3,2,0:T(8,128)} %fusion.70, f32[4,176,32,40]{1,3,2,0:T(8,128)} %fusion.71, bf16[4,176,1024,1]{2,1,3,0:T(8,128)(2,1)} %bitcast.238, ...), kind=kOutput, calls=%fused_computation.26 | convolution fusion | flops 1868922880 | bytes 24543232 | tf_op jit(solution)/shard_map/secd,efd->secf/dot_general | solution.py:200
  265.8 8.3 convert_bitcast_fusion
  274.1 8.5 fusion.72
  282.7 11.8 %fusion.1 = bf16[32,4,40,1024]{3,2,0,1:T(8,128)(2,1)} fusion(f32[4,1024,32,40]{1,3,2,0:T(8,128)} %fusion.72, bf16[4,1024,176,1]{1,2,3,0:T(8,128)(2,1)} %bitcast.227, bf16[32,4,40,176]{3,2,0,1:T(8,128)(2,1)S(1)} %get-tuple-element.29), kind=kOutput, calls=%fused_computation.13 | convolution fusion | flops 1855979520 | bytes 34701312 | tf_op jit(solution)/shard_map/secf,edf->secd/dot_general | solution.py:218
  298.3 8.4 bitcast_convert_fusion
  306.7 7.3 bitcast_convert_fusion.1
  314.0 244.0 %all-reduce.10.cloned.1.call-done = (bf16[32,4,40,1024]{3,2,0,1:T(8,128)(2,1)}, bf16[32,4,40,1024]{3,2,0,1:T(8,128)(2,1)}) async-done(((bf16[32,4,40,1024]{3,2,0,1:T(8,128)(2,1)}, bf16[32,4,40,1024]{3,2,0,1:T(8,128)(2,1)}), (bf16[32,4,40,1024]{3,2,0,1:T(8,128)(2,1)}, bf16[32,4,40,1024]{3,2,0,1:T(8,128)(2,1)})) %all-reduce.10.cloned.1.call-update) | async-done | bytes 20971536
  560.4 4.6 all_to_all.86
  567.2 4.4 all_to_all.87
  573.0 5.6 multiply_reduce_fusion.2
  579.0 11.1 %scatter_fusion = f32[128,8]{0,1:T(8,128)S(1)} fusion(f32[128,8]{0,1:T(8,128)S(1)} %broadcast_in_dim.66, s32[256]{0:T(256)S(1)} %reshape.347, f32[256]{0:T(256)S(1)} %reshape.349), kind=kCustom, calls=%fused_computation.5 | custom fusion | flops 256 | bytes 5120 | tf_op jit(solution)/shard_map/transpose(jvp(jit(take_along_axis)))/scatter-add | solution.py:44
  590.3 2.0 multiply_reduce_fusion.5
  596.8 5.1 all-to-all-start.6
  602.2 7.2 bitcast_convert_fusion.2
  609.4 3.7 pad_maximum_fusion
  613.3 13.7 %multiply_reduce_fusion = (f32[2048]{0:T(1024)S(1)}, f32[2048,2048]{0,1:T(8,128)}) fusion(f32[2048,2048]{0,1:T(8,128)} %get-tuple-element.43, f32[2048]{0:T(1024)S(1)} %copy-done.24, bf16[2048,3,1,64]{0,3,1,2:T(8,128)(2,1)S(1)} %copy-done.10, bf16[8,8,16,128]{3,2,1,0:T(8,128)(2,1)S(1)} %bitcast.228), kind=kOutput, calls=%fused_computation.8 | convolution fusion | flops 553646080 | bytes 34095104 | tf_op jit(solution)/shard_map/qhd,khd->hqk/dot_general | solution.py:88
  629.8 8.4 multiply_convert_fusion
  638.2 2.7 fusion.18
  642.4 3.2 fusion.21
  646.6 2.9 copy.183
  649.5 2.5 reshape.383
  651.9 6.7 all-to-all-start.7
  659.0 3.7 fusion.52
  662.7 9.0 all-to-all-done.7
  671.6 2.9 reshape.384
  674.5 2.2 copy.193
  676.7 7.8 fusion.55
  686.6 2.3 slice_convert_fusion
  689.4 7.7 fusion.29
  697.1 65.5 %all-reduce.2 = (f32[1024]{0:T(1024)}, f32[1024]{0:T(1024)}, f32[1024,8]{0,1:T(8,128)}) all-reduce(f32[1024]{0:T(1024)S(1)} %get-tuple-element.13, f32[1024]{0:T(1024)S(1)} %get-tuple-element.11, f32[1024,8]{0,1:T(8,128)S(1)} %fusion.36), channel_id=1, replica_groups=mesh['dp'=4,'expert'=2,'mp'=16] {'dp','expert','mp'}, use_global_device_ids=true, to_apply=%region_21.23 | all-reduce | flops 10240 | bytes 81920 | tf_op jit(solution)/shard_map/psum | solution.py:253
  763.6 137.8 %all-reduce.8.cloned.1.call-done = (f32[1024,3072]{1,0:T(8,128)}, f32[1024,1024]{1,0:T(8,128)}) async-done(((f32[1024,3072]{1,0:T(8,128)}, f32[1024,1024]{1,0:T(8,128)}), (f32[1024,3072]{1,0:T(8,128)}, f32[1024,1024]{1,0:T(8,128)})) %all-reduce.8.cloned.1.call-update) | async-done | bytes 16777232 | tf_op jit(solution)/shard_map/psum | solution.py:253
  901.4 11.1 %copy.218 = f32[1024,3072]{1,0:T(8,128)} copy(f32[1024,3072]{1,0:T(8,128)} %get-tuple-element.55) | data formatting | bytes 25165824
  912.5 2.0 copy.219
  (203 shorter events, 44.3 us)
Async XLA Ops:
  7.2 86.9 %copy-start = (f32[1024,8]{0,1:T(8,128)S(1)}, f32[1024,8]{0,1:T(8,128)}, u32[]{:S(2)}) copy-start(f32[1024,8]{0,1:T(8,128)} %param.19) | copy-start | bytes 98308
  7.2 97.6 %all-gather.4.cloned.1.call-start = ((), (), s32[]{:S(2)}) async-start(), calls=%async_computation.10 | async-start | bytes 5406720 | tf_op jit(solution)/shard_map/all_gather | solution.py:18
  12.0 5.7 copy-start.40
  12.0 5.7 copy-start.35
  40.1 16.8 %copy-start.9 = (bf16[2048,3,1,64]{0,3,1,2:T(8,128)(2,1)}, bf16[2048,3,1,64]{0,3,1,2:T(8,128)(2,1)S(1)}, u32[]{:S(2)}) copy-start(bf16[2048,3,1,64]{0,3,1,2:T(8,128)(2,1)S(1)} %copy_bitcast_fusion) | copy-start | bytes 2359300
  57.0 7.6 copy-start.23
  57.0 14.2 %copy-start.34 = (s32[128,2]{0,1:T(2,128)S(1)}, s32[128,2]{0,1:T(2,128)}, u32[]{:S(2)}) copy-start(s32[128,2]{0,1:T(2,128)} %param.23) | copy-start | bytes 3076
  57.0 14.2 %copy-start.39 = (s32[128,2]{0,1:T(2,128)S(1)}, s32[128,2]{0,1:T(2,128)}, u32[]{:S(2)}) copy-start(s32[128,2]{0,1:T(2,128)} %param.24) | copy-start | bytes 3076
  66.1 16.6 %copy-start.30 = (f32[1024]{0:T(1024)S(1)}, f32[1024]{0:T(1024)}, u32[]{:S(2)}) copy-start(f32[1024]{0:T(1024)} %param.18) | copy-start | bytes 12292
  67.3 11.2 %all-to-all-start.1 = ((bf16[16,2,4096]{2,1,0:T(2,128)(2,1)}), bf16[16,2,4096]{2,1,0:T(2,128)(2,1)S(1)}, u32[]{:S(2)}, u32[]{:S(2)}) async-start(bf16[16,2,4096]{2,1,0:T(2,128)(2,1)} %reshape.381), calls=%async_computation.1 | async-start | bytes 524288 | tf_op jit(solution)/shard_map/all_to_all | solution.py:69
  70.9 99.7 %all-gather.6.cloned.1.call-start = ((), (), s32[]{:S(2)}) async-start(), calls=%async_computation.11 | async-start | bytes 11141120 | tf_op jit(solution)/shard_map/all_gather | solution.py:160
  79.8 13.2 %copy-start.18 = (bf16[128,1024]{1,0:T(8,128)(2,1)S(1)}, bf16[128,1024]{1,0:T(8,128)(2,1)}, u32[]{:S(2)}) copy-start(bf16[128,1024]{1,0:T(8,128)(2,1)} %param.25) | copy-start | bytes 786436
  82.7 10.7 %copy-start.42 = (f32[128]{0:T(128)}, f32[128]{0:T(128)S(1)}, u32[]{:S(2)}) copy-start(f32[128]{0:T(128)S(1)} %get-tuple-element.44) | copy-start | bytes 1540
  82.7 12.0 %copy-start.2 = (f32[128,1024]{1,0:T(8,128)}, f32[128,1024]{1,0:T(8,128)S(1)}, u32[]{:S(2)}) copy-start(f32[128,1024]{1,0:T(8,128)S(1)} %get-tuple-element.45) | copy-start | bytes 1572868
  82.7 12.0 %copy-start.37 = (f32[128]{0:T(128)}, f32[128]{0:T(128)S(1)}, u32[]{:S(2)}) copy-start(f32[128]{0:T(128)S(1)} %fusion.63) | copy-start | bytes 1540
  92.8 160.7 %all-gather.8.cloned.1.call-start = ((), (), s32[]{:S(2)}) async-start(), calls=%async_computation.12 | async-start | bytes 11141120 | tf_op jit(solution)/shard_map/all_gather | solution.py:198
  104.3 453.7 %all-reduce.10.cloned.1.call-start = ((), (), s32[]{:S(2)}) async-start(), calls=%async_computation.16 | async-start | bytes 41943040
  108.8 69.9 %copy-start.16 = (bf16[1024,704]{0,1:T(8,128)(2,1)}, bf16[1024,704]{0,1:T(8,128)(2,1)S(1)}, u32[]{:S(2)}) copy-start(bf16[1024,704]{0,1:T(8,128)(2,1)S(1)} %get-tuple-element.33) | copy-start | bytes 4325380
  108.8 69.9 %copy-start.14 = (bf16[1024,704]{0,1:T(8,128)(2,1)}, bf16[1024,704]{0,1:T(8,128)(2,1)S(1)}, u32[]{:S(2)}) copy-start(bf16[1024,704]{0,1:T(8,128)(2,1)S(1)} %get-tuple-element.32) | copy-start | bytes 4325380
  170.6 8.1 copy-start.1
  253.4 12.4 %copy-start.22 = (bf16[1024,704]{0,1:T(8,128)(2,1)S(1)}, bf16[1024,704]{0,1:T(8,128)(2,1)}, u32[]{:S(2)}) copy-start(bf16[1024,704]{0,1:T(8,128)(2,1)} %get-tuple-element.34) | copy-start | bytes 4325380
  265.8 8.3 copy-start.5
  265.8 8.3 copy-start.15
  294.5 390.1 %reduce-scatter.11.cloned.1.call-start = ((), (), s32[]{:S(2)}) async-start(), calls=%async_computation.14 | async-start | bytes 1802240 | tf_op jit(solution)/shard_map/reduce_scatter | solution.py:265
  566.2 6.8 copy-start.20
  566.2 6.8 copy-start.25
  567.2 5.8 copy-start.21
  579.0 11.2 %copy-start.29 = (f32[128,8]{0,1:T(8,128)S(1)}, f32[128,8]{0,1:T(8,128)}, u32[]{:S(2)}) copy-start(f32[128,8]{0,1:T(8,128)} %copy-done.28) | copy-start | bytes 12292
  579.0 11.2 %copy-start.33 = (f32[128]{0:T(128)S(1)}, f32[128]{0:T(128)}, u32[]{:S(2)}) copy-start(f32[128]{0:T(128)} %copy-done.32) | copy-start | bytes 1540
  579.0 11.3 %copy-start.3 = (f32[128,1024]{1,0:T(8,128)S(1)}, f32[128,1024]{1,0:T(8,128)}, u32[]{:S(2)}) copy-start(f32[128,1024]{1,0:T(8,128)} %copy-done.2) | copy-start | bytes 1572868
  579.0 11.3 %copy-start.31 = (f32[1024]{0:T(1024)S(1)}, f32[1024]{0:T(1024)}, u32[]{:S(2)}) copy-start(f32[1024]{0:T(1024)} %param.18) | copy-start | bytes 12292
  579.0 11.3 %copy-start.38 = (f32[128]{0:T(128)S(1)}, f32[128]{0:T(128)}, u32[]{:S(2)}) copy-start(f32[128]{0:T(128)} %copy-done.37) | copy-start | bytes 1540
  579.0 13.3 %copy-start.43 = (f32[128]{0:T(128)S(1)}, f32[128]{0:T(128)}, u32[]{:S(2)}) copy-start(f32[128]{0:T(128)} %copy-done.42) | copy-start | bytes 1540
  590.2 12.0 %copy-start.6 = (bf16[32,4,40,176]{3,2,0,1:T(8,128)(2,1)S(1)}, bf16[32,4,40,176]{3,2,0,1:T(8,128)(2,1)}, u32[]{:S(2)}) copy-start(bf16[32,4,40,176]{3,2,0,1:T(8,128)(2,1)} %copy-done.5) | copy-start | bytes 5406724
  596.8 16.3 %all-to-all-start.6 = ((bf16[128,1,16,64]{0,3,1,2:T(8,128)(2,1)}), bf16[128,1,16,64]{0,3,1,2:T(8,128)(2,1)S(1)}, u32[]{:S(2)}, u32[]{:S(2)}) async-start(bf16[128,1,16,64]{0,3,1,2:T(8,128)(2,1)} %bitcast.242), calls=%async_computation.6 | async-start | bytes 524288 | tf_op jit(solution)/shard_map/all_to_all | solution.py:65
  601.9 84.7 %reduce-scatter.9.cloned.1.call-start = ((), (), s32[]{:S(2)}) async-start(), calls=%async_computation.13 | async-start | bytes 3604480 | tf_op jit(solution)/shard_map/reduce_scatter | solution.py:33
  613.3 13.8 %slice-start = ((s8[16777216]{0:T(1024)(128)(4,1)}), s8[4194304]{0:T(1024)(128)(4,1)S(1)}, s32[]{:S(2)}) async-start(s8[16777216]{0:T(1024)(128)(4,1)} %bitcast.216), calls=%async_computation.17 | async-start | bytes 8388608
  613.3 13.8 %slice-start.1 = ((s8[16777216]{0:T(1024)(128)(4,1)}), s8[4194304]{0:T(1024)(128)(4,1)S(1)}, s32[]{:S(2)}) async-start(s8[16777216]{0:T(1024)(128)(4,1)} %bitcast.216), calls=%async_computation.18 | async-start | bytes 8388608
  613.3 15.3 %slice-start.2 = ((s8[16777216]{0:T(1024)(128)(4,1)}), s8[4194304]{0:T(1024)(128)(4,1)S(1)}, s32[]{:S(2)}) async-start(s8[16777216]{0:T(1024)(128)(4,1)} %bitcast.216), calls=%async_computation.19 | async-start | bytes 8388608
  613.3 16.5 %slice-start.3 = ((s8[16777216]{0:T(1024)(128)(4,1)}), s8[4194304]{0:T(1024)(128)(4,1)S(1)}, s32[]{:S(2)}) async-start(s8[16777216]{0:T(1024)(128)(4,1)} %bitcast.216), calls=%async_computation.20 | async-start | bytes 8388608
  645.6 13.4 %copy-start.12 = (f32[128,1024]{1,0:T(8,128)S(1)}, f32[128,1024]{1,0:T(8,128)}, u32[]{:S(2)}) copy-start(f32[128,1024]{1,0:T(8,128)} %copy-done.11) | copy-start | bytes 1572868
  651.9 19.7 %all-to-all-start.7 = ((bf16[16,2,12288]{2,1,0:T(2,128)(2,1)}), bf16[16,2,12288]{2,1,0:T(2,128)(2,1)}, u32[]{:S(2)}, u32[]{:S(2)}) async-start(bf16[16,2,12288]{2,1,0:T(2,128)(2,1)} %reshape.383), calls=%async_computation.7 | async-start | bytes 1572864 | tf_op jit(solution)/shard_map/all_to_all | solution.py:69
  658.7 18.1 %copy-start.8 = (bf16[128,1024]{1,0:T(8,128)(2,1)S(1)}, bf16[128,1024]{1,0:T(8,128)(2,1)}, u32[]{:S(2)}) copy-start(bf16[128,1024]{1,0:T(8,128)(2,1)} %param.14) | copy-start | bytes 786436
  658.7 18.1 %copy-start.27 = (f32[1024]{0:T(1024)S(1)}, f32[1024]{0:T(1024)}, u32[]{:S(2)}) copy-start(f32[1024]{0:T(1024)} %param.15) | copy-start | bytes 12292
  658.7 18.0 %copy-start.36 = (f32[128]{0:T(128)S(1)}, f32[128]{0:T(128)}, u32[]{:S(2)}) copy-start(f32[128]{0:T(128)} %copy-done.35) | copy-start | bytes 1540
  658.7 242.7 %all-reduce.8.cloned.1.call-start = ((), (), s32[]{:S(2)}) async-start(), calls=%async_computation.15 | async-start | bytes 33554432 | tf_op jit(solution)/shard_map/psum | solution.py:253
  689.4 73.2 %copy-start.41 = (f32[128]{0:T(128)S(1)}, f32[128]{0:T(128)}, u32[]{:S(2)}) copy-start(f32[128]{0:T(128)} %copy-done.40) | copy-start | bytes 1540
  901.4 11.1 %copy-start.17 = (f32[1024,1024]{1,0:T(8,128)S(1)}, f32[1024,1024]{1,0:T(8,128)}, u32[]{:S(2)}) copy-start(f32[1024,1024]{1,0:T(8,128)} %get-tuple-element.56) | copy-start | bytes 12582916
  (11 other events, 35.0 us)
Sparse Core Ops, SparseCore 0:
  11.9 55.3 all-gather.3
  92.9 77.6 all-gather.5
  173.3 80.1 all-gather.7
  294.6 263.3 all-reduce.9
  560.4 23.2 reduce-scatter.10
  613.2 37.6 reduce-scatter.8
  684.7 216.6 all-reduce.7
where the time goes:
time: 930 us; the launch traced here: 922 us
  waiting for transfers between devices  529 us (57%)
  matrix products  146 us (16%)
  blocking collectives  107 us (12%)
  other arithmetic  54.1 us (6%)
  local copies, waits for them, and re-layouts  52.2 us (6%)
  starting transfers between devices  17 us (2%)
  between operations  16.2 us (2%)
    unnamed x8, waiting for transfers between devices  244 us
    psum x1, waiting for transfers between devices, body(): lax.psum((attn_gain_term, qkv_term, out_term, moe_gain_term, router_term)...  138 us
    all_gather x1, waiting for transfers between devices, body(): cot_rows = lax.all_gather(cot_arrived, 'mp', axis=0, tiled=True)  69.7 us
    psum x1, blocking collectives, body(): lax.psum((attn_gain_term, qkv_term, out_term, moe_gain_term, router_term)...  65.5 us
    all_gather x1, waiting for transfers between devices, body(): expert_rows = lax.all_gather(arrived, 'mp', axis=0, tiled=True)  61.8 us
    unnamed x109, local copies, waits for them, and re-layouts  27.7 us
    all_to_all x1, blocking collectives, to_heads(): return lax.all_to_all(rows, 'mp', split_axis=2, concat_axis=0, tiled=True)  21.9 us
  transfers between devices with their start and end apart: 10, of which 6 were waited for; matrix products, arithmetic and copies ran while one was open for 20% of the time, Pallas kernels for 0%

commit v1 on v0

v1 whole, which is shorter than its diff:
```python
from functools import partial

import jax
import jax.numpy as jnp
from jax import lax
from jax.experimental import pallas as pl
from jax.experimental.pallas import tpu as pltpu
from jax.sharding import PartitionSpec as P

HEADS = 16
EPSILON = 1e-06
HIGHEST = lax.Precision.HIGHEST
MESH = pl.DeviceIdType.MESH
F32 = jnp.float32
BF16 = jnp.bfloat16
VMEM = pltpu.VMEM
ROWS = 40
FFB = 176
FFQ = 704
DB = 256
NT = (((1,), (1,)), ((), ()))
TN = (((0,), (0,)), ((), ()))


def dot(a, b):
    return jnp.dot(a, b, preferred_element_type=F32)


def dot_nt(a, b):
    return lax.dot_general(a, b, NT, preferred_element_type=F32)


def dot_tn(a, b):
    return lax.dot_general(a, b, TN, preferred_element_type=F32)


def spot():
    m = lax.axis_index("mp")
    return lax.axis_index("dp"), lax.axis_index("expert"), m, m // 4, m % 4


def params(cid, mb=60):
    return pltpu.CompilerParams(
        collective_id=cid, has_side_effects=True, vmem_limit_bytes=mb * 1024 * 1024
    )


def swapped(c, z):
    return z % 2, 2 * (z // 2) + c


def weight_kernel(w_ref, out_ref, stage, s_send, s_recv, x_send, x_recv, here):
    x, c, m, z, y = spot()
    pc, pz = swapped(c, z)
    away = (pc - c) * (pc - c)
    barrier = pltpu.get_barrier_semaphore()

    def remote(el):
        return (away == 1) | (el != y)

    for el in range(4):

        @pl.when(remote(el))
        def _():
            pl.semaphore_signal(
                barrier, inc=1, device_id={"expert": pc, "mp": pz * 4 + el}, device_id_type=MESH
            )

    for d in range(1, 4):
        pl.semaphore_signal(barrier, inc=1, device_id={"dp": (x + d) % 4}, device_id_type=MESH)
    pl.semaphore_wait(barrier, 6 + away)

    def rows(at):
        return stage.at[:, pl.ds(pl.multiple_of(at * FFB, 16), FFB), :]

    def hop(el):
        return pltpu.make_async_remote_copy(
            src_ref=w_ref.at[el],
            dst_ref=rows(y),
            send_sem=s_send.at[el],
            recv_sem=s_recv.at[y],
            device_id={"expert": pc, "mp": pz * 4 + el},
            device_id_type=MESH,
        )

    def landed(el):
        return pltpu.make_async_remote_copy(
            src_ref=w_ref.at[el],
            dst_ref=rows(el),
            send_sem=s_send.at[el],
            recv_sem=s_recv.at[el],
            device_id={"expert": pc, "mp": pz * 4 + el},
            device_id_type=MESH,
        )

    for el in range(4):

        @pl.when(remote(el))
        def _():
            hop(el).start()

    @pl.when(away == 0)
    def _():
        own = pltpu.make_async_copy(w_ref.at[y], rows(y), here.at[0])
        own.start()
        own.wait()

    for el in range(4):

        @pl.when(remote(el))
        def _():
            landed(el).wait_recv()

    def columns(at):
        return out_ref.at[:, :, pl.ds(pl.multiple_of(at * DB, DB), DB)]

    def fan(d, at):
        return pltpu.make_async_remote_copy(
            src_ref=stage,
            dst_ref=columns(at),
            send_sem=x_send.at[d],
            recv_sem=x_recv.at[d],
            device_id={"dp": (x + d) % 4},
            device_id_type=MESH,
        )

    for d in (2, 1, 3):
        fan(d, x).start()
    own = pltpu.make_async_copy(stage, columns(x), here.at[0])
    own.start()
    own.wait()
    for d in range(1, 4):
        fan(d, (x + 4 - d) % 4).wait_recv()
    for d in range(1, 4):
        fan(d, x).wait_send()
    for el in range(4):

        @pl.when(remote(el))
        def _():
            hop(el).wait_send()


def fetch_weights(blocks):
    return pl.pallas_call(
        weight_kernel,
        out_shape=jax.ShapeDtypeStruct((3, FFQ, 4 * DB), BF16),
        in_specs=[pl.BlockSpec(memory_space=VMEM)],
        out_specs=pl.BlockSpec(memory_space=pl.ANY),
        scratch_shapes=[
            VMEM((3, FFQ, DB), BF16),
            pltpu.SemaphoreType.DMA((4,)),
            pltpu.SemaphoreType.DMA((4,)),
            pltpu.SemaphoreType.DMA((4,)),
            pltpu.SemaphoreType.DMA((4,)),
            pltpu.SemaphoreType.DMA((1,)),
        ],
        compiler_params=params(1, 32),
    )(blocks)


def grad_kernel(g_ref, out_ref, s_send, s_recv, here):
    x, c, m, z, y = spot()
    pc, pz = swapped(c, z)
    away = (pc - c) * (pc - c)
    barrier = pltpu.get_barrier_semaphore()

    def remote(at):
        return (away == 1) | (at != y)

    for at in range(4):

        @pl.when(remote(at))
        def _():
            pl.semaphore_signal(
                barrier, inc=1, device_id={"expert": pc, "mp": pz * 4 + at}, device_id_type=MESH
            )

    pl.semaphore_wait(barrier, 3 + away)

    def hop(at, slot):
        return pltpu.make_async_remote_copy(
            src_ref=g_ref.at[:, pl.ds(at * FFB, FFB), :],
            dst_ref=out_ref.at[slot],
            send_sem=s_send.at[at],
            recv_sem=s_recv.at[slot],
            device_id={"expert": pc, "mp": pz * 4 + at},
            device_id_type=MESH,
        )

    for at in range(4):

        @pl.when(remote(at))
        def _():
            hop(at, y).start()

    @pl.when(away == 0)
    def _():
        own = pltpu.make_async_copy(
            g_ref.at[:, pl.ds(pl.multiple_of(y * FFB, 16), FFB), :], out_ref.at[y], here.at[0]
        )
        own.start()
        own.wait()

    for at in range(4):

        @pl.when(remote(at))
        def _():
            hop(at, at).wait_recv()

    for at in range(4):

        @pl.when(remote(at))
        def _():
            hop(at, y).wait_send()


def return_grads(grads):
    return pl.pallas_call(
        grad_kernel,
        out_shape=jax.ShapeDtypeStruct((4, 3, FFB, DB), BF16),
        in_specs=[pl.BlockSpec(memory_space=VMEM)],
        out_specs=pl.BlockSpec(memory_space=VMEM),
        scratch_shapes=[
            pltpu.SemaphoreType.DMA((4,)),
            pltpu.SemaphoreType.DMA((4,)),
            pltpu.SemaphoreType.DMA((1,)),
        ],
        compiler_params=params(2, 32),
    )(grads)


GELU_A = 0.7978845608
GELU_B = 0.044715


def moe_kernel(
    send_ref,
    w_ref,
    ret_ref,
    grad_ref,
    recv,
    own_part,
    sib_send,
    sib_recv,
    back,
    xs,
    cs,
    hid,
    gcs,
    ucs,
    d_send,
    d_recv,
    f_send,
    f_recv,
    p_send,
    p_recv,
    r_send,
    r_recv,
):
    x, c, m, z, y = spot()
    barrier = pltpu.get_barrier_semaphore()

    def greet(k, carry):
        pl.semaphore_signal(barrier, inc=1, device_id={"mp": (m + k) % 16}, device_id_type=MESH)
        return carry

    lax.fori_loop(1, 16, greet, 0)
    pl.semaphore_signal(barrier, inc=1, device_id={"expert": 1 - c}, device_id_type=MESH)
    pl.semaphore_wait(barrier, 16)

    def expert_of(t):
        return ((t // 4) % 2) * 4 + t % 4

    def dispatch(k):
        t = (m + k) % 16
        return pltpu.make_async_remote_copy(
            src_ref=send_ref.at[expert_of(t)],
            dst_ref=recv.at[0, k],
            send_sem=d_send.at[k],
            recv_sem=d_recv.at[k],
            device_id={"mp": t},
            device_id_type=MESH,
        )

    def forward(k):
        return pltpu.make_async_remote_copy(
            src_ref=recv.at[0, k],
            dst_ref=recv.at[1, k],
            send_sem=f_send.at[k],
            recv_sem=f_recv.at[k],
            device_id={"expert": 1 - c},
            device_id_type=MESH,
        )

    def partials(j):
        return pltpu.make_async_remote_copy(
            src_ref=sib_send.at[j],
            dst_ref=sib_recv.at[j],
            send_sem=p_send.at[j],
            recv_sem=p_recv.at[j],
            device_id={"expert": 1 - c},
            device_id_type=MESH,
        )

    def giving(k):
        return pltpu.make_async_remote_copy(
            src_ref=back.at[k],
            dst_ref=ret_ref.at[m],
            send_sem=r_send.at[k],
            recv_sem=r_recv.at[k],
            device_id={"mp": (m + 16 - k) % 16},
            device_id_type=MESH,
        )

    def start_dispatch(k, carry):
        dispatch(k).start()
        return carry

    lax.fori_loop(1, 16, start_dispatch, 0)
    recv[0, 0] = send_ref[expert_of(m)]

    def finish(j):
        partials(j).wait_recv()
        back[pl.ds(4 * j, 4)] = (own_part[...] + sib_recv[j].astype(F32)).astype(BF16)
        for i in range(4):
            k = 4 * j + i

            @pl.when(k > 0)
            def _():
                giving(k).start()

            @pl.when(k == 0)
            def _():
                ret_ref[m] = back[0]

    def chunk(j, carry):
        for i in range(4):
            k = 4 * j + i

            @pl.when(k > 0)
            def _():
                dispatch(k).wait_recv()

            forward(k).start()

        @pl.when(j > 0)
        def _():
            finish(j - 1)

        for i in range(4):
            forward(4 * j + i).wait_recv()
        blk = recv[:, pl.ds(4 * j, 4)].astype(F32)
        span = pl.ds(pl.multiple_of(j * 8 * ROWS, 16), 8 * ROWS)
        xs[span] = blk[:, :, :ROWS].reshape(8 * ROWS, 4 * DB).astype(BF16)
        cs[span] = blk[:, :, ROWS:].reshape(8 * ROWS, 4 * DB).astype(BF16)
        gate = dot_nt(xs[span], w_ref[0])
        up = dot_nt(xs[span], w_ref[1])
        hid_cot = dot_nt(cs[span], w_ref[2])
        sq = gate * gate
        th = jnp.tanh(GELU_A * (gate + GELU_B * (gate * sq)))
        half = 0.5 * (1.0 + th)
        act = gate * half
        slope = half + 0.5 * gate * (1.0 - th * th) * (GELU_A * (1.0 + 3.0 * GELU_B * sq))
        hid[span] = (act * up).astype(BF16)
        gcs[span] = (hid_cot * up * slope).astype(BF16)
        ucs[span] = (hid_cot * act).astype(BF16)
        out = dot(hid[span], w_ref[2]).reshape(2, 4, ROWS, 4 * DB)
        rows = (dot(gcs[span], w_ref[0]) + dot(ucs[span], w_ref[1])).reshape(2, 4, ROWS, 4 * DB)
        own_part[:, :ROWS] = out[0]
        own_part[:, ROWS:] = rows[0]
        sib_send[j] = jnp.concatenate([out[1], rows[1]], axis=1).astype(BF16)
        partials(j).start()
        return carry

    lax.fori_loop(0, 4, chunk, 0)
    finish(3)
    for i, (a, b) in enumerate(((gcs, xs), (ucs, xs), (hid, cs))):
        g = dot_tn(a[...], b[...])
        for at in range(4):
            grad_ref[at, i] = g[:, at * DB : (at + 1) * DB].astype(BF16)

    def drain(k, carry):
        pltpu.make_async_remote_copy(
            src_ref=back.at[k],
            dst_ref=ret_ref.at[(m + k) % 16],
            send_sem=r_send.at[k],
            recv_sem=r_recv.at[k],
            device_id={"mp": (m + 16 - k) % 16},
            device_id_type=MESH,
        ).wait()
        dispatch(k).wait_send()
        forward(k).wait_send()
        return carry

    lax.fori_loop(1, 16, drain, 0)
    forward(0).wait_send()
    for j in range(4):
        partials(j).wait_send()


def moe(send, weights):
    dma = pltpu.SemaphoreType.DMA
    block = (2 * ROWS, 4 * DB)
    return pl.pallas_call(
        moe_kernel,
        out_shape=(
            jax.ShapeDtypeStruct((16, *block), BF16),
            jax.ShapeDtypeStruct((4, 3, FFQ, DB), BF16),
        ),
        in_specs=[pl.BlockSpec(memory_space=VMEM)] * 2,
        out_specs=(pl.BlockSpec(memory_space=VMEM),) * 2,
        scratch_shapes=[
            VMEM((2, 16, *block), BF16),
            VMEM((4, *block), F32),
            VMEM((4, 4, *block), BF16),
            VMEM((4, 4, *block), BF16),
            VMEM((16, *block), BF16),
            VMEM((32 * ROWS, 4 * DB), BF16),
            VMEM((32 * ROWS, 4 * DB), BF16),
            VMEM((32 * ROWS, FFQ), BF16),
            VMEM((32 * ROWS, FFQ), BF16),
            VMEM((32 * ROWS, FFQ), BF16),
            dma((16,)),
            dma((16,)),
            dma((16,)),
            dma((16,)),
            dma((4,)),
            dma((4,)),
            dma((16,)),
            dma((16,)),
        ],
        compiler_params=params(3, 62),
    )(send, weights)


def rms_norm(values, gain):
    return values * lax.rsqrt(jnp.mean(values * values, axis=-1, keepdims=True) + EPSILON) * gain


def gating(moe_in, router_weight, routes):
    logits = jnp.dot(moe_in, router_weight, precision=HIGHEST, preferred_element_type=F32)
    probs = jax.nn.softmax(logits, axis=-1)
    onehot = (routes[:, :, None] == jnp.arange(8, dtype=routes.dtype)).astype(F32)
    chosen = jnp.sum(probs[:, None, :] * onehot, axis=2)
    return chosen / jnp.sum(chosen, axis=1, keepdims=True)


def to_heads(rows):
    return lax.all_to_all(rows, "mp", split_axis=2, concat_axis=0, tiled=True)


def to_tokens(rows):
    return lax.all_to_all(rows, "mp", split_axis=0, concat_axis=2, tiled=True)


def attention_forward(queries, key_heads, value_heads):
    router_scores = jnp.einsum("qhd,khd->hqk", queries, key_heads, preferred_element_type=F32) * 0.125
    log_total = jax.nn.logsumexp(router_scores, axis=-1, keepdims=True)
    probs_low = jnp.exp(router_scores - log_total).astype(BF16)
    context = jnp.einsum("hqk,khd->qhd", probs_low, value_heads, preferred_element_type=F32)
    return (context.astype(BF16), log_total)


def attention_backward(queries, key_heads, value_heads, log_total, context_cot):
    scores_again = jnp.einsum("qhd,khd->hqk", queries, key_heads, preferred_element_type=F32) * 0.125
    probs_full = jnp.exp(scores_again - log_total)
    probs_again = probs_full.astype(BF16)
    probs_cot = jnp.einsum("qhd,khd->hqk", context_cot, value_heads, preferred_element_type=F32)
    inner = jnp.sum(probs_full * probs_cot, axis=-1, keepdims=True)
    score_cot = (probs_full * (probs_cot - inner)).astype(BF16)
    query_cot = jnp.einsum("hqk,khd->qhd", score_cot, key_heads, preferred_element_type=F32) * 0.125
    key_part = jnp.einsum("hqk,qhd->khd", score_cot, queries, preferred_element_type=F32) * 0.125
    value_part = jnp.einsum("hqk,qhd->khd", probs_again, context_cot, preferred_element_type=F32)
    return (query_cot, key_part, value_part)


def body(
    block_input,
    attn_gain,
    qkv_weight,
    out_weight,
    moe_gain,
    router_weight,
    gate_weight,
    up_weight,
    down_weight,
    routes,
    slot_index,
    cotangent,
):
    tok_rows, width = block_input.shape
    head_size = width // HEADS
    blocks = jnp.stack(
        [
            jnp.swapaxes(gate_weight, 1, 2).astype(BF16),
            jnp.swapaxes(up_weight, 1, 2).astype(BF16),
            down_weight.astype(BF16),
        ],
        axis=1,
    )
    weights = fetch_weights(blocks)
    inputs = block_input.astype(F32)
    qkv_low = qkv_weight.astype(BF16)
    out_low = out_weight.astype(BF16)
    normed, norm_back = jax.vjp(rms_norm, inputs, attn_gain)
    normed_low = normed.astype(BF16)
    packed = dot(normed_low, qkv_low).astype(BF16)
    by_head = to_heads(packed.reshape(tok_rows, 3, HEADS, head_size))
    queries = by_head[:, 0]
    key_heads = by_head[:, 1]
    value_heads = by_head[:, 2]
    context_here, log_total = attention_forward(queries, key_heads, value_heads)
    context = to_tokens(context_here[:, None]).reshape(tok_rows, width)
    middle = inputs + dot(context, out_low)
    moe_in, moe_back = jax.vjp(rms_norm, middle, moe_gain)
    gates, gate_back = jax.vjp(partial(gating, routes=routes), moe_in, router_weight)
    valid = slot_index < ROWS
    place = routes * (2 * ROWS) + slot_index
    keep = valid.astype(F32)
    upstream = cotangent.astype(F32)
    pair_rows = jnp.repeat(moe_in.astype(BF16), 2, axis=0)
    pair_cots = (gates[:, :, None] * upstream[:, None, :]).astype(BF16).reshape(2 * tok_rows, width)
    target = jnp.where(valid, place, 16 * ROWS).reshape(-1)
    cot_target = jnp.where(valid, place + ROWS, 16 * ROWS).reshape(-1)
    send = jnp.zeros((16 * ROWS, width), BF16)
    send = send.at[target].set(pair_rows, mode="drop").at[cot_target].set(pair_cots, mode="drop")
    returned, grads = moe(send.reshape(8, 2 * ROWS, width), weights)
    returned = returned.reshape(2, 8 * 2 * ROWS, width).astype(F32)
    returned = (returned[0] + returned[1]).astype(BF16)
    fetch_at = jnp.where(valid, place, 0)
    fetched = jnp.take(returned, fetch_at, axis=0).astype(F32) * keep[:, :, None]
    block_output = (middle + jnp.sum(gates[:, :, None] * fetched, axis=1)).astype(BF16)
    gate_cot = jnp.sum(upstream[:, None, :] * fetched, axis=2)
    moe_cot = jnp.sum(
        jnp.take(returned, fetch_at + ROWS, axis=0).astype(F32) * keep[:, :, None], axis=1
    )
    router_in_cot, router_term = gate_back(gate_cot)
    middle_norm_cot, moe_gain_term = moe_back(moe_cot + router_in_cot)
    middle_cot = upstream + middle_norm_cot
    branch_cot = middle_cot.astype(BF16)
    out_term = dot_tn(context, branch_cot)
    context_cot = dot_nt(branch_cot, out_low)
    context_cot = context_cot.astype(BF16).reshape(tok_rows, HEADS, head_size)
    cot_heads = to_heads(context_cot[:, None])[:, 0]
    query_cot, key_part, value_part = attention_backward(
        queries, key_heads, value_heads, log_total, cot_heads
    )
    stacked = jnp.stack(
        [query_cot.astype(BF16), key_part.astype(BF16), value_part.astype(BF16)], axis=1
    )
    packed_cot = to_tokens(stacked).reshape(tok_rows, 3 * width)
    qkv_term = dot_tn(normed_low, packed_cot)
    normed_cot = dot_nt(packed_cot, qkv_low)
    input_norm_cot, attn_gain_term = norm_back(normed_cot)
    input_grad = middle_cot + input_norm_cot
    everyone = ("dp", "expert", "mp")
    out_grad = lax.psum(out_term.astype(BF16), everyone).astype(F32)
    qkv_grad = lax.psum(qkv_term.astype(BF16), everyone).astype(F32)
    small = jnp.concatenate([attn_gain_term, moe_gain_term, router_term.reshape(-1)])
    small = lax.psum(small, everyone)
    mine = lax.psum_scatter(grads, "dp", scatter_dimension=0, tiled=True)
    mine = return_grads(mine.reshape(3, FFQ, DB)).astype(F32)
    return (
        block_output,
        input_grad,
        small[:width],
        qkv_grad,
        out_grad,
        small[width : 2 * width],
        small[2 * width :].reshape(width, 8),
        jnp.swapaxes(mine[:, 0], 1, 2),
        jnp.swapaxes(mine[:, 1], 1, 2),
        mine[:, 2],
    )


def solution(mesh):
    tokens = P(("dp", "expert", "mp"), None)
    cols = P("expert", "dp", "mp")
    rows = P("expert", "mp", "dp")
    return jax.shard_map(
        body,
        mesh=mesh,
        in_specs=(tokens, P(), P(), P(), P(), P(), cols, cols, rows, tokens, tokens, tokens),
        out_specs=(tokens, tokens, P(), P(), P(), P(), P(), cols, cols, rows),
        check_vma=False,
    )
```

time: 930 us -> 605 us (0.65)
  waiting for transfers between devices: 529 us -> 135 us
  Pallas kernels: 0 us -> 168 us
  matrix products: 146 us -> 72.3 us
  blocking collectives: 107 us -> 84 us
    unnamed x8 -> x2, waiting for transfers between devices: 244 us -> 0.32 us
    pallas_call x0 -> x3, Pallas kernels: none -> 168 us  [the longest x1 82.2 us: moe(): pl.pallas_call(moe_kernel, out_shape=(jax.ShapeDtypeStruct((16, *block),...]
    all_gather x3 -> x0, waiting for transfers between devices: 132 us -> none  [the longest x1 69.7 us: body(): cot_rows = lax.all_gather(cot_arrived, 'mp', axis=0, tiled=True)]
    dot_general x18 -> x9, matrix products: 118 us -> 41.2 us  [the longest x2 9.9 us: dot_nt(): return lax.dot_general(a, b, NT, preferred_element_type=F32)]
    psum x1, waiting for transfers between devices: 138 us -> 114 us  [body(): qkv_grad = lax.psum(qkv_term.astype(BF16), everyone).astype(F32)]
    all_to_all x4 -> x0, blocking collectives: 19.8 us -> none  [the longest x1 6.61 us: body(): lax.all_to_all(send_rows.reshape(group_count, local_experts, capacity, wi...]
    unnamed x109 -> x85, local copies, waits for them, and re-layouts: 27.7 us -> 15.2 us
    scatter-add x1 -> x0, other arithmetic: 11.1 us -> none  [gating(): chosen = jnp.take_along_axis(probs, routes, axis=1)]
  transfers between devices with their start and end apart: 10 -> 5, of which waited for: 6 -> 3; matrix products, arithmetic and copies ran while one was open for 20% -> 6% of each run, Pallas kernels for 0% -> 12%
where the time goes in v1:
time: 605 us; the launch traced here: 596 us
  Pallas kernels  168 us (28%)
  waiting for transfers between devices  135 us (22%)
  blocking collectives  84 us (14%)
  matrix products  72.3 us (12%)
  other arithmetic  56.1 us (9%)
  local copies, waits for them, and re-layouts  47.7 us (8%)
  between operations  16.5 us (3%)
  starting transfers between devices  16.3 us (3%)
    psum x1, waiting for transfers between devices, body(): qkv_grad = lax.psum(qkv_term.astype(BF16), everyone).astype(F32)  114 us
    pallas_call x1, Pallas kernels, moe(): pl.pallas_call(moe_kernel, out_shape=(jax.ShapeDtypeStruct((16, *block),...  82.2 us
    psum x1, blocking collectives, body(): small = lax.psum(small, everyone)  70 us
    pallas_call x1, Pallas kernels, fetch_weights(): pl.pallas_call(weight_kernel, out_shape=jax.ShapeDtypeStruct((3, FFQ, 4 *...  69.3 us
    pallas_call x1, Pallas kernels, return_grads(): pl.pallas_call(grad_kernel, out_shape=jax.ShapeDtypeStruct((4, 3, FFB, DB...  16.7 us
    unnamed x85, local copies, waits for them, and re-layouts  15.2 us
    all_to_all x1, blocking collectives, to_heads(): return lax.all_to_all(rows, 'mp', split_axis=2, concat_axis=0, tiled=True)  14 us
    dot_general x1, matrix products, attention_backward(): jnp.einsum('qhd,khd->hqk', context_cot, value_heads, preferred_element_ty...  13.6 us
  transfers between devices with their start and end apart: 5, of which 3 were waited for; matrix products, arithmetic and copies ran while one was open for 6% of the time, Pallas kernels for 12%

profile of v1, /device:TPU:1, one launch (start us, length us, event | category | flops | bytes accessed | tf_op | source)
XLA Modules:
  0.0 595.6 jit_solution(488713328315559741)
XLA Ops:
  9.7 5.8 convolution_convert_fusion.1
  16.9 8.6 %all-to-all-start = ((bf16[128,3,16,64]{0,3,1,2:T(8,128)(2,1)}), bf16[128,3,16,64]{0,3,1,2:T(8,128)(2,1)S(1)}, u32[]{:S(2)}, u32[]{:S(2)}) async-start(bf16[128,3,16,64]{0,3,1,2:T(8,128)(2,1)} %copy.133), calls=%async_computation | async-start | bytes 1572864 | tf_op jit(solution)/shard_map/all_to_all | solution.py:449
  28.3 10.4 %all-to-all-done = bf16[128,3,16,64]{0,3,1,2:T(8,128)(2,1)S(1)} async-done(((bf16[128,3,16,64]{0,3,1,2:T(8,128)(2,1)}), bf16[128,3,16,64]{0,3,1,2:T(8,128)(2,1)S(1)}, u32[]{:S(2)}, u32[]{:S(2)}) %all-to-all-start) | async-done | bytes 786464 | tf_op jit(solution)/shard_map/all_to_all | solution.py:449
  38.8 8.1 %multiply_reduce_fusion.1 = (f32[2048]{0:T(1024)S(1)}, f32[2048,2048]{0,1:T(8,128)}) fusion(bf16[2048,3,1,64]{0,3,1,2:T(8,128)(2,1)S(1)} %copy_bitcast_fusion), kind=kOutput, calls=%fused_computation.8 | convolution fusion | flops 545257472 | bytes 17309696 | tf_op jit(solution)/shard_map/qhd,khd->hqk/dot_general | solution.py:457
  46.9 8.5 %exponential_reduce_fusion = f32[2048]{0:T(1024)S(1)} fusion(f32[2048,2048]{0,1:T(8,128)} %get-tuple-element.103, f32[2048]{0:T(1024)S(1)} %is-finite_select_fusion), kind=kLoop, calls=%fused_computation.7 | loop fusion | flops 12580864 | bytes 16793600 | tf_op jit(solution)/shard_map/reduce_sum | solution.py:458
  55.5 7.4 %fusion.9 = bf16[2048,1,1,64]{0,3,2,1:T(8,128)(2,1)S(1)} fusion(f32[2048,2048]{0,1:T(8,128)} %get-tuple-element.103, f32[2048]{0:T(1024)S(1)} %log_add_fusion, bf16[2048,3,1,64]{0,3,1,2:T(8,128)(2,1)S(1)} %copy_bitcast_fusion), kind=kOutput, calls=%fused_computation.25 | convolution fusion | flops 549584896 | bytes 17309696 | tf_op jit(solution)/shard_map/hqk,khd->qhd/dot_general | solution.py:460
  65.6 3.8 all-to-all-start.1
  72.0 1.2 mul.248
  73.3 3.0 mul.249
  76.3 69.3 %shard_map.195.w_ref = bf16[3,704,1024]{2,1,0:T(8,128)(2,1)S(1)} custom-call(bf16[4,3,176,256]{3,2,1,0:T(8,128)(2,1)S(1)} %pad_maximum_fusion.w_ref), custom_call_target="tpu_custom_call" | custom-call | tf_op jit(solution)/shard_map/pallas_call | solution.py:144
  145.6 2.0 copy-done.2
  149.6 2.9 multiply_reduce_fusion.7
  155.5 2.0 broadcast_in_dim.69
  157.5 2.0 reshape.349
  159.5 3.3 scatter_custom_fusion
  162.8 4.3 scatter_custom_fusion.1
  167.1 82.2 %shard_map.196 = (bf16[16,80,1024]{2,1,0:T(8,128)(2,1)}, bf16[4,3,704,256]{3,2,1,0:T(8,128)(2,1)}) custom-call(bf16[8,80,1024]{2,1,0:T(8,128)(2,1)} %bitcast.13.send_ref, bf16[3,704,1024]{2,1,0:T(8,128)(2,1)} %copy-done.2), custom_call_target="tpu_custom_call" | custom-call | tf_op jit(solution)/shard_map/pallas_call | solution.py:404
  249.4 2.4 convert_element_type.147
  252.3 2.0 gather_fusion.1
  254.3 2.0 gather_fusion
  256.2 1.2 reshape.368
  257.5 2.0 reshape.372
  259.5 8.6 %multiply_reduce_fusion.2 = (f32[128,2]{1,0:T(8,128)S(1)}, f32[128,1024]{1,0:T(8,128)}, f32[128,1024]{1,0:T(8,128)S(1)}) fusion(f32[128,2]{1,0:T(8,128)S(1)} %copy.144, f32[128,1024]{1,0:T(8,128)} %convert_element_type.140, bf16[128,2,1024]{2,1,0:T(2,128)(2,1)S(1)} %reshape.368, pred[128,2]{1,0:T(8,128)(4,1)S(1)} %copy-done.15, f32[128,2]{1,0:T(8,128)S(1)} %copy.138, ...), kind=kLoop, calls=%fused_computation.32 | loop fusion | flops 2621184 | bytes 2625024 | tf_op jit(solution)/shard_map/reduce_sum | solution.py:533
  269.1 1.9 fusion.21
  271.1 3.0 convolution_convert_fusion.5
  274.2 14.0 %all_to_all.63 = bf16[128,1,16,64]{0,3,1,2:T(8,128)(2,1)S(1)} all-to-all(bf16[128,1,16,64]{0,3,1,2:T(8,128)(2,1)S(1)} %bitcast.136), channel_id=1, replica_groups=mesh['dp'=4,'expert'=2,'mp'=16] {'mp'}, dimensions={2} | all-to-all | bytes 524288 | tf_op jit(solution)/shard_map/all_to_all | solution.py:449
  288.4 7.5 %fusion.10 = bf16[2048,1,1,64]{0,3,2,1:T(8,128)(2,1)S(1)} fusion(f32[2048,2048]{0,1:T(8,128)} %get-tuple-element.103, f32[2048]{0:T(1024)S(1)} %log_add_fusion, bf16[8,8,16,128]{3,2,1,0:T(8,128)(2,1)S(1)} %bitcast.129), kind=kOutput, calls=%fused_computation.26 | convolution fusion | flops 549584896 | bytes 17309696 | tf_op jit(solution)/shard_map/hqk,qhd->khd/dot_general | solution.py:473
  296.0 13.6 %multiply_reduce_fusion = (f32[2048]{0:T(1024)S(1)}, f32[2048,2048]{0,1:T(8,128)}) fusion(f32[2048,2048]{0,1:T(8,128)} %get-tuple-element.103, f32[2048]{0:T(1024)S(1)} %log_add_fusion, bf16[2048,3,1,64]{0,3,1,2:T(8,128)(2,1)S(1)} %copy_bitcast_fusion, bf16[8,8,16,128]{3,2,1,0:T(8,128)(2,1)S(1)} %bitcast.130), kind=kOutput, calls=%fused_computation.5 | convolution fusion | flops 553646080 | bytes 34095104 | tf_op jit(solution)/shard_map/qhd,khd->hqk/dot_general | solution.py:468
  309.7 1.6 slice-done.3
  311.2 10.8 %multiply_convert_fusion = bf16[2048,2048]{0,1:T(8,128)(2,1)} fusion(f32[2048,2048]{0,1:T(8,128)} %get-tuple-element.110, f32[2048,2048]{0,1:T(8,128)S(1)} %bitcast.122, f32[2048]{0:T(1024)S(1)} %get-tuple-element.109, f32[2048]{0:T(1024)S(1)} %log_add_fusion), kind=kLoop, calls=%fused_computation.4 | loop fusion | flops 20971520 | bytes 41959424 | tf_op jit(solution)/shard_map/convert_element_type | solution.py:470
  322.0 6.2 %fusion.7 = bf16[2048,1,1,64]{0,3,2,1:T(8,128)(2,1)S(1)} fusion(bf16[2048,2048]{0,1:T(8,128)(2,1)} %multiply_convert_fusion, bf16[2048,3,1,64]{0,3,1,2:T(8,128)(2,1)S(1)} %copy_bitcast_fusion), kind=kOutput, calls=%fused_computation.23 | convolution fusion | flops 537133056 | bytes 8912896 | tf_op jit(solution)/shard_map/hqk,qhd->khd/dot_general | solution.py:472
  328.2 1.6 fusion.8
  329.9 2.5 copy.152
  332.4 4.2 reshape.379
  336.6 3.6 all-to-all-start.3
  340.3 2.1 convolution_convert_fusion.4
  342.3 9.6 %all-to-all-done.3 = bf16[16,2,12288]{2,1,0:T(2,128)(2,1)S(1)} async-done(((bf16[16,2,12288]{2,1,0:T(2,128)(2,1)}), bf16[16,2,12288]{2,1,0:T(2,128)(2,1)S(1)}, u32[]{:S(2)}, u32[]{:S(2)}) %all-to-all-start.3) | async-done | bytes 786464 | tf_op jit(solution)/shard_map/all_to_all | solution.py:453
  351.9 2.5 reshape.380
  354.4 2.9 copy.159
  357.3 4.6 convolution_convert_fusion
  363.9 6.9 %fusion.20 = (f32[1024]{0:T(1024)S(1)}, f32[128]{0:T(128)S(1)}, f32[128,1024]{1,0:T(8,128)S(1)}) fusion(bf16[128,1024]{1,0:T(8,128)(2,1)S(1)} %copy-done.5, f32[128]{0:T(128)S(1)} %fusion.46, f32[1024]{0:T(1024)S(1)} %copy-done.13, bf16[128,3072]{0,1:T(8,128)(2,1)S(1)} %bitcast.128, f32[1024,3072]{1,0:T(8,128)} %param.16), kind=kOutput, calls=%fused_computation.57 | convolution fusion | flops 809368448 | bytes 14164992 | tf_op jit(solution)/shard_map/dot_general | solution.py:30
  370.8 70.0 %psum.21 = f32[10240]{0:T(1024)S(1)} all-reduce(f32[10240]{0:T(1024)S(1)} %pad_maximum_fusion.2), channel_id=1, replica_groups=mesh['dp'=4,'expert'=2,'mp'=16] {'dp','expert','mp'}, use_global_device_ids=true, to_apply=%region_21.23 | all-reduce | flops 10240 | bytes 81920 | tf_op jit(solution)/shard_map/psum | solution.py:560
  443.5 114.2 %all-reduce.3.cloned.1.call-done = (bf16[1024,3072]{1,0:T(8,128)(2,1)}, bf16[1024,1024]{1,0:T(8,128)(2,1)}) async-done(((bf16[1024,3072]{1,0:T(8,128)(2,1)}, bf16[1024,1024]{1,0:T(8,128)(2,1)}), (bf16[1024,3072]{1,0:T(8,128)(2,1)}, bf16[1024,1024]{1,0:T(8,128)(2,1)})) %all-reduce.3.cloned.1.call-update) | async-done | bytes 8388624 | tf_op jit(solution)/shard_map/psum | solution.py:558
  557.7 4.2 convert_element_type.169
  562.0 6.4 %convert_element_type.167 = f32[1024,3072]{1,0:T(8,128)} convert(bf16[1024,3072]{1,0:T(8,128)(2,1)S(1)} %copy-done.6) | non-fusion elementwise | flops 3145728 | bytes 18874368 | tf_op jit(solution)/shard_map/convert_element_type | solution.py:558
  568.4 1.2 copy-done.3
  569.6 16.7 %shard_map.197 = bf16[4,3,176,256]{3,2,1,0:T(8,128)(2,1)S(1)} custom-call(bf16[3,704,256]{2,1,0:T(8,128)(2,1)S(1)} %bitcast.120), custom_call_target="tpu_custom_call" | custom-call | tf_op jit(solution)/shard_map/pallas_call | solution.py:218
  586.5 1.4 slice_bitcast_fusion
  (153 shorter events, 22.7 us)
Async XLA Ops:
  8.0 144.5 %copy-start = (f32[1024,8]{0,1:T(8,128)S(1)}, f32[1024,8]{0,1:T(8,128)}, u32[]{:S(2)}) copy-start(f32[1024,8]{0,1:T(8,128)} %param.19) | copy-start | bytes 98308
  9.1 0.6 copy-start.29
  9.7 15.8 %copy-start.21 = (s32[128,2]{0,1:T(2,128)S(1)}, s32[128,2]{0,1:T(2,128)}, u32[]{:S(2)}) copy-start(s32[128,2]{0,1:T(2,128)} %param.23) | copy-start | bytes 3076
  9.7 15.8 %copy-start.28 = (s32[128,2]{0,1:T(2,128)S(1)}, s32[128,2]{0,1:T(2,128)}, u32[]{:S(2)}) copy-start(s32[128,2]{0,1:T(2,128)} %param.24) | copy-start | bytes 3076
  9.7 16.6 %copy-start.11 = (f32[4,176,256]{2,1,0:T(8,128)S(1)}, f32[4,176,256]{2,1,0:T(8,128)}, u32[]{:S(2)}) copy-start(f32[4,176,256]{2,1,0:T(8,128)} %param.22) | copy-start | bytes 2162692
  9.7 16.7 %copy-start.12 = (f32[4,256,176]{1,2,0:T(8,128)S(1)}, f32[4,256,176]{1,2,0:T(8,128)}, u32[]{:S(2)}) copy-start(f32[4,256,176]{1,2,0:T(8,128)} %param.21) | copy-start | bytes 2162692
  16.9 21.8 %all-to-all-start = ((bf16[128,3,16,64]{0,3,1,2:T(8,128)(2,1)}), bf16[128,3,16,64]{0,3,1,2:T(8,128)(2,1)S(1)}, u32[]{:S(2)}, u32[]{:S(2)}) async-start(bf16[128,3,16,64]{0,3,1,2:T(8,128)(2,1)} %copy.133), calls=%async_computation | async-start | bytes 1572864 | tf_op jit(solution)/shard_map/all_to_all | solution.py:449
  55.4 15.7 %copy-start.8 = (bf16[128,1024]{1,0:T(8,128)(2,1)S(1)}, bf16[128,1024]{1,0:T(8,128)(2,1)}, u32[]{:S(2)}) copy-start(bf16[128,1024]{1,0:T(8,128)(2,1)} %param.25) | copy-start | bytes 786436
  62.9 86.7 %copy-start.5 = (bf16[128,1024]{1,0:T(8,128)(2,1)S(1)}, bf16[128,1024]{1,0:T(8,128)(2,1)}, u32[]{:S(2)}) copy-start(bf16[128,1024]{1,0:T(8,128)(2,1)} %param.14) | copy-start | bytes 786436
  65.6 82.6 %all-to-all-start.1 = ((bf16[16,2,4096]{2,1,0:T(2,128)(2,1)}), bf16[16,2,4096]{2,1,0:T(2,128)(2,1)S(1)}, u32[]{:S(2)}, u32[]{:S(2)}) async-start(bf16[16,2,4096]{2,1,0:T(2,128)(2,1)} %reshape.377), calls=%async_computation.1 | async-start | bytes 524288 | tf_op jit(solution)/shard_map/all_to_all | solution.py:453
  73.3 79.2 %copy-start.14 = (f32[1024]{0:T(1024)S(1)}, f32[1024]{0:T(1024)}, u32[]{:S(2)}) copy-start(f32[1024]{0:T(1024)} %param.18) | copy-start | bytes 12292
  73.3 81.3 %copy-start.22 = (s32[128,2]{0,1:T(2,128)S(1)}, s32[128,2]{0,1:T(2,128)}, u32[]{:S(2)}) copy-start(s32[128,2]{0,1:T(2,128)} %param.23) | copy-start | bytes 3076
  145.6 2.1 copy-start.2
  149.4 13.4 %copy-start.7 = (f32[256,1024]{1,0:T(8,128)S(1)}, f32[256,1024]{1,0:T(8,128)}, u32[]{:S(2)}) copy-start(f32[256,1024]{1,0:T(8,128)} %mul.249) | copy-start | bytes 3145732
  149.6 17.6 %copy-start.9 = (bf16[128,1,16,1,64]{0,4,2,3,1:T(8,128)(2,1)}, bf16[128,1,16,1,64]{0,4,2,3,1:T(8,128)(2,1)S(1)}, u32[]{:S(2)}) copy-start(bf16[128,1,16,1,64]{0,4,2,3,1:T(8,128)(2,1)S(1)} %copy.137) | copy-start | bytes 786436
  152.5 0.7 copy-start.33
  152.5 2.6 copy-start.17
  153.2 0.6 copy-start.24
  154.6 0.6 copy-start.19
  154.7 0.6 copy-start.26
  251.8 7.7 %copy-start.15 = (pred[128,2]{1,0:T(8,128)(4,1)S(1)}, pred[128,2]{1,0:T(8,128)(4,1)}, u32[]{:S(2)}) copy-start(pred[128,2]{1,0:T(8,128)(4,1)} %copy.139) | copy-start | bytes 772
  251.8 7.7 %copy-start.16 = (pred[128,2]{1,0:T(8,128)(4,1)S(1)}, pred[128,2]{1,0:T(8,128)(4,1)}, u32[]{:S(2)}) copy-start(pred[128,2]{1,0:T(8,128)(4,1)} %copy.145) | copy-start | bytes 772
  252.2 15.9 %copy-start.20 = (f32[128,2]{0,1:T(2,128)S(1)}, f32[128,2]{0,1:T(2,128)}, u32[]{:S(2)}) copy-start(f32[128,2]{0,1:T(2,128)} %copy-done.19) | copy-start | bytes 3076
  252.2 15.9 %copy-start.32 = (f32[128]{0:T(128)S(1)}, f32[128]{0:T(128)}, u32[]{:S(2)}) copy-start(f32[128]{0:T(128)} %multiply_divide_fusion.1) | copy-start | bytes 1540
  252.2 16.0 %copy-start.27 = (f32[128]{0:T(128)S(1)}, f32[128]{0:T(128)}, u32[]{:S(2)}) copy-start(f32[128]{0:T(128)} %copy-done.26) | copy-start | bytes 1540
  252.2 16.0 %copy-start.23 = (s32[128,2]{0,1:T(2,128)S(1)}, s32[128,2]{0,1:T(2,128)}, u32[]{:S(2)}) copy-start(s32[128,2]{0,1:T(2,128)} %param.23) | copy-start | bytes 3076
  252.3 16.0 %copy-start.31 = (f32[128]{0:T(128)S(1)}, f32[128]{0:T(128)}, u32[]{:S(2)}) copy-start(f32[128]{0:T(128)} %multiply_divide_fusion) | copy-start | bytes 1540
  252.3 16.0 %copy-start.18 = (f32[128]{0:T(128)S(1)}, f32[128]{0:T(128)}, u32[]{:S(2)}) copy-start(f32[128]{0:T(128)} %copy-done.17) | copy-start | bytes 1540
  252.3 16.0 %copy-start.25 = (f32[128]{0:T(128)S(1)}, f32[128]{0:T(128)}, u32[]{:S(2)}) copy-start(f32[128]{0:T(128)} %copy-done.24) | copy-start | bytes 1540
  252.3 16.8 %copy-start.34 = (f32[128]{0:T(128)S(1)}, f32[128]{0:T(128)}, u32[]{:S(2)}) copy-start(f32[128]{0:T(128)} %copy-done.33) | copy-start | bytes 1540
  288.4 21.2 %slice-start = ((s8[16777216]{0:T(1024)(128)(4,1)}), s8[4194304]{0:T(1024)(128)(4,1)S(1)}, s32[]{:S(2)}) async-start(s8[16777216]{0:T(1024)(128)(4,1)} %bitcast.121), calls=%async_computation.7 | async-start | bytes 8388608
  296.0 13.7 %slice-start.1 = ((s8[16777216]{0:T(1024)(128)(4,1)}), s8[4194304]{0:T(1024)(128)(4,1)S(1)}, s32[]{:S(2)}) async-start(s8[16777216]{0:T(1024)(128)(4,1)} %bitcast.121), calls=%async_computation.8 | async-start | bytes 8388608
  296.0 13.7 %slice-start.2 = ((s8[16777216]{0:T(1024)(128)(4,1)}), s8[4194304]{0:T(1024)(128)(4,1)S(1)}, s32[]{:S(2)}) async-start(s8[16777216]{0:T(1024)(128)(4,1)} %bitcast.121), calls=%async_computation.9 | async-start | bytes 8388608
  296.0 15.2 %slice-start.3 = ((s8[16777216]{0:T(1024)(128)(4,1)}), s8[4194304]{0:T(1024)(128)(4,1)S(1)}, s32[]{:S(2)}) async-start(s8[16777216]{0:T(1024)(128)(4,1)} %bitcast.121), calls=%async_computation.10 | async-start | bytes 8388608
  322.0 6.2 %copy-start.4 = (bf16[2048,2048]{0,1:T(8,128)(2,1)S(1)}, bf16[2048,2048]{0,1:T(8,128)(2,1)}, u32[]{:S(2)}) copy-start(bf16[2048,2048]{0,1:T(8,128)(2,1)} %multiply_convert_fusion) | copy-start | bytes 25165828
  329.8 10.5 %copy-start.10 = (bf16[128,1,16,1,64]{0,4,2,3,1:T(8,128)(2,1)S(1)}, bf16[128,1,16,1,64]{0,4,2,3,1:T(8,128)(2,1)}, u32[]{:S(2)}) copy-start(bf16[128,1,16,1,64]{0,4,2,3,1:T(8,128)(2,1)} %copy-done.9) | copy-start | bytes 786436
  329.9 27.4 %copy-start.13 = (f32[1024]{0:T(1024)S(1)}, f32[1024]{0:T(1024)}, u32[]{:S(2)}) copy-start(f32[1024]{0:T(1024)} %param.15) | copy-start | bytes 12292
  336.6 15.3 %all-to-all-start.3 = ((bf16[16,2,12288]{2,1,0:T(2,128)(2,1)}), bf16[16,2,12288]{2,1,0:T(2,128)(2,1)S(1)}, u32[]{:S(2)}, u32[]{:S(2)}) async-start(bf16[16,2,12288]{2,1,0:T(2,128)(2,1)} %reshape.379), calls=%async_computation.3 | async-start | bytes 1572864 | tf_op jit(solution)/shard_map/all_to_all | solution.py:453
  340.2 217.5 %all-reduce.3.cloned.1.call-start = ((), (), s32[]{:S(2)}) async-start(), calls=%async_computation.6 | async-start | bytes 16777216 | tf_op jit(solution)/shard_map/psum | solution.py:558
  362.0 206.4 %reduce-scatter.2.cloned.1.call-start = ((), (), s32[]{:S(2)}) async-start(), calls=%async_computation.5 | async-start | bytes 5406720 | tf_op jit(solution)/shard_map/reduce_scatter | solution.py:561
  362.6 79.4 %copy-start.30 = (f32[128]{0:T(128)S(1)}, f32[128]{0:T(128)}, u32[]{:S(2)}) copy-start(f32[128]{0:T(128)} %copy-done.29) | copy-start | bytes 1540
  557.7 4.2 copy-start.6
  562.0 25.9 %copy-start.1 = (f32[1024,8]{0,1:T(8,128)S(1)}, f32[1024,8]{0,1:T(8,128)}, u32[]{:S(2)}) copy-start(f32[1024,8]{0,1:T(8,128)} %param.19) | copy-start | bytes 98308
  568.4 1.2 copy-start.3
Sparse Core Ops, SparseCore 0:
  362.1 195.5 all-reduce.2
Sparse Core Ops, SparseCore 1:
  365.0 54.7 reduce-scatter.1

commit v2 on v1

v2 whole, which is shorter than its diff:
```python
from functools import partial

import jax
import jax.numpy as jnp
from jax import lax
from jax.experimental import pallas as pl
from jax.experimental.pallas import tpu as pltpu
from jax.sharding import PartitionSpec as P

HEADS = 16
EPSILON = 1e-06
HIGHEST = lax.Precision.HIGHEST
MESH = pl.DeviceIdType.MESH
F32 = jnp.float32
BF16 = jnp.bfloat16
VMEM = pltpu.VMEM
ROWS = 40
FFB = 176
FFQ = 704
DB = 256
NT = (((1,), (1,)), ((), ()))
TN = (((0,), (0,)), ((), ()))


def dot(a, b):
    return jnp.dot(a, b, preferred_element_type=F32)


def dot_nt(a, b):
    return lax.dot_general(a, b, NT, preferred_element_type=F32)


def dot_tn(a, b):
    return lax.dot_general(a, b, TN, preferred_element_type=F32)


def spot():
    m = lax.axis_index("mp")
    return lax.axis_index("dp"), lax.axis_index("expert"), m, m // 4, m % 4


def params(cid, mb=60):
    return pltpu.CompilerParams(
        collective_id=cid, has_side_effects=True, vmem_limit_bytes=mb * 1024 * 1024
    )


def swapped(c, z):
    return z % 2, 2 * (z // 2) + c


def mp_at(m, k):
    return {"mp": (m + k) % 16}


def y_at(z, y, d):
    return {"mp": z * 4 + (y + d) % 4}


def z_at(z, y, d):
    return {"mp": ((z + d) % 4) * 4 + y}


def push(src, dst, send, recv, device):
    return pltpu.make_async_remote_copy(
        src_ref=src, dst_ref=dst, send_sem=send, recv_sem=recv, device_id=device, device_id_type=MESH
    )


def lanes(at, size):
    return pl.ds(pl.multiple_of(at * size, size), size)


def greet_mp(barrier, m):
    def one(k, carry):
        pl.semaphore_signal(barrier, inc=1, device_id=mp_at(m, k), device_id_type=MESH)
        return carry

    lax.fori_loop(1, 16, one, 0)


def attend_kernel(
    x_ref,
    gain_ref,
    wq_ref,
    gate_ref,
    up_ref,
    down_ref,
    ctx_ref,
    qkv_ref,
    ctx_here_ref,
    lse_ref,
    nall_ref,
    w_out_ref,
    down_out_ref,
    normed,
    heads,
    blocks,
    stage,
    key_rows,
    ctx_low,
    here,
    s_send,
    s_recv,
    x_send,
    x_recv,
    a_send,
    a_recv,
    n_send,
    n_recv,
    c_send,
    c_recv,
):
    x, c, m, z, y = spot()
    pc, pz = swapped(c, z)
    away = (pc - c) * (pc - c)
    barrier = pltpu.get_barrier_semaphore()

    def remote(el):
        return (away == 1) | (el != y)

    def partner(el):
        return {"expert": pc, "mp": pz * 4 + el}

    greet_mp(barrier, m)
    for el in range(4):

        @pl.when(remote(el))
        def _():
            pl.semaphore_signal(barrier, inc=1, device_id=partner(el), device_id_type=MESH)

    for d in range(1, 4):
        pl.semaphore_signal(barrier, inc=1, device_id={"dp": (x + d) % 4}, device_id_type=MESH)

    for el in range(4):
        blocks[el, 0] = gate_ref[el].T.astype(BF16)
        blocks[el, 1] = up_ref[el].T.astype(BF16)
        blocks[el, 2] = down_ref[el].astype(BF16)
    pl.semaphore_wait(barrier, 15 + 6 + away)

    def units(at):
        return stage.at[:, pl.ds(pl.multiple_of(at * FFB, 16), FFB), :]

    def block_out(el):
        return push(blocks.at[el], units(y), s_send.at[el], s_recv.at[y], partner(el))

    def block_in(el):
        return push(blocks.at[el], units(el), s_send.at[el], s_recv.at[el], partner(el))

    for el in range(4):

        @pl.when(remote(el))
        def _():
            block_out(el).start()

    xf = x_ref[...].astype(F32)
    scale = lax.rsqrt(jnp.mean(xf * xf, axis=-1, keepdims=True) + EPSILON)
    normed[...] = (xf * scale * gain_ref[...]).astype(BF16)
    half = 512

    def near(part, d):
        cols = pl.ds(part * half, half)
        device = y_at(z, y, d) if part == 0 else z_at(z, y, d)
        return lambda at: push(
            normed.at[:, cols],
            nall_ref.at[at // 4, at % 4, :, cols],
            n_send.at[part, 0, d],
            n_recv.at[part, 0, d],
            device,
        )

    def far(part, d):
        cols = pl.ds(part * half, half)
        if part == 0:
            return lambda at: push(
                nall_ref.at[z, :, :, cols],
                nall_ref.at[at // 4, :, :, cols],
                n_send.at[part, 1, d],
                n_recv.at[part, 1, d],
                z_at(z, y, d),
            )
        return lambda at: push(
            nall_ref.at[:, y, :, cols],
            nall_ref.at[:, at % 4, :, cols],
            n_send.at[part, 1, d],
            n_recv.at[part, 1, d],
            y_at(z, y, d),
        )

    y_from = [z * 4 + (y + 4 - d) % 4 for d in range(4)]
    z_from = [((z + 4 - d) % 4) * 4 + y for d in range(4)]

    wide = 512
    for i in range(6):
        part = dot(normed[...], wq_ref[:, i * wide : (i + 1) * wide])
        heads[i // 2, (i % 2) * 8 : (i % 2) * 8 + 8] = part.T.astype(BF16).reshape(8, 64, 128)

    def head_out(k):
        t = (m + k) % 16
        return push(
            heads.at[:, t],
            qkv_ref.at[:, :, lanes(m, 128)],
            a_send.at[k],
            a_recv.at[k],
            mp_at(m, k),
        )

    def head_in(k):
        return push(
            heads.at[:, 0],
            qkv_ref.at[:, :, lanes((m + 16 - k) % 16, 128)],
            a_send.at[k],
            a_recv.at[k],
            mp_at(m, k),
        )

    def each(lo, hi, f):
        def one(k, carry):
            f(k)
            return carry

        lax.fori_loop(lo, hi, one, 0)

    each(1, 16, lambda k: head_out(k).start())
    own = pltpu.make_async_copy(heads.at[:, m], qkv_ref.at[:, :, lanes(m, 128)], here.at[0])
    own.start()
    mine = pltpu.make_async_copy(normed, nall_ref.at[z, y], here.at[1])
    mine.start()
    for d in (2, 1, 3):
        near(0, d)(m).start()
        near(1, d)(m).start()

    @pl.when(away == 0)
    def _():
        kept = pltpu.make_async_copy(blocks.at[y], units(y), here.at[2])
        kept.start()
        kept.wait()

    for el in range(4):

        @pl.when(remote(el))
        def _():
            block_in(el).wait_recv()

    def fan(d, at):
        return push(
            stage.at[:2],
            w_out_ref.at[:, :, lanes(at, DB)],
            x_send.at[d],
            x_recv.at[d],
            {"dp": (x + d) % 4},
        )

    for d in (2, 1, 3):
        fan(d, x).start()
    stay = pltpu.make_async_copy(stage.at[:2], w_out_ref.at[:, :, lanes(x, DB)], here.at[3])
    stay.start()
    down_out_ref[...] = stage[2]

    own.wait()
    each(1, 16, lambda k: head_in(k).wait_recv())
    for d in (2, 1, 3):
        near(0, d)(y_from[d]).wait_recv()
        near(1, d)(z_from[d]).wait_recv()
    mine.wait()
    for d in (2, 1, 3):
        far(0, d)(m).start()
        far(1, d)(m).start()

    key_rows[...] = qkv_ref[1].astype(F32).T.astype(BF16)

    def ctx_out(t):
        return push(
            ctx_low.at[:, lanes(t, 128)],
            ctx_ref.at[pl.ds(pl.multiple_of(m * 64, 64), 64), :],
            c_send.at[(t + 16 - m) % 16],
            c_recv.at[(t + 16 - m) % 16],
            {"mp": t},
        )

    def ctx_in(k):
        s = (m + 16 - k) % 16
        return push(
            ctx_low.at[:, pl.ds(0, 128)],
            ctx_ref.at[pl.ds(pl.multiple_of(s * 64, 64), 64), :],
            c_send.at[k],
            c_recv.at[k],
            {"mp": s},
        )

    def queries(i):
        b = (m // 2 + i) % 8
        cols = lanes(b, 256)
        q = (qkv_ref[0, :, cols].astype(F32) * 0.125).astype(BF16)
        s = dot(key_rows[...], q)
        top = jnp.max(s, axis=0, keepdims=True)
        p = jnp.exp(s - top)
        total = jnp.sum(p, axis=0, keepdims=True)
        ctx = dot(qkv_ref[2], p.astype(BF16)) / total
        lse_ref[:, cols] = top + jnp.log(total)
        ctx_here_ref[:, cols] = ctx
        ctx_low[:, cols] = ctx.astype(BF16)

    def pair(i, carry):
        queries(2 * i)
        queries(2 * i + 1)
        for u in range(2):
            b = (m // 2 + 2 * i + u) % 8
            for v in range(2):
                t = 2 * b + v

                @pl.when(t != m)
                def _():
                    ctx_out(t).start()

        return carry

    lax.fori_loop(0, 4, pair, 0)
    ctx_ref[pl.ds(pl.multiple_of(m * 64, 64), 64), :] = ctx_low[:, lanes(m, 128)]
    each(1, 16, lambda k: ctx_in(k).wait_recv())

    for d in (1, 2, 3):
        far(0, d)(z_from[d]).wait_recv()
        far(1, d)(y_from[d]).wait_recv()
        fan(d, (x + 4 - d) % 4).wait_recv()
    for d in (1, 2, 3):
        near(0, d)(m).wait_send()
        near(1, d)(m).wait_send()
        far(0, d)(m).wait_send()
        far(1, d)(m).wait_send()
        fan(d, x).wait_send()
    stay.wait()
    each(1, 16, lambda k: head_out(k).wait_send())
    each(1, 16, lambda k: ctx_in(k).wait_send())
    for el in range(4):

        @pl.when(remote(el))
        def _():
            block_out(el).wait_send()


def attend(block_input, gain, qkv_low, gate_weight, up_weight, down_weight):
    dma = pltpu.SemaphoreType.DMA
    vm = pl.BlockSpec(memory_space=VMEM)
    hbm = pl.BlockSpec(memory_space=pl.ANY)
    shape = jax.ShapeDtypeStruct
    return pl.pallas_call(
        attend_kernel,
        out_shape=(
            shape((1024, 128), BF16),
            shape((3, 64, 2048), BF16),
            shape((64, 2048), F32),
            shape((1, 2048), F32),
            shape((4, 4, 128, 1024), BF16),
            shape((2, FFQ, 4 * DB), BF16),
            shape((FFQ, DB), BF16),
        ),
        in_specs=[vm] * 6,
        out_specs=(vm, vm, vm, vm, hbm, hbm, vm),
        scratch_shapes=[
            VMEM((128, 1024), BF16),
            VMEM((3, 16, 64, 128), BF16),
            VMEM((4, 3, FFB, DB), BF16),
            VMEM((3, FFQ, DB), BF16),
            VMEM((2048, 64), BF16),
            VMEM((64, 2048), BF16),
            dma((4,)),
            dma((4,)),
            dma((4,)),
            dma((4,)),
            dma((4,)),
            dma((16,)),
            dma((16,)),
            dma((2, 2, 4)),
            dma((2, 2, 4)),
            dma((16,)),
            dma((16,)),
        ],
        compiler_params=params(1, 60),
    )(block_input, gain.reshape(1, -1), qkv_low, gate_weight, up_weight, down_weight)


GELU_A = 0.7978845608
GELU_B = 0.044715


def moe_kernel(
    send_ref,
    w_ref,
    down_ref,
    ret_ref,
    grad_ref,
    recv,
    own_part,
    sib_send,
    sib_recv,
    back,
    xs,
    cs,
    hid,
    gcs,
    ucs,
    down,
    here,
    x_send,
    x_recv,
    d_send,
    d_recv,
    f_send,
    f_recv,
    p_send,
    p_recv,
    r_send,
    r_recv,
):
    x, c, m, z, y = spot()
    barrier = pltpu.get_barrier_semaphore()

    def greet(k, carry):
        pl.semaphore_signal(barrier, inc=1, device_id={"mp": (m + k) % 16}, device_id_type=MESH)
        return carry

    lax.fori_loop(1, 16, greet, 0)
    pl.semaphore_signal(barrier, inc=1, device_id={"expert": 1 - c}, device_id_type=MESH)
    for d in range(1, 4):
        pl.semaphore_signal(barrier, inc=1, device_id={"dp": (x + d) % 4}, device_id_type=MESH)
    pl.semaphore_wait(barrier, 19)

    def fan(d, at):
        return push(
            down_ref, down.at[:, lanes(at, DB)], x_send.at[d], x_recv.at[d], {"dp": (x + d) % 4}
        )

    for d in (2, 1, 3):
        fan(d, x).start()
    stay = pltpu.make_async_copy(down_ref, down.at[:, lanes(x, DB)], here.at[0])
    stay.start()

    def expert_of(t):
        return ((t // 4) % 2) * 4 + t % 4

    def dispatch(k):
        t = (m + k) % 16
        return pltpu.make_async_remote_copy(
            src_ref=send_ref.at[expert_of(t)],
            dst_ref=recv.at[0, k],
            send_sem=d_send.at[k],
            recv_sem=d_recv.at[k],
            device_id={"mp": t},
            device_id_type=MESH,
        )

    def forward(k):
        return pltpu.make_async_remote_copy(
            src_ref=recv.at[0, k],
            dst_ref=recv.at[1, k],
            send_sem=f_send.at[k],
            recv_sem=f_recv.at[k],
            device_id={"expert": 1 - c},
            device_id_type=MESH,
        )

    def partials(j):
        return pltpu.make_async_remote_copy(
            src_ref=sib_send.at[j],
            dst_ref=sib_recv.at[j],
            send_sem=p_send.at[j],
            recv_sem=p_recv.at[j],
            device_id={"expert": 1 - c},
            device_id_type=MESH,
        )

    def giving(k):
        return pltpu.make_async_remote_copy(
            src_ref=back.at[k],
            dst_ref=ret_ref.at[m],
            send_sem=r_send.at[k],
            recv_sem=r_recv.at[k],
            device_id={"mp": (m + 16 - k) % 16},
            device_id_type=MESH,
        )

    def start_dispatch(k, carry):
        dispatch(k).start()
        return carry

    lax.fori_loop(1, 16, start_dispatch, 0)
    recv[0, 0] = send_ref[expert_of(m)]

    def finish(j):
        partials(j).wait_recv()
        back[pl.ds(4 * j, 4)] = (own_part[...] + sib_recv[j].astype(F32)).astype(BF16)
        for i in range(4):
            k = 4 * j + i

            @pl.when(k > 0)
            def _():
                giving(k).start()

            @pl.when(k == 0)
            def _():
                ret_ref[m] = back[0]

    def chunk(j, carry):
        for i in range(4):
            k = 4 * j + i

            @pl.when(k > 0)
            def _():
                dispatch(k).wait_recv()

            forward(k).start()

        @pl.when(j > 0)
        def _():
            finish(j - 1)

        for i in range(4):
            forward(4 * j + i).wait_recv()
        blk = recv[:, pl.ds(4 * j, 4)].astype(F32)
        span = pl.ds(pl.multiple_of(j * 8 * ROWS, 16), 8 * ROWS)
        xs[span] = blk[:, :, :ROWS].reshape(8 * ROWS, 4 * DB).astype(BF16)
        cs[span] = blk[:, :, ROWS:].reshape(8 * ROWS, 4 * DB).astype(BF16)
        gate = dot_nt(xs[span], w_ref[0])
        up = dot_nt(xs[span], w_ref[1])
        hid_cot = dot_nt(cs[span], down[...])
        sq = gate * gate
        th = jnp.tanh(GELU_A * (gate + GELU_B * (gate * sq)))
        half = 0.5 * (1.0 + th)
        act = gate * half
        slope = half + 0.5 * gate * (1.0 - th * th) * (GELU_A * (1.0 + 3.0 * GELU_B * sq))
        hid[span] = (act * up).astype(BF16)
        gcs[span] = (hid_cot * up * slope).astype(BF16)
        ucs[span] = (hid_cot * act).astype(BF16)
        out = dot(hid[span], down[...]).reshape(2, 4, ROWS, 4 * DB)
        rows = (dot(gcs[span], w_ref[0]) + dot(ucs[span], w_ref[1])).reshape(2, 4, ROWS, 4 * DB)
        own_part[:, :ROWS] = out[0]
        own_part[:, ROWS:] = rows[0]
        sib_send[j] = jnp.concatenate([out[1], rows[1]], axis=1).astype(BF16)
        partials(j).start()
        return carry

    stay.wait()
    for d in (1, 2, 3):
        fan(d, (x + 4 - d) % 4).wait_recv()
    lax.fori_loop(0, 4, chunk, 0)
    finish(3)
    for i, (a, b) in enumerate(((gcs, xs), (ucs, xs), (hid, cs))):
        g = dot_tn(a[...], b[...])
        for at in range(4):
            grad_ref[at, i] = g[:, at * DB : (at + 1) * DB].astype(BF16)

    def drain(k, carry):
        pltpu.make_async_remote_copy(
            src_ref=back.at[k],
            dst_ref=ret_ref.at[(m + k) % 16],
            send_sem=r_send.at[k],
            recv_sem=r_recv.at[k],
            device_id={"mp": (m + 16 - k) % 16},
            device_id_type=MESH,
        ).wait()
        dispatch(k).wait_send()
        forward(k).wait_send()
        return carry

    lax.fori_loop(1, 16, drain, 0)
    forward(0).wait_send()
    for d in (1, 2, 3):
        fan(d, x).wait_send()
    for j in range(4):
        partials(j).wait_send()


def moe(send, weights, down):
    dma = pltpu.SemaphoreType.DMA
    block = (2 * ROWS, 4 * DB)
    return pl.pallas_call(
        moe_kernel,
        out_shape=(
            jax.ShapeDtypeStruct((16, *block), BF16),
            jax.ShapeDtypeStruct((4, 3, FFQ, DB), BF16),
        ),
        in_specs=[pl.BlockSpec(memory_space=VMEM)] * 3,
        out_specs=(pl.BlockSpec(memory_space=VMEM),) * 2,
        scratch_shapes=[
            VMEM((2, 16, *block), BF16),
            VMEM((4, *block), F32),
            VMEM((4, 4, *block), BF16),
            VMEM((4, 4, *block), BF16),
            VMEM((16, *block), BF16),
            VMEM((32 * ROWS, 4 * DB), BF16),
            VMEM((32 * ROWS, 4 * DB), BF16),
            VMEM((32 * ROWS, FFQ), BF16),
            VMEM((32 * ROWS, FFQ), BF16),
            VMEM((32 * ROWS, FFQ), BF16),
            VMEM((FFQ, 4 * DB), BF16),
            dma((1,)),
            dma((4,)),
            dma((4,)),
            dma((16,)),
            dma((16,)),
            dma((16,)),
            dma((16,)),
            dma((4,)),
            dma((4,)),
            dma((16,)),
            dma((16,)),
        ],
        compiler_params=params(3, 62),
    )(send, weights, down)


def attend_back_kernel(
    dctx_ref,
    qkv_ref,
    ctx_ref,
    lse_ref,
    nall_ref,
    wq_ref,
    x_ref,
    gain_ref,
    mid_ref,
    o_ref,
    few_ref,
    g_ref,
    in_ref,
    gain_out_ref,
    full_ref,
    g_out_ref,
    o_out_ref,
    few_out_ref,
    o_sib,
    o_half,
    o_mp,
    o_quarter,
    o_dp,
    few_mp,
    few_sum,
    few_rest,
    cot,
    key_rows,
    value_rows,
    row_dot,
    dk,
    dv,
    pc_here,
    pc_tok,
    slices,
    parts,
    g_in,
    g_sum,
    gain_row,
    gain_mp,
    gain_rest,
    here,
    a_send,
    a_recv,
    b_send,
    b_recv,
    q_send,
    q_recv,
    f_send,
    f_recv,
    t_send,
    t_recv,
    x_send,
    x_recv,
    s_send,
    s_recv,
    u_send,
    u_recv,
    v_send,
    v_recv,
    o_send,
    o_recv,
    om_send,
    om_recv,
    og_send,
    og_recv,
    ox_send,
    ox_recv,
    fm_send,
    fm_recv,
    fr_send,
    fr_recv,
):
    x, c, m, z, y = spot()
    pc, pz = swapped(c, z)
    away = (pc - c) * (pc - c)
    barrier = pltpu.get_barrier_semaphore()

    def remote(el):
        return (away == 1) | (el != y)

    def partner(el):
        return {"expert": pc, "mp": pz * 4 + el}

    def rest(r):
        return {"dp": (x + r % 4) % 4, "expert": (c + r // 4) % 2}

    def each(lo, hi, f):
        def one(k, carry):
            f(k)
            return carry

        lax.fori_loop(lo, hi, one, 0)

    greet_mp(barrier, m)
    for el in range(4):

        @pl.when(remote(el))
        def _():
            pl.semaphore_signal(barrier, inc=1, device_id=partner(el), device_id_type=MESH)

    for r in range(1, 8):
        pl.semaphore_signal(barrier, inc=1, device_id=rest(r), device_id_type=MESH)
    pl.semaphore_wait(barrier, 15 + 3 + away + 7)

    def cot_out(k):
        t = (m + k) % 16
        return push(dctx_ref.at[t], cot.at[:, lanes(m, 128)], a_send.at[k], a_recv.at[k], {"mp": t})

    def cot_in(k):
        s = (m + 16 - k) % 16
        return push(dctx_ref.at[0], cot.at[:, lanes(s, 128)], a_send.at[k], a_recv.at[k], {"mp": s})

    each(1, 16, lambda k: cot_out(k).start())
    cot[:, lanes(m, 128)] = dctx_ref[m]

    def fan(d):
        t = (x + d) % 4
        return push(g_ref.at[t], g_in.at[d], x_send.at[d], x_recv.at[d], {"dp": t})

    for d in (2, 1, 3):
        fan(d).start()
    keep = pltpu.make_async_copy(g_ref.at[x], g_in.at[0], here.at[0])
    keep.start()

    def halves():
        return push(
            o_ref.at[1 - c], o_sib, o_send.at[0], o_recv.at[0], {"expert": 1 - c}
        )

    def thirty(k):
        t = (m + k) % 16
        return push(o_half.at[t], o_mp.at[k], om_send.at[k], om_recv.at[k], {"mp": t})

    def quarters(d):
        t = (x + d) % 4
        return push(
            o_quarter.at[:, lanes(t, DB)], o_dp.at[d], ox_send.at[0, d], ox_recv.at[0, d], {"dp": t}
        )

    def regain(d, at):
        return push(
            o_out_ref.at[c, m, :, lanes(x, DB)],
            o_out_ref.at[c, m, :, lanes(at, DB)],
            ox_send.at[1, d],
            ox_recv.at[1, d],
            {"dp": (x + d) % 4},
        )

    def regather(k, at):
        return push(
            o_out_ref.at[c, m], o_out_ref.at[c, at], og_send.at[k], og_recv.at[k], mp_at(m, k)
        )

    def retwin(core):
        return push(
            o_out_ref.at[core], o_out_ref.at[core], o_send.at[1], o_recv.at[1], {"expert": 1 - c}
        )

    def few_near(k):
        return push(few_ref, few_mp.at[k], fm_send.at[k], fm_recv.at[k], mp_at(m, k))

    def few_far(r):
        return push(few_sum, few_rest.at[r], fr_send.at[r], fr_recv.at[r], rest(r))

    halves().start()
    key_rows[...] = qkv_ref[1].astype(F32).T.astype(BF16)
    value_rows[...] = qkv_ref[2].astype(F32).T.astype(BF16)
    dk[...] = jnp.zeros_like(dk)
    dv[...] = jnp.zeros_like(dv)
    each(1, 16, lambda k: cot_in(k).wait_recv())
    row_dot[...] = jnp.sum(cot[...].astype(F32) * ctx_ref[...], axis=0, keepdims=True)

    def queries(b):
        cols = lanes(b, 256)
        q = (qkv_ref[0, :, cols].astype(F32) * 0.125).astype(BF16)
        p = jnp.exp(dot(key_rows[...], q) - lse_ref[:, cols])
        dp = dot(value_rows[...], cot[:, cols])
        ds = (p * (dp - row_dot[:, cols])).astype(BF16)
        pc_here[0, :, cols] = (dot(qkv_ref[1], ds) * 0.125).astype(BF16)
        dk[...] += dot_nt(ds, q)
        dv[...] += dot_nt(p.astype(BF16), cot[:, cols])

    def pair(i, carry):
        queries(2 * i)
        queries(2 * i + 1)
        return carry

    pair(0, 0)
    halves().wait_recv()
    o_half[...] = (o_ref[c].astype(F32) + o_sib[...].astype(F32)).astype(BF16)
    each(1, 16, lambda k: thirty(k).start())
    each(1, 16, lambda k: few_near(k).start())
    lax.fori_loop(1, 4, pair, 0)
    pc_here[1] = dk[...].T.astype(BF16)
    pc_here[2] = dv[...].T.astype(BF16)

    def pc_out(k):
        t = (m + k) % 16
        return push(
            pc_here.at[:, :, lanes(t, 128)], pc_tok.at[:, m], b_send.at[k], b_recv.at[k], {"mp": t}
        )

    def pc_in(k):
        s = (m + 16 - k) % 16
        return push(
            pc_here.at[:, :, pl.ds(0, 128)], pc_tok.at[:, s], b_send.at[k], b_recv.at[k], {"mp": s}
        )

    each(1, 16, lambda k: pc_out(k).start())
    pc_tok[:, m] = pc_here[:, :, lanes(m, 128)]

    each(1, 16, lambda k: thirty(k).wait_recv())
    o_sum = o_half[m].astype(F32)
    for k in range(1, 16):
        o_sum += o_mp[k].astype(F32)
    o_quarter[...] = o_sum.astype(BF16)
    for d in (2, 1, 3):
        quarters(d).start()
    each(1, 16, lambda k: few_near(k).wait_recv())
    few_all = few_ref[...].astype(F32)
    for k in range(1, 16):
        few_all += few_mp[k].astype(F32)
    few_sum[...] = few_all.astype(BF16)
    for r in range(1, 8):
        few_far(r).start()

    slices[...] = dot(pc_here[...].reshape(192, 2048), nall_ref[...]).astype(BF16)

    def share_out(r):
        t = 2 * ((x + r % 4) % 4) + (c + r // 4) % 2
        return push(slices.at[:, lanes(t, 128)], parts.at[r], q_send.at[r], q_recv.at[r], rest(r))

    for r in range(1, 8):
        share_out(r).start()
    for d in (1, 2, 3):
        quarters(d).wait_recv()
    o_fin = o_quarter[:, lanes(x, DB)].astype(F32)
    for d in (1, 2, 3):
        o_fin += o_dp[d].astype(F32)
    o_out_ref[c, m, :, lanes(x, DB)] = o_fin.astype(BF16)
    for d in (2, 1, 3):
        regain(d, x).start()
    total = slices[:, lanes(2 * x + c, 128)].astype(F32)
    for r in range(1, 8):
        share_out(r).wait_recv()
    for r in range(1, 8):
        total += parts[r].astype(F32)
    full_ref[:, c, x, z, y] = total.astype(BF16).reshape(3, 64, 128)

    def along(axis, d):
        if axis == 0:
            return {"dp": (x + d) % 4}
        return z_at(z, y, d) if axis == 1 else y_at(z, y, d)

    orders = ((0, 2, 1), (2, 1, 0), (1, 0, 2))

    def spread(p, s, d, back):
        at = [x, z, y]
        axis = orders[p][s]
        if back:
            at[axis] = (at[axis] + 4 - d) % 4
        for done in orders[p][:s]:
            at[done] = slice(None)
        src = [x, z, y]
        for done in orders[p][:s]:
            src[done] = slice(None)
        return push(
            full_ref.at[(p, c, *src)],
            full_ref.at[(p, c, *at)],
            f_send.at[p, s, d],
            f_recv.at[p, s, d],
            along(axis, d),
        )

    def twin(p, back):
        core = 1 - c if back else c
        return push(
            full_ref.at[p, core],
            full_ref.at[p, core],
            t_send.at[p],
            t_recv.at[p],
            {"expert": 1 - c},
        )

    for p in range(3):
        for d in (2, 1, 3):
            spread(p, 0, d, False).start()

    each(1, 16, lambda k: pc_in(k).wait_recv())
    dn = dot(wq_ref[...], pc_tok[...].reshape(3072, 128)).T
    xf = x_ref[...].astype(F32)
    scale = lax.rsqrt(jnp.mean(xf * xf, axis=-1, keepdims=True) + EPSILON)
    hat = xf * scale
    gained = dn * gain_ref[...]
    in_ref[...] = mid_ref[...] + scale * (
        gained - hat * jnp.mean(gained * hat, axis=-1, keepdims=True)
    )
    gain_row[...] = jnp.sum(dn * hat, axis=0, keepdims=True)

    def gain_out(k):
        return push(gain_row, gain_mp.at[k], u_send.at[k], u_recv.at[k], mp_at(m, k))

    def gain_far(r):
        return push(gain_mp.at[0], gain_rest.at[r], v_send.at[r], v_recv.at[r], rest(r))

    each(1, 16, lambda k: gain_out(k).start())
    for d in (1, 2, 3):
        regain(d, (x + 4 - d) % 4).wait_recv()
    each(1, 16, lambda k: regather(k, m).start())
    for r in range(1, 8):
        few_far(r).wait_recv()
        few_all += few_rest[r].astype(F32)
    few_out_ref[...] = few_all

    for p in range(3):
        for d in (1, 2, 3):
            spread(p, 0, d, True).wait_recv()
    for p in range(3):
        for d in (2, 1, 3):
            spread(p, 1, d, False).start()

    each(1, 16, lambda k: gain_out(k).wait_recv())
    got = gain_row[...]
    for k in range(1, 16):
        got += gain_mp[k]
    gain_mp[0] = got
    for r in range(1, 8):
        gain_far(r).start()

    for p in range(3):
        for d in (1, 2, 3):
            spread(p, 1, d, True).wait_recv()
    for p in range(3):
        for d in (2, 1, 3):
            spread(p, 2, d, False).start()

    keep.wait()
    for d in (1, 2, 3):
        fan(d).wait_recv()
    for i in range(3):
        g_sum[i] = (
            g_in[0, i].astype(F32)
            + g_in[1, i].astype(F32)
            + g_in[2, i].astype(F32)
            + g_in[3, i].astype(F32)
        ).astype(BF16)

    def home_out(at):
        return push(
            g_sum.at[:, pl.ds(at * FFB, FFB), :],
            g_out_ref.at[y],
            s_send.at[at],
            s_recv.at[y],
            partner(at),
        )

    def home_in(at):
        return push(
            g_sum.at[:, pl.ds(at * FFB, FFB), :],
            g_out_ref.at[at],
            s_send.at[at],
            s_recv.at[at],
            partner(at),
        )

    for at in range(4):

        @pl.when(remote(at))
        def _():
            home_out(at).start()

    @pl.when(away == 0)
    def _():
        kept = pltpu.make_async_copy(
            g_sum.at[:, pl.ds(pl.multiple_of(y * FFB, 16), FFB), :], g_out_ref.at[y], here.at[1]
        )
        kept.start()
        kept.wait()

    each(1, 16, lambda k: regather(k, (m + 16 - k) % 16).wait_recv())
    retwin(c).start()
    for r in range(1, 8):
        gain_far(r).wait_recv()
    for r in range(1, 8):
        got += gain_rest[r]
    gain_out_ref[...] = got

    for p in range(3):
        for d in (1, 2, 3):
            spread(p, 2, d, True).wait_recv()
        twin(p, False).start()
    for at in range(4):

        @pl.when(remote(at))
        def _():
            home_in(at).wait_recv()

    retwin(1 - c).wait_recv()
    for p in range(3):
        twin(p, True).wait_recv()
    for p in range(3):
        twin(p, False).wait_send()
        for s in range(3):
            for d in (1, 2, 3):
                spread(p, s, d, False).wait_send()
    halves().wait_send()
    retwin(c).wait_send()
    each(1, 16, lambda k: thirty(k).wait_send())
    each(1, 16, lambda k: regather(k, m).wait_send())
    each(1, 16, lambda k: few_near(k).wait_send())
    for d in (1, 2, 3):
        quarters(d).wait_send()
        regain(d, x).wait_send()
    for r in range(1, 8):
        few_far(r).wait_send()
    each(1, 16, lambda k: cot_out(k).wait_send())
    each(1, 16, lambda k: pc_out(k).wait_send())
    each(1, 16, lambda k: gain_out(k).wait_send())
    for d in (1, 2, 3):
        fan(d).wait_send()
    for r in range(1, 8):
        share_out(r).wait_send()
        gain_far(r).wait_send()
    for at in range(4):

        @pl.when(remote(at))
        def _():
            home_out(at).wait_send()


def attend_back(
    dctx, qkv, ctx, lse, nall, qkv_low, block_input, gain, middle_cot, out_term, few, grads
):
    dma = pltpu.SemaphoreType.DMA
    vm = pl.BlockSpec(memory_space=VMEM)
    hbm = pl.BlockSpec(memory_space=pl.ANY)
    shape = jax.ShapeDtypeStruct
    return pl.pallas_call(
        attend_back_kernel,
        out_shape=(
            shape((128, 1024), F32),
            shape((1, 1024), F32),
            shape((3, 2, 4, 4, 4, 64, 128), BF16),
            shape((4, 3, FFB, DB), BF16),
            shape((2, 16, 32, 1024), BF16),
            shape((16, 1024), F32),
        ),
        in_specs=[vm] * 11 + [hbm],
        out_specs=(vm,) * 6,
        scratch_shapes=[
            VMEM((16, 32, 1024), BF16),
            VMEM((16, 32, 1024), BF16),
            VMEM((16, 32, 1024), BF16),
            VMEM((32, 1024), BF16),
            VMEM((4, 32, DB), BF16),
            VMEM((16, 16, 1024), BF16),
            VMEM((16, 1024), BF16),
            VMEM((8, 16, 1024), BF16),
            VMEM((64, 2048), BF16),
            VMEM((2048, 64), BF16),
            VMEM((2048, 64), BF16),
            VMEM((1, 2048), F32),
            VMEM((2048, 64), F32),
            VMEM((2048, 64), F32),
            VMEM((3, 64, 2048), BF16),
            VMEM((3, 16, 64, 128), BF16),
            VMEM((192, 1024), BF16),
            VMEM((8, 192, 128), BF16),
            VMEM((4, 3, FFQ, DB), BF16),
            VMEM((3, FFQ, DB), BF16),
            VMEM((1, 1024), F32),
            VMEM((16, 1, 1024), F32),
            VMEM((8, 1, 1024), F32),
            dma((2,)),
            dma((16,)),
            dma((16,)),
            dma((16,)),
            dma((16,)),
            dma((8,)),
            dma((8,)),
            dma((3, 3, 4)),
            dma((3, 3, 4)),
            dma((3,)),
            dma((3,)),
            dma((4,)),
            dma((4,)),
            dma((4,)),
            dma((4,)),
            dma((16,)),
            dma((16,)),
            dma((8,)),
            dma((8,)),
            dma((2,)),
            dma((2,)),
            dma((16,)),
            dma((16,)),
            dma((16,)),
            dma((16,)),
            dma((2, 4)),
            dma((2, 4)),
            dma((16,)),
            dma((16,)),
            dma((8,)),
            dma((8,)),
        ],
        compiler_params=params(2, 60),
    )(
        dctx,
        qkv,
        ctx,
        lse,
        nall.reshape(2048, 1024),
        qkv_low,
        block_input,
        gain.reshape(1, -1),
        middle_cot,
        out_term,
        few,
        grads,
    )


def unfold_kernel(g_ref, o_ref):
    o_ref[...] = g_ref[...].reshape(3072, 128).astype(F32).T


def unfold(full):
    return pl.pallas_call(
        unfold_kernel,
        out_shape=jax.ShapeDtypeStruct((1024, 3072), F32),
        grid=(4, 2),
        in_specs=[
            pl.BlockSpec((3, None, None, 4, 4, 64, 128), lambda i, j: (0, j, i, 0, 0, 0, 0)),
        ],
        out_specs=pl.BlockSpec((128, 3072), lambda i, j: (2 * i + j, 0)),
        compiler_params=pltpu.CompilerParams(vmem_limit_bytes=32 * 1024 * 1024),
    )(full)


def rms_norm(values, gain):
    return values * lax.rsqrt(jnp.mean(values * values, axis=-1, keepdims=True) + EPSILON) * gain


def gating(moe_in, router_weight, routes):
    logits = jnp.dot(moe_in, router_weight, precision=HIGHEST, preferred_element_type=F32)
    probs = jax.nn.softmax(logits, axis=-1)
    onehot = (routes[:, :, None] == jnp.arange(8, dtype=routes.dtype)).astype(F32)
    chosen = jnp.sum(probs[:, None, :] * onehot, axis=2)
    return chosen / jnp.sum(chosen, axis=1, keepdims=True)


def body(
    block_input,
    attn_gain,
    qkv_weight,
    out_weight,
    moe_gain,
    router_weight,
    gate_weight,
    up_weight,
    down_weight,
    routes,
    slot_index,
    cotangent,
):
    tok_rows, width = block_input.shape
    inputs = block_input.astype(F32)
    qkv_low = qkv_weight.astype(BF16)
    out_low = out_weight.astype(BF16)
    ctx_tok, qkv, ctx_here, lse, nall, weights, down = attend(
        block_input, attn_gain, qkv_low, gate_weight, up_weight, down_weight
    )
    context = ctx_tok.T
    middle = inputs + dot(context, out_low)
    moe_in, moe_back = jax.vjp(rms_norm, middle, moe_gain)
    gates, gate_back = jax.vjp(partial(gating, routes=routes), moe_in, router_weight)
    valid = slot_index < ROWS
    place = routes * (2 * ROWS) + slot_index
    keep = valid.astype(F32)
    upstream = cotangent.astype(F32)
    pair_rows = jnp.repeat(moe_in.astype(BF16), 2, axis=0)
    pair_cots = (gates[:, :, None] * upstream[:, None, :]).astype(BF16).reshape(2 * tok_rows, width)
    target = jnp.where(valid, place, 16 * ROWS).reshape(-1)
    cot_target = jnp.where(valid, place + ROWS, 16 * ROWS).reshape(-1)
    send = jnp.zeros((16 * ROWS, width), BF16)
    send = send.at[target].set(pair_rows, mode="drop").at[cot_target].set(pair_cots, mode="drop")
    returned, grads = moe(send.reshape(8, 2 * ROWS, width), weights, down)
    returned = returned.reshape(2, 8 * 2 * ROWS, width).astype(F32)
    returned = (returned[0] + returned[1]).astype(BF16)
    fetch_at = jnp.where(valid, place, 0)
    fetched = jnp.take(returned, fetch_at, axis=0).astype(F32) * keep[:, :, None]
    block_output = (middle + jnp.sum(gates[:, :, None] * fetched, axis=1)).astype(BF16)
    gate_cot = jnp.sum(upstream[:, None, :] * fetched, axis=2)
    moe_cot = jnp.sum(
        jnp.take(returned, fetch_at + ROWS, axis=0).astype(F32) * keep[:, :, None], axis=1
    )
    router_in_cot, router_term = gate_back(gate_cot)
    middle_norm_cot, moe_gain_term = moe_back(moe_cot + router_in_cot)
    middle_cot = upstream + middle_norm_cot
    branch_cot = middle_cot.astype(BF16)
    out_term = dot(ctx_tok, branch_cot)
    context_cot = dot_nt(out_low, branch_cot).astype(BF16).reshape(HEADS, 64, tok_rows)
    few = jnp.concatenate([router_term.T, moe_gain_term[None], jnp.zeros((7, width), F32)], axis=0)
    input_grad, gain_grad, full, mine, out_grad, few = attend_back(
        context_cot,
        qkv,
        ctx_here,
        lse,
        nall,
        qkv_low,
        block_input,
        attn_gain,
        middle_cot,
        out_term.astype(BF16).reshape(2, 16, 32, width),
        few.astype(BF16),
        grads,
    )
    mine = mine.astype(F32)
    return (
        block_output,
        input_grad,
        gain_grad.reshape(-1),
        unfold(full),
        out_grad.reshape(width, width).astype(F32),
        few[8],
        few[:8].T,
        jnp.swapaxes(mine[:, 0], 1, 2),
        jnp.swapaxes(mine[:, 1], 1, 2),
        mine[:, 2],
    )


def solution(mesh):
    tokens = P(("dp", "expert", "mp"), None)
    cols = P("expert", "dp", "mp")
    rows = P("expert", "mp", "dp")
    return jax.shard_map(
        body,
        mesh=mesh,
        in_specs=(tokens, P(), P(), P(), P(), P(), cols, cols, rows, tokens, tokens, tokens),
        out_specs=(tokens, tokens, P(), P(), P(), P(), P(), cols, cols, rows),
        check_vma=False,
    )
```

time: 605 us -> 361 us (0.60)
  waiting for transfers between devices: 135 us -> 0 us
  Pallas kernels: 168 us -> 280 us
  blocking collectives: 84 us -> 0 us
  matrix products: 72.3 us -> 7.56 us
  local copies, waits for them, and re-layouts: 47.7 us -> 23.6 us
  starting transfers between devices: 16.3 us -> 0 us
  between operations: 16.5 us -> 1.41 us
  other arithmetic: 56.1 us -> 45.4 us
    psum x1 -> x0, waiting for transfers between devices: 114 us -> none  [body(): qkv_grad = lax.psum(qkv_term.astype(BF16), everyone).astype(F32)]
    pallas_call x2 -> x3, Pallas kernels: 86 us -> 194 us  [the longest x1 119 us: attend_back(): pl.pallas_call(attend_back_kernel, out_shape=(shape((128, 1024), F32), sh...]
    psum x1 -> x0, blocking collectives: 70 us -> none  [body(): small = lax.psum(small, everyone)]
    dot_general x8 -> x0, matrix products: 51.2 us -> none  [the longest x1 13.6 us: attention_backward(): jnp.einsum('qhd,khd->hqk', context_cot, value_heads, preferred_element_ty...]
    all_to_all x3 -> x0, waiting for transfers between devices: 20 us -> none  [the longest x1 10.4 us: to_heads(): return lax.all_to_all(rows, 'mp', split_axis=2, concat_axis=0, tiled=True)]
    all_to_all x3 -> x0, starting transfers between devices: 16 us -> none  [the longest x1 8.6 us: to_heads(): return lax.all_to_all(rows, 'mp', split_axis=2, concat_axis=0, tiled=True)]
    all_to_all x1 -> x0, blocking collectives: 14 us -> none  [to_heads(): return lax.all_to_all(rows, 'mp', split_axis=2, concat_axis=0, tiled=True)]
    reduce_sum x1, other arithmetic: 8.57 us -> 22 us  [body(): gate_cot = jnp.sum(upstream[:, None, :] * fetched, axis=2)]
  transfers between devices with their start and end apart: 5 -> 0, of which waited for: 3 -> 0; matrix products, arithmetic and copies ran while one was open for 6% -> 0% of each run, Pallas kernels for 12% -> 0%
where the time goes in v2:
time: 361 us; the launch traced here: 358 us
  Pallas kernels  280 us (78%)
  other arithmetic  45.4 us (13%)
  local copies, waits for them, and re-layouts  23.6 us (7%)
  matrix products  7.56 us (2%)
    pallas_call x1, Pallas kernels, attend_back(): pl.pallas_call(attend_back_kernel, out_shape=(shape((128, 1024), F32), sh...  119 us
    pallas_call x1, Pallas kernels, moe(): pl.pallas_call(moe_kernel, out_shape=(jax.ShapeDtypeStruct((16, *block),...  85.5 us
    pallas_call x1, Pallas kernels, attend(): pl.pallas_call(attend_kernel, out_shape=(shape((1024, 128), BF16), shape(...  68.8 us
    reduce_sum x1, other arithmetic, body(): gate_cot = jnp.sum(upstream[:, None, :] * fetched, axis=2)  22 us
    convert_element_type x1, other arithmetic, body(): qkv_low = qkv_weight.astype(BF16)  8.25 us

profile of v2, /device:TPU:1, one launch (start us, length us, event | category | flops | bytes accessed | tf_op | source)
XLA Modules:
  0.0 357.6 jit_solution(15958899678202514805)
XLA Ops:
  0.7 0.6 pad.2.clone
  1.3 0.7 compare_and_fusion
  2.1 0.1 copy.57
  2.2 0.7 copy.63
  3.3 0.1 reshape.244
  3.7 0.1 reshape.198
  3.9 0.1 reshape.248
  4.1 1.9 convert_element_type.69
  6.0 2.4 copy.54.gate_ref
  8.4 1.3 copy.55.up_ref
  9.7 0.3 mul.169
  10.0 1.7 mul.170
  11.7 8.2 %convert_element_type.66.wq_ref = bf16[1024,3072]{1,0:T(8,128)(2,1)} convert(f32[1024,3072]{1,0:T(8,128)} %param.16) | non-fusion elementwise | flops 3145728 | bytes 18874368 | tf_op jit(solution)/shard_map/convert_element_type | solution.py:1182
  19.9 68.8 %shard_map.195 = (bf16[1024,128]{1,0:T(8,128)(2,1)}, bf16[3,64,2048]{2,1,0:T(8,128)(2,1)}, f32[64,2048]{1,0:T(8,128)}, f32[1,2048]{1,0:T(1,128)}, bf16[4,4,128,1...) custom-call(bf16[128,1024]{1,0:T(8,128)(2,1)} %x_ref.3, f32[1,1024]{1,0:T(1,128)} %bitcast.41, ...), custom_call_target="tpu_custom_call" | custom-call | tf_op jit(solution)/shard_map/pallas_call | solution.py:347
  88.8 2.8 multiply_reduce_fusion.5
  91.7 0.6 fusion.20
  92.3 0.5 multiply_divide_fusion
  93.0 0.5 multiply_divide_fusion.1
  93.6 0.1 div.69
  93.9 0.3 broadcast_in_dim.58
  94.2 1.0 reshape.228
  95.2 2.5 scatter_custom_fusion
  97.7 2.7 scatter_custom_fusion.1
  100.5 1.0 copy-done.4
  101.5 85.5 %shard_map.196 = (bf16[16,80,1024]{2,1,0:T(8,128)(2,1)}, bf16[4,3,704,256]{3,2,1,0:T(8,128)(2,1)}) custom-call(bf16[8,80,1024]{2,1,0:T(8,128)(2,1)} %bitcast.38, bf16[2,704,1024]{2,1,0:T(8,128)(2,1)} %get-tuple-element.27.w_ref, bf16[704,256]{1,0:T(8,128)(2,1)} %get-tuple-element.28.down_ref), custom_call_target="tpu_custom_call" | custom-call | tf_op jit(solution)/shard_map/pallas_call | solution.py:577
  187.0 2.4 convert_element_type.71
  189.4 0.4 fusion
  189.8 1.2 gather_fusion.1
  191.0 1.2 gather_fusion
  192.2 0.2 reshape.247
  192.5 1.0 reshape.251
  193.5 22.0 %multiply_reduce_fusion = (f32[128,2]{1,0:T(8,128)S(1)}, f32[128,1024]{1,0:T(8,128)S(1)}, f32[128,1024]{1,0:T(8,128)S(1)}) fusion(f32[128,2]{1,0:T(8,128)S(1)} %copy.62, f32[128,1024]{1,0:T(8,128)S(1)} %copy-done.10, bf16[128,2,1024]{2,1,0:T(2,128)(2,1)S(1)} %reshape.247, pred[128,2]{1,0:T(8,128)(4,1)S(1)} %copy.57, f32[128,2]{1,0:T(8,128)S(1)} %copy.56, ...), kind=kLoop, calls=%fused_computation.13 | loop fusion | flops 2621184 | bytes 2625024 | tf_op jit(solution)/shard_map/reduce_sum | solution.py:1207
  215.7 0.8 multiply_reduce_fusion.3
  216.6 0.9 fusion.6
  217.5 0.5 convolution_convert_fusion.2
  218.0 0.7 maximum_maximum_fusion.few_ref
  218.6 0.8 fusion.1
  219.5 0.8 copy.67
  220.3 2.0 convolution_convert_fusion
  222.4 118.8 %shard_map.197 = (f32[128,1024]{1,0:T(8,128)}, f32[1,1024]{1,0:T(1,128)}, bf16[3,2,4,4,4,64,128]{6,5,4,3,2,1,0:T(8,128)(2,1)}, bf16[4,3,176,256]{3,2,1,0:T(8,128...) custom-call(bf16[16,64,128]{2,1,0:T(8,128)(2,1)} %bitcast.40, ...), custom_call_target="tpu_custom_call" | custom-call | tf_op jit(solution)/shard_map/pallas_call | solution.py:1052
  341.2 1.4 slice.25
  342.5 1.4 slice_bitcast_fusion.3
  343.9 1.6 convert_element_type.84
  345.5 1.4 slice_bitcast_fusion
  346.9 2.6 bitcast_convert_fusion
  349.6 6.4 %shard_map.198 = f32[1024,3072]{1,0:T(8,128)} custom-call(bf16[3,2,4,4,4,64,128]{6,5,4,3,2,1,0:T(8,128)(2,1)S(1)} %bitcast.34), custom_call_target="tpu_custom_call" | custom-call | tf_op jit(solution)/shard_map/pallas_call | solution.py:1142
  356.0 0.8 copy.71
  356.8 0.6 copy.72
  (101 shorter events, 1.4 us)
Async XLA Ops:
  0.6 91.0 %copy-start = (f32[1024,8]{0,1:T(8,128)S(1)}, f32[1024,8]{0,1:T(8,128)}, u32[]{:S(2)}) copy-start(f32[1024,8]{0,1:T(8,128)} %param.19) | copy-start | bytes 98308
  0.7 7.7 %copy-start.12 = (f32[4,256,176]{1,2,0:T(8,128)S(1)}, f32[4,256,176]{1,2,0:T(8,128)}, u32[]{:S(2)}) copy-start(f32[4,256,176]{1,2,0:T(8,128)} %param.21) | copy-start | bytes 2162692
  4.1 5.6 %copy-start.7 = (bf16[128,1024]{1,0:T(8,128)(2,1)S(1)}, bf16[128,1024]{1,0:T(8,128)(2,1)}, u32[]{:S(2)}) copy-start(bf16[128,1024]{1,0:T(8,128)(2,1)} %param.25) | copy-start | bytes 786436
  19.9 68.8 %copy-start.6 = (bf16[128,1024]{1,0:T(8,128)(2,1)S(1)}, bf16[128,1024]{1,0:T(8,128)(2,1)}, u32[]{:S(2)}) copy-start(bf16[128,1024]{1,0:T(8,128)(2,1)} %x_ref.3) | copy-start | bytes 786436
  88.8 2.9 copy-start.14
  88.8 4.1 %copy-start.22 = (s32[128,2]{0,1:T(2,128)S(1)}, s32[128,2]{0,1:T(2,128)}, u32[]{:S(2)}) copy-start(s32[128,2]{0,1:T(2,128)} %param.23) | copy-start | bytes 3076
  91.6 1.3 copy-start.32
  91.7 6.0 %copy-start.18 = (f32[128]{0:T(128)}, f32[128]{0:T(128)S(1)}, u32[]{:S(2)}) copy-start(f32[128]{0:T(128)S(1)} %fusion.19) | copy-start | bytes 1540
  92.3 1.2 copy-start.16
  92.3 5.4 %copy-start.5 = (f32[256,1024]{1,0:T(8,128)S(1)}, f32[256,1024]{1,0:T(8,128)}, u32[]{:S(2)}) copy-start(f32[256,1024]{1,0:T(8,128)} %mul.170) | copy-start | bytes 3145732
  92.3 0.6 copy-start.24
  92.9 0.6 copy-start.20
  93.0 0.6 copy-start.26
  100.4 1.1 copy-start.4
  192.1 1.3 copy-start.10
  192.1 1.3 copy-start.15
  192.4 23.2 %copy-start.21 = (f32[128,2]{0,1:T(2,128)S(1)}, f32[128,2]{0,1:T(2,128)}, u32[]{:S(2)}) copy-start(f32[128,2]{0,1:T(2,128)} %copy-done.20) | copy-start | bytes 3076
  192.4 23.2 %copy-start.31 = (f32[128]{0:T(128)S(1)}, f32[128]{0:T(128)}, u32[]{:S(2)}) copy-start(f32[128]{0:T(128)} %multiply_divide_fusion.1) | copy-start | bytes 1540
  192.4 23.2 %copy-start.27 = (f32[128]{0:T(128)S(1)}, f32[128]{0:T(128)}, u32[]{:S(2)}) copy-start(f32[128]{0:T(128)} %copy-done.26) | copy-start | bytes 1540
  192.4 23.2 %copy-start.23 = (s32[128,2]{0,1:T(2,128)S(1)}, s32[128,2]{0,1:T(2,128)}, u32[]{:S(2)}) copy-start(s32[128,2]{0,1:T(2,128)} %param.23) | copy-start | bytes 3076
  192.4 23.2 %copy-start.17 = (f32[128]{0:T(128)S(1)}, f32[128]{0:T(128)}, u32[]{:S(2)}) copy-start(f32[128]{0:T(128)} %copy-done.16) | copy-start | bytes 1540
  192.4 23.2 %copy-start.30 = (f32[128]{0:T(128)S(1)}, f32[128]{0:T(128)}, u32[]{:S(2)}) copy-start(f32[128]{0:T(128)} %multiply_divide_fusion) | copy-start | bytes 1540
  192.4 23.3 %copy-start.19 = (f32[128]{0:T(128)S(1)}, f32[128]{0:T(128)}, u32[]{:S(2)}) copy-start(f32[128]{0:T(128)} %copy-done.18) | copy-start | bytes 1540
  192.4 23.3 %copy-start.25 = (f32[128]{0:T(128)S(1)}, f32[128]{0:T(128)}, u32[]{:S(2)}) copy-start(f32[128]{0:T(128)} %copy-done.24) | copy-start | bytes 1540
  193.5 23.1 %copy-start.33 = (f32[128]{0:T(128)S(1)}, f32[128]{0:T(128)}, u32[]{:S(2)}) copy-start(f32[128]{0:T(128)} %copy-done.32) | copy-start | bytes 1540
  193.5 23.1 %copy-start.8 = (bf16[128,1024]{1,0:T(8,128)(2,1)S(1)}, bf16[128,1024]{1,0:T(8,128)(2,1)}, u32[]{:S(2)}) copy-start(bf16[128,1024]{1,0:T(8,128)(2,1)} %param.25) | copy-start | bytes 786436
  215.7 2.2 copy-start.29
  215.7 2.9 copy-start.2
  217.5 2.9 copy-start.3
  218.6 1.7 copy-start.11
  343.9 3.0 copy-start.9
  343.9 5.6 %slice-start = ((s8[6291456]{0:T(1024)(128)(4,1)}), s8[4194304]{0:T(1024)(128)(4,1)S(1)}, s32[]{:S(2)}) async-start(s8[6291456]{0:T(1024)(128)(4,1)} %bitcast.33), calls=%async_computation | async-start | bytes 8388608
  345.5 4.0 %slice-start.1 = ((s8[6291456]{0:T(1024)(128)(4,1)}), s8[2097152]{0:T(1024)(128)(4,1)S(1)}, s32[]{:S(2)}) async-start(s8[6291456]{0:T(1024)(128)(4,1)} %bitcast.33), calls=%async_computation.1 | async-start | bytes 4194304
  349.5 6.5 %copy-start.13 = (f32[128,1024]{1,0:T(8,128)S(1)}, f32[128,1024]{1,0:T(8,128)}, u32[]{:S(2)}) copy-start(f32[128,1024]{1,0:T(8,128)} %get-tuple-element.78) | copy-start | bytes 1572868
  349.5 7.3 %copy-start.28 = (f32[1,1024]{1,0:T(1,128)S(1)}, f32[1,1024]{1,0:T(1,128)}, u32[]{:S(2)}) copy-start(f32[1,1024]{1,0:T(1,128)} %get-tuple-element.36) | copy-start | bytes 12292
  349.5 7.8 %copy-start.1 = (f32[1024,8]{0,1:T(8,128)S(1)}, f32[1024,8]{0,1:T(8,128)}, u32[]{:S(2)}) copy-start(f32[1024,8]{0,1:T(8,128)} %param.19) | copy-start | bytes 98308

commit v3 on v2

--- a/solution.py
+++ b/solution.py
@@ -1,5 +1,3 @@
-from functools import partial
-
 import jax
 import jax.numpy as jnp
 from jax import lax
@@ -7,7 +5,6 @@
 from jax.experimental.pallas import tpu as pltpu
 from jax.sharding import PartitionSpec as P
 
-HEADS = 16
 EPSILON = 1e-06
 HIGHEST = lax.Precision.HIGHEST
 MESH = pl.DeviceIdType.MESH
@@ -79,20 +76,58 @@
     lax.fori_loop(1, 16, one, 0)
 
 
+def places(routes, slots):
+    return jnp.where(slots < ROWS, routes * (2 * ROWS) + slots, -1.0)
+
+
+def picks(columns):
+    lane = lax.broadcasted_iota(jnp.int32, (128, 8), 1).astype(F32)
+    return [(columns[:, j : j + 1] == lane).astype(F32) for j in range(2)]
+
+
+def gates_of(probs, hot):
+    chosen = [jnp.sum(probs * h, axis=1, keepdims=True) for h in hot]
+    total = chosen[0] + chosen[1]
+    return [v / total for v in chosen], total
+
+
+def exact(a, b, dims):
+    return lax.dot_general(a, b, dims, precision=HIGHEST, preferred_element_type=F32)
+
+
+def unit(v):
+    scale = lax.rsqrt(jnp.mean(v * v, axis=-1, keepdims=True) + EPSILON)
+    return v * scale, scale
+
+
 def attend_kernel(
     x_ref,
     gain_ref,
-    wq_ref,
     gate_ref,
     up_ref,
     down_ref,
+    moe_gain_ref,
+    router_ref,
+    pairs_ref,
+    cot_ref,
+    wq_hbm,
+    wo_hbm,
+    send_ref,
+    mid_ref,
+    probs_ref,
     ctx_ref,
     qkv_ref,
     ctx_here_ref,
     lse_ref,
+    down_out_ref,
     nall_ref,
     w_out_ref,
-    down_out_ref,
+    wq_out_ref,
+    wo_out_ref,
+    wq_wide,
+    wo_wide,
+    wq_ref,
+    wo_ref,
     normed,
     heads,
     blocks,
@@ -132,9 +167,24 @@
     for d in range(1, 4):
         pl.semaphore_signal(barrier, inc=1, device_id={"dp": (x + d) % 4}, device_id_type=MESH)
 
+    wide = 512
+
+    def load(i):
+        cols = pl.ds(i * wide, wide)
+        return pltpu.make_async_copy(wq_hbm.at[:, cols], wq_wide.at[:, cols], here.at[4 + i])
+
+    def save(i):
+        cols = pl.ds(i * wide, wide)
+        return pltpu.make_async_copy(wq_ref.at[:, cols], wq_out_ref.at[:, cols], here.at[4 + i])
+
+    load_o = pltpu.make_async_copy(wo_hbm, wo_wide, here.at[10])
+    save_o = pltpu.make_async_copy(wo_ref, wo_out_ref, here.at[10])
+    for i in range(6):
+        load(i).start()
+    load_o.start()
     for el in range(4):
-        blocks[el, 0] = gate_ref[el].T.astype(BF16)
-        blocks[el, 1] = up_ref[el].T.astype(BF16)
+        blocks[el, 0] = gate_ref[el].astype(BF16)
+        blocks[el, 1] = up_ref[el].astype(BF16)
         blocks[el, 2] = down_ref[el].astype(BF16)
     pl.semaphore_wait(barrier, 15 + 6 + away)
 
@@ -153,9 +203,7 @@
         def _():
             block_out(el).start()
 
-    xf = x_ref[...].astype(F32)
-    scale = lax.rsqrt(jnp.mean(xf * xf, axis=-1, keepdims=True) + EPSILON)
-    normed[...] = (xf * scale * gain_ref[...]).astype(BF16)
+    normed[...] = (unit(x_ref[...].astype(F32))[0] * gain_ref[...]).astype(BF16)
     half = 512
 
     def near(part, d):
@@ -190,9 +238,12 @@
     y_from = [z * 4 + (y + 4 - d) % 4 for d in range(4)]
     z_from = [((z + 4 - d) % 4) * 4 + y for d in range(4)]
 
-    wide = 512
     for i in range(6):
-        part = dot(normed[...], wq_ref[:, i * wide : (i + 1) * wide])
+        load(i).wait()
+        cols = slice(i * wide, (i + 1) * wide)
+        wq_ref[:, cols] = wq_wide[:, cols].astype(BF16)
+        save(i).start()
+        part = dot(normed[...], wq_ref[:, cols])
         heads[i // 2, (i % 2) * 8 : (i % 2) * 8 + 8] = part.T.astype(BF16).reshape(8, 64, 128)
 
     def head_out(k):
@@ -256,6 +307,9 @@
     stay = pltpu.make_async_copy(stage.at[:2], w_out_ref.at[:, :, lanes(x, DB)], here.at[3])
     stay.start()
     down_out_ref[...] = stage[2]
+    load_o.wait()
+    wo_ref[...] = wo_wide[...].astype(BF16)
+    save_o.start()
 
     own.wait()
     each(1, 16, lambda k: head_in(k).wait_recv())
@@ -319,6 +373,26 @@
     ctx_ref[pl.ds(pl.multiple_of(m * 64, 64), 64), :] = ctx_low[:, lanes(m, 128)]
     each(1, 16, lambda k: ctx_in(k).wait_recv())
 
+    mid = x_ref[...].astype(F32) + dot_tn(ctx_ref[...], wo_ref[...])
+    mid_ref[...] = mid
+    moe_in = unit(mid)[0] * moe_gain_ref[...]
+    logits = exact(moe_in, router_ref[...], NT)
+    grown = jnp.exp(logits - jnp.max(logits, axis=1, keepdims=True))
+    probs = grown / jnp.sum(grown, axis=1, keepdims=True)
+    probs_ref[...] = probs
+    gates, _ = gates_of(probs, picks(pairs_ref[...].T))
+    upstream = cot_ref[...].astype(F32)
+    rows = [moe_in.astype(BF16)] + [(g * upstream).astype(BF16) for g in gates]
+    row = lax.broadcasted_iota(jnp.int32, (16 * ROWS, 128), 0).astype(F32)
+    at = [places(pairs_ref[j : j + 1], pairs_ref[2 + j : 3 + j]) for j in range(2)]
+    hot = [((row == at[0]) | (row == at[1]))] + [row == jnp.where(a < 0, a, a + ROWS) for a in at]
+    hot = jnp.concatenate([h.astype(F32) for h in hot], axis=1).astype(BF16)
+    sent = dot(hot, jnp.concatenate(rows, axis=0))
+    send_ref[...] = sent.astype(BF16).reshape(8, 2 * ROWS, 1024)
+
+    for i in range(6):
+        save(i).wait()
+    save_o.wait()
     for d in (1, 2, 3):
         far(0, d)(z_from[d]).wait_recv()
         far(1, d)(y_from[d]).wait_recv()
@@ -339,7 +413,19 @@
             block_out(el).wait_send()
 
 
-def attend(block_input, gain, qkv_low, gate_weight, up_weight, down_weight):
+def attend(
+    block_input,
+    gain,
+    gate_weight,
+    up_weight,
+    down_weight,
+    moe_gain,
+    router,
+    pairs,
+    cotangent,
+    qkv_weight,
+    out_weight,
+):
     dma = pltpu.SemaphoreType.DMA
     vm = pl.BlockSpec(memory_space=VMEM)
     hbm = pl.BlockSpec(memory_space=pl.ANY)
@@ -347,28 +433,37 @@
     return pl.pallas_call(
         attend_kernel,
         out_shape=(
+            shape((8, 2 * ROWS, 1024), BF16),
+            shape((128, 1024), F32),
+            shape((128, 8), F32),
             shape((1024, 128), BF16),
             shape((3, 64, 2048), BF16),
             shape((64, 2048), F32),
             shape((1, 2048), F32),
+            shape((FFQ, DB), BF16),
             shape((4, 4, 128, 1024), BF16),
             shape((2, FFQ, 4 * DB), BF16),
-            shape((FFQ, DB), BF16),
+            shape((1024, 3072), BF16),
+            shape((1024, 1024), BF16),
         ),
-        in_specs=[vm] * 6,
-        out_specs=(vm, vm, vm, vm, hbm, hbm, vm),
+        in_specs=[vm] * 9 + [hbm] * 2,
+        out_specs=(vm,) * 8 + (hbm,) * 4,
         scratch_shapes=[
+            VMEM((1024, 3072), F32),
+            VMEM((1024, 1024), F32),
+            VMEM((1024, 3072), BF16),
+            VMEM((1024, 1024), BF16),
             VMEM((128, 1024), BF16),
             VMEM((3, 16, 64, 128), BF16),
             VMEM((4, 3, FFB, DB), BF16),
             VMEM((3, FFQ, DB), BF16),
             VMEM((2048, 64), BF16),
             VMEM((64, 2048), BF16),
+            dma((11,)),
             dma((4,)),
             dma((4,)),
             dma((4,)),
             dma((4,)),
-            dma((4,)),
             dma((16,)),
             dma((16,)),
             dma((2, 2, 4)),
@@ -376,8 +471,20 @@
             dma((16,)),
             dma((16,)),
         ],
-        compiler_params=params(1, 60),
-    )(block_input, gain.reshape(1, -1), qkv_low, gate_weight, up_weight, down_weight)
+        compiler_params=params(1, 62),
+    )(
+        block_input,
+        gain.reshape(1, -1),
+        jnp.swapaxes(gate_weight, 1, 2),
+        jnp.swapaxes(up_weight, 1, 2),
+        down_weight,
+        moe_gain.reshape(1, -1),
+        router.T,
+        pairs,
+        cotangent,
+        qkv_weight,
+        out_weight,
+    )
 
 
 GELU_A = 0.7978845608
@@ -390,6 +497,7 @@
     down_ref,
     ret_ref,
     grad_ref,
+    first_ref,
     recv,
     own_part,
     sib_send,
@@ -401,9 +509,12 @@
     gcs,
     ucs,
     down,
+    first,
     here,
     x_send,
     x_recv,
+    g_send,
+    g_recv,
     d_send,
     d_recv,
     f_send,
@@ -545,7 +656,18 @@
         fan(d, (x + 4 - d) % 4).wait_recv()
     lax.fori_loop(0, 4, chunk, 0)
     finish(3)
-    for i, (a, b) in enumerate(((gcs, xs), (ucs, xs), (hid, cs))):
+
+    def lead(d):
+        t = (x + d) % 4
+        return push(first.at[t], first_ref.at[d], g_send.at[d], g_recv.at[d], {"dp": t})
+
+    g = dot_tn(gcs[...], xs[...])
+    for at in range(4):
+        first[at] = g[:, at * DB : (at + 1) * DB].astype(BF16)
+    for d in (2, 1, 3):
+        lead(d).start()
+    first_ref[0] = first[x]
+    for i, (a, b) in enumerate(((ucs, xs), (hid, cs))):
         g = dot_tn(a[...], b[...])
         for at in range(4):
             grad_ref[at, i] = g[:, at * DB : (at + 1) * DB].astype(BF16)
@@ -567,6 +689,9 @@
     forward(0).wait_send()
     for d in (1, 2, 3):
         fan(d, x).wait_send()
+        lead(d).wait_recv()
+    for d in (1, 2, 3):
+        lead(d).wait_send()
     for j in range(4):
         partials(j).wait_send()
 
@@ -578,10 +703,11 @@
         moe_kernel,
         out_shape=(
             jax.ShapeDtypeStruct((16, *block), BF16),
-            jax.ShapeDtypeStruct((4, 3, FFQ, DB), BF16),
+            jax.ShapeDtypeStruct((4, 2, FFQ, DB), BF16),
+            jax.ShapeDtypeStruct((4, FFQ, DB), BF16),
         ),
         in_specs=[pl.BlockSpec(memory_space=VMEM)] * 3,
-        out_specs=(pl.BlockSpec(memory_space=VMEM),) * 2,
+        out_specs=(pl.BlockSpec(memory_space=VMEM),) * 3,
         scratch_shapes=[
             VMEM((2, 16, *block), BF16),
             VMEM((4, *block), F32),
@@ -594,9 +720,12 @@
             VMEM((32 * ROWS, FFQ), BF16),
             VMEM((32 * ROWS, FFQ), BF16),
             VMEM((FFQ, 4 * DB), BF16),
+            VMEM((4, FFQ, DB), BF16),
             dma((1,)),
             dma((4,)),
             dma((4,)),
+            dma((4,)),
+            dma((4,)),
             dma((16,)),
             dma((16,)),
             dma((16,)),
@@ -611,24 +740,37 @@
 
 
 def attend_back_kernel(
-    dctx_ref,
+    ret_ref,
+    mid_ref,
+    probs_ref,
+    pairs_ref,
+    cot_ref,
+    moe_gain_ref,
+    router_ref,
+    wo_ref,
+    tok_ref,
     qkv_ref,
     ctx_ref,
     lse_ref,
-    nall_ref,
-    wq_ref,
     x_ref,
     gain_ref,
-    mid_ref,
-    o_ref,
-    few_ref,
+    first_ref,
     g_ref,
+    nall_hbm,
+    wq_hbm,
+    y_ref,
     in_ref,
     gain_out_ref,
     full_ref,
     g_out_ref,
     o_out_ref,
     few_out_ref,
+    dctx_ref,
+    nall_ref,
+    wq_ref,
+    mid_cot,
+    o_ref,
+    few_ref,
     o_sib,
     o_half,
     o_mp,
@@ -636,6 +778,7 @@
     o_dp,
     few_mp,
     few_sum,
+    few_done,
     few_rest,
     cot,
     key_rows,
@@ -716,17 +859,6 @@
         pl.semaphore_signal(barrier, inc=1, device_id=rest(r), device_id_type=MESH)
     pl.semaphore_wait(barrier, 15 + 3 + away + 7)
 
-    def cot_out(k):
-        t = (m + k) % 16
-        return push(dctx_ref.at[t], cot.at[:, lanes(m, 128)], a_send.at[k], a_recv.at[k], {"mp": t})
-
-    def cot_in(k):
-        s = (m + 16 - k) % 16
-        return push(dctx_ref.at[0], cot.at[:, lanes(s, 128)], a_send.at[k], a_recv.at[k], {"mp": s})
-
-    each(1, 16, lambda k: cot_out(k).start())
-    cot[:, lanes(m, 128)] = dctx_ref[m]
-
     def fan(d):
         t = (x + d) % 4
         return push(g_ref.at[t], g_in.at[d], x_send.at[d], x_recv.at[d], {"dp": t})
@@ -735,6 +867,53 @@
         fan(d).start()
     keep = pltpu.make_async_copy(g_ref.at[x], g_in.at[0], here.at[0])
     keep.start()
+    load_n = pltpu.make_async_copy(nall_hbm, nall_ref, here.at[2])
+    load_n.start()
+    load_w = pltpu.make_async_copy(wq_hbm, wq_ref, here.at[3])
+    load_w.start()
+
+    columns = pairs_ref[...].T
+    hot = picks(columns)
+    probs = probs_ref[...]
+    gates, total = gates_of(probs, hot)
+    at = places(columns[:, 0:2], columns[:, 2:4])
+    lane = lax.broadcasted_iota(jnp.int32, (128, 16 * ROWS), 1).astype(F32)
+    at = [at[:, j : j + 1] for j in range(2)]
+    given = (ret_ref[:8].astype(F32) + ret_ref[8:].astype(F32)).astype(BF16)
+    given = given.reshape(16 * ROWS, 1024)
+    fetched = [dot((lane == a).astype(F32).astype(BF16), given) for a in at]
+    low = [lane == jnp.where(a < 0, a, a + ROWS) for a in at]
+    moe_cot = dot((low[0] | low[1]).astype(F32).astype(BF16), given)
+    mid = mid_ref[...]
+    upstream = cot_ref[...].astype(F32)
+    y_ref[...] = (mid + gates[0] * fetched[0] + gates[1] * fetched[1]).astype(BF16)
+    gate_cot = [jnp.sum(upstream * f, axis=1, keepdims=True) for f in fetched]
+    inner = gate_cot[0] * gates[0] + gate_cot[1] * gates[1]
+    probs_cot = sum(h * ((g - inner) / total) for h, g in zip(hot, gate_cot))
+    logit_cot = probs * (probs_cot - jnp.sum(probs * probs_cot, axis=1, keepdims=True))
+    hat, scale = unit(mid)
+    moe_cot += exact(logit_cot, router_ref[...], (((1,), (0,)), ((), ())))
+    few_ref[:8] = exact(logit_cot, hat * moe_gain_ref[...], TN)
+    few_ref[8:] = jnp.concatenate(
+        [jnp.sum(moe_cot * hat, axis=0, keepdims=True), jnp.zeros((7, 1024), F32)], axis=0
+    )
+    gained = moe_cot * moe_gain_ref[...]
+    mid_cot[...] = upstream + scale * (gained - hat * jnp.mean(gained * hat, axis=-1, keepdims=True))
+    branch_cot = mid_cot[...].astype(BF16)
+    dctx_ref[...] = dot_nt(wo_ref[...], branch_cot).astype(BF16).reshape(16, 64, 128)
+
+    def cot_out(k):
+        t = (m + k) % 16
+        return push(dctx_ref.at[t], cot.at[:, lanes(m, 128)], a_send.at[k], a_recv.at[k], {"mp": t})
+
+    def cot_in(k):
+        s = (m + 16 - k) % 16
+        return push(dctx_ref.at[0], cot.at[:, lanes(s, 128)], a_send.at[k], a_recv.at[k], {"mp": s})
+
+    each(1, 16, lambda k: cot_out(k).start())
+    cot[:, lanes(m, 128)] = dctx_ref[m]
+
+    o_ref[...] = dot(tok_ref[...], branch_cot).astype(BF16).reshape(2, 16, 32, 1024)
 
     def halves():
         return push(
@@ -770,12 +949,23 @@
             o_out_ref.at[core], o_out_ref.at[core], o_send.at[1], o_recv.at[1], {"expert": 1 - c}
         )
 
+    def few_share(r):
+        t = 2 * ((x + r % 4) % 4) + (c + r // 4) % 2
+        return push(
+            few_ref.at[:, lanes(t, 128)], few_rest.at[r], fr_send.at[0, r], fr_recv.at[0, r], rest(r)
+        )
+
     def few_near(k):
-        return push(few_ref, few_mp.at[k], fm_send.at[k], fm_recv.at[k], mp_at(m, k))
-
-    def few_far(r):
-        return push(few_sum, few_rest.at[r], fr_send.at[r], fr_recv.at[r], rest(r))
-
+        return push(few_sum, few_mp.at[k], fm_send.at[k], fm_recv.at[k], mp_at(m, k))
+
+    def few_back(r, back):
+        t = 2 * ((x + 4 - r % 4) % 4) + (c + r // 4) % 2 if back else 2 * x + c
+        return push(
+            few_done, few_out_ref.at[:, lanes(t, 128)], fr_send.at[1, r], fr_recv.at[1, r], rest(r)
+        )
+
+    for r in range(1, 8):
+        few_share(r).start()
     halves().start()
     key_rows[...] = qkv_ref[1].astype(F32).T.astype(BF16)
     value_rows[...] = qkv_ref[2].astype(F32).T.astype(BF16)
@@ -803,6 +993,11 @@
     halves().wait_recv()
     o_half[...] = (o_ref[c].astype(F32) + o_sib[...].astype(F32)).astype(BF16)
     each(1, 16, lambda k: thirty(k).start())
+    few_all = few_ref[:, lanes(2 * x + c, 128)]
+    for r in range(1, 8):
+        few_share(r).wait_recv()
+        few_all += few_rest[r]
+    few_sum[...] = few_all
     each(1, 16, lambda k: few_near(k).start())
     lax.fori_loop(1, 4, pair, 0)
     pc_here[1] = dk[...].T.astype(BF16)
@@ -831,13 +1026,15 @@
     for d in (2, 1, 3):
         quarters(d).start()
     each(1, 16, lambda k: few_near(k).wait_recv())
-    few_all = few_ref[...].astype(F32)
+    few_all = few_sum[...]
     for k in range(1, 16):
-        few_all += few_mp[k].astype(F32)
-    few_sum[...] = few_all.astype(BF16)
+        few_all += few_mp[k]
+    few_done[...] = few_all
+    few_out_ref[:, lanes(2 * x + c, 128)] = few_all
     for r in range(1, 8):
-        few_far(r).start()
-
+        few_back(r, False).start()
+
+    load_n.wait()
     slices[...] = dot(pc_here[...].reshape(192, 2048), nall_ref[...]).astype(BF16)
 
     def share_out(r):
@@ -901,12 +1098,11 @@
             spread(p, 0, d, False).start()
 
     each(1, 16, lambda k: pc_in(k).wait_recv())
+    load_w.wait()
     dn = dot(wq_ref[...], pc_tok[...].reshape(3072, 128)).T
-    xf = x_ref[...].astype(F32)
-    scale = lax.rsqrt(jnp.mean(xf * xf, axis=-1, keepdims=True) + EPSILON)
-    hat = xf * scale
+    hat, scale = unit(x_ref[...].astype(F32))
     gained = dn * gain_ref[...]
-    in_ref[...] = mid_ref[...] + scale * (
+    in_ref[...] = mid_cot[...] + scale * (
         gained - hat * jnp.mean(gained * hat, axis=-1, keepdims=True)
     )
     gain_row[...] = jnp.sum(dn * hat, axis=0, keepdims=True)
@@ -921,11 +1117,6 @@
     for d in (1, 2, 3):
         regain(d, (x + 4 - d) % 4).wait_recv()
     each(1, 16, lambda k: regather(k, m).start())
-    for r in range(1, 8):
-        few_far(r).wait_recv()
-        few_all += few_rest[r].astype(F32)
-    few_out_ref[...] = few_all
-
     for p in range(3):
         for d in (1, 2, 3):
             spread(p, 0, d, True).wait_recv()
@@ -951,13 +1142,19 @@
     keep.wait()
     for d in (1, 2, 3):
         fan(d).wait_recv()
-    for i in range(3):
-        g_sum[i] = (
+    for i in range(2):
+        g_sum[i + 1] = (
             g_in[0, i].astype(F32)
             + g_in[1, i].astype(F32)
             + g_in[2, i].astype(F32)
             + g_in[3, i].astype(F32)
         ).astype(BF16)
+    g_sum[0] = (
+        first_ref[0].astype(F32)
+        + first_ref[1].astype(F32)
+        + first_ref[2].astype(F32)
+        + first_ref[3].astype(F32)
+    ).astype(BF16)
 
     def home_out(at):
         return push(
@@ -1010,6 +1207,8 @@
             home_in(at).wait_recv()
 
     retwin(1 - c).wait_recv()
+    for r in range(1, 8):
+        few_back(r, True).wait_recv()
     for p in range(3):
         twin(p, True).wait_recv()
     for p in range(3):
@@ -1026,7 +1225,8 @@
         quarters(d).wait_send()
         regain(d, x).wait_send()
     for r in range(1, 8):
-        few_far(r).wait_send()
+        few_share(r).wait_send()
+        few_back(r, False).wait_send()
     each(1, 16, lambda k: cot_out(k).wait_send())
     each(1, 16, lambda k: pc_out(k).wait_send())
     each(1, 16, lambda k: gain_out(k).wait_send())
@@ -1042,9 +1242,7 @@
             home_out(at).wait_send()
 
 
-def attend_back(
-    dctx, qkv, ctx, lse, nall, qkv_low, block_input, gain, middle_cot, out_term, few, grads
-):
+def attend_back(*operands):
     dma = pltpu.SemaphoreType.DMA
     vm = pl.BlockSpec(memory_space=VMEM)
     hbm = pl.BlockSpec(memory_space=pl.ANY)
@@ -1052,6 +1250,7 @@
     return pl.pallas_call(
         attend_back_kernel,
         out_shape=(
+            shape((128, 1024), BF16),
             shape((128, 1024), F32),
             shape((1, 1024), F32),
             shape((3, 2, 4, 4, 4, 64, 128), BF16),
@@ -1059,17 +1258,24 @@
             shape((2, 16, 32, 1024), BF16),
             shape((16, 1024), F32),
         ),
-        in_specs=[vm] * 11 + [hbm],
-        out_specs=(vm,) * 6,
+        in_specs=[vm] * 15 + [hbm] * 3,
+        out_specs=(vm,) * 7,
         scratch_shapes=[
+            VMEM((16, 64, 128), BF16),
+            VMEM((2048, 1024), BF16),
+            VMEM((1024, 3072), BF16),
+            VMEM((128, 1024), F32),
+            VMEM((2, 16, 32, 1024), BF16),
+            VMEM((16, 1024), F32),
             VMEM((16, 32, 1024), BF16),
             VMEM((16, 32, 1024), BF16),
             VMEM((16, 32, 1024), BF16),
             VMEM((32, 1024), BF16),
             VMEM((4, 32, DB), BF16),
-            VMEM((16, 16, 1024), BF16),
-            VMEM((16, 1024), BF16),
-            VMEM((8, 16, 1024), BF16),
+            VMEM((16, 16, 128), F32),
+            VMEM((16, 128), F32),
+            VMEM((16, 128), F32),
+            VMEM((8, 16, 128), F32),
             VMEM((64, 2048), BF16),
             VMEM((2048, 64), BF16),
             VMEM((2048, 64), BF16),
@@ -1080,12 +1286,12 @@
             VMEM((3, 16, 64, 128), BF16),
             VMEM((192, 1024), BF16),
             VMEM((8, 192, 128), BF16),
-            VMEM((4, 3, FFQ, DB), BF16),
+            VMEM((4, 2, FFQ, DB), BF16),
             VMEM((3, FFQ, DB), BF16),
             VMEM((1, 1024), F32),
             VMEM((16, 1, 1024), F32),
             VMEM((8, 1, 1024), F32),
-            dma((2,)),
+            dma((4,)),
             dma((16,)),
             dma((16,)),
             dma((16,)),
@@ -1114,24 +1320,11 @@
             dma((2, 4)),
             dma((16,)),
             dma((16,)),
-            dma((8,)),
-            dma((8,)),
+            dma((2, 8)),
+            dma((2, 8)),
         ],
-        compiler_params=params(2, 60),
-    )(
-        dctx,
-        qkv,
-        ctx,
-        lse,
-        nall.reshape(2048, 1024),
-        qkv_low,
-        block_input,
-        gain.reshape(1, -1),
-        middle_cot,
-        out_term,
-        few,
-        grads,
-    )
+        compiler_params=params(2, 62),
+    )(*operands)
 
 
 def unfold_kernel(g_ref, o_ref):
@@ -1149,18 +1342,6 @@
         out_specs=pl.BlockSpec((128, 3072), lambda i, j: (2 * i + j, 0)),
         compiler_params=pltpu.CompilerParams(vmem_limit_bytes=32 * 1024 * 1024),
     )(full)
-
-
-def rms_norm(values, gain):
-    return values * lax.rsqrt(jnp.mean(values * values, axis=-1, keepdims=True) + EPSILON) * gain
-
-
-def gating(moe_in, router_weight, routes):
-    logits = jnp.dot(moe_in, router_weight, precision=HIGHEST, preferred_element_type=F32)
-    probs = jax.nn.softmax(logits, axis=-1)
-    onehot = (routes[:, :, None] == jnp.arange(8, dtype=routes.dtype)).astype(F32)
-    chosen = jnp.sum(probs[:, None, :] * onehot, axis=2)
-    return chosen / jnp.sum(chosen, axis=1, keepdims=True)
 
 
 def body(
@@ -1177,57 +1358,41 @@
     slot_index,
     cotangent,
 ):
-    tok_rows, width = block_input.shape
-    inputs = block_input.astype(F32)
-    qkv_low = qkv_weight.astype(BF16)
-    out_low = out_weight.astype(BF16)
-    ctx_tok, qkv, ctx_here, lse, nall, weights, down = attend(
-        block_input, attn_gain, qkv_low, gate_weight, up_weight, down_weight
+    width = block_input.shape[1]
+    pairs = jnp.concatenate([routes.T, slot_index.T, jnp.zeros((4, 128), jnp.int32)]).astype(F32)
+    send, middle, probs, ctx_tok, qkv, ctx_here, lse, down, nall, weights, qkv_low, out_low = attend(
+        block_input,
+        attn_gain,
+        gate_weight,
+        up_weight,
+        down_weight,
+        moe_gain,
+        router_weight,
+        pairs,
+        cotangent,
+        qkv_weight,
+        out_weight,
     )
-    context = ctx_tok.T
-    middle = inputs + dot(context, out_low)
-    moe_in, moe_back = jax.vjp(rms_norm, middle, moe_gain)
-    gates, gate_back = jax.vjp(partial(gating, routes=routes), moe_in, router_weight)
-    valid = slot_index < ROWS
-    place = routes * (2 * ROWS) + slot_index
-    keep = valid.astype(F32)
-    upstream = cotangent.astype(F32)
-    pair_rows = jnp.repeat(moe_in.astype(BF16), 2, axis=0)
-    pair_cots = (gates[:, :, None] * upstream[:, None, :]).astype(BF16).reshape(2 * tok_rows, width)
-    target = jnp.where(valid, place, 16 * ROWS).reshape(-1)
-    cot_target = jnp.where(valid, place + ROWS, 16 * ROWS).reshape(-1)
-    send = jnp.zeros((16 * ROWS, width), BF16)
-    send = send.at[target].set(pair_rows, mode="drop").at[cot_target].set(pair_cots, mode="drop")
-    returned, grads = moe(send.reshape(8, 2 * ROWS, width), weights, down)
-    returned = returned.reshape(2, 8 * 2 * ROWS, width).astype(F32)
-    returned = (returned[0] + returned[1]).astype(BF16)
-    fetch_at = jnp.where(valid, place, 0)
-    fetched = jnp.take(returned, fetch_at, axis=0).astype(F32) * keep[:, :, None]
-    block_output = (middle + jnp.sum(gates[:, :, None] * fetched, axis=1)).astype(BF16)
-    gate_cot = jnp.sum(upstream[:, None, :] * fetched, axis=2)
-    moe_cot = jnp.sum(
-        jnp.take(returned, fetch_at + ROWS, axis=0).astype(F32) * keep[:, :, None], axis=1
-    )
-    router_in_cot, router_term = gate_back(gate_cot)
-    middle_norm_cot, moe_gain_term = moe_back(moe_cot + router_in_cot)
-    middle_cot = upstream + middle_norm_cot
-    branch_cot = middle_cot.astype(BF16)
-    out_term = dot(ctx_tok, branch_cot)
-    context_cot = dot_nt(out_low, branch_cot).astype(BF16).reshape(HEADS, 64, tok_rows)
-    few = jnp.concatenate([router_term.T, moe_gain_term[None], jnp.zeros((7, width), F32)], axis=0)
-    input_grad, gain_grad, full, mine, out_grad, few = attend_back(
-        context_cot,
+    returned, grads, first = moe(send, weights, down)
+    block_output, input_grad, gain_grad, full, mine, out_grad, few = attend_back(
+        returned,
+        middle,
+        probs,
+        pairs,
+        cotangent,
+        moe_gain.reshape(1, -1),
+        router_weight.T,
+        out_low,
+        ctx_tok,
         qkv,
         ctx_here,
         lse,
-        nall,
+        block_input,
+        attn_gain.reshape(1, -1),
+        first,
+        grads,
+        nall.reshape(2048, 1024),
         qkv_low,
-        block_input,
-        attn_gain,
-        middle_cot,
-        out_term.astype(BF16).reshape(2, 16, 32, width),
-        few.astype(BF16),
-        grads,
     )
     mine = mine.astype(F32)
     return (

time: 361 us -> 290 us (0.80)
  other arithmetic: 45.4 us -> 5.55 us
  local copies, waits for them, and re-layouts: 23.6 us -> 6.31 us
  matrix products: 7.56 us -> 0 us
  Pallas kernels: 280 us -> 275 us
    reduce_sum x6 -> x0, other arithmetic: 22.1 us -> none  [the longest x1 22 us: body(): gate_cot = jnp.sum(upstream[:, None, :] * fetched, axis=2)]
    convert_element_type x5 -> x1, other arithmetic: 13 us -> 1.36 us  [body(): jnp.concatenate([routes.T, slot_index.T, jnp.zeros((4, 128), jnp.int32)])]
    dot_general x6 -> x0, matrix products: 7.56 us -> none  [the longest x2 4.84 us: dot(): return jnp.dot(a, b, preferred_element_type=F32)]
    pallas_call x2, Pallas kernels: 188 us -> 183 us  [the longest x1 112 us: attend_back(): pl.pallas_call(attend_back_kernel, out_shape=(shape((128, 1024), BF16), s...]
    unnamed x76 -> x15, local copies, waits for them, and re-layouts: 6.42 us -> 2.11 us
where the time goes in v3:
time: 290 us; the launch traced here: 287 us
  Pallas kernels  275 us (95%)
  local copies, waits for them, and re-layouts  6.31 us (2%)
  other arithmetic  5.55 us (2%)
    pallas_call x1, Pallas kernels, attend_back(): pl.pallas_call(attend_back_kernel, out_shape=(shape((128, 1024), BF16), s...  112 us
    pallas_call x1, Pallas kernels, moe(): pl.pallas_call(moe_kernel, out_shape=(jax.ShapeDtypeStruct((16, *block),...  85.2 us
    pallas_call x1, Pallas kernels, attend(): pl.pallas_call(attend_kernel, out_shape=(shape((8, 2 * ROWS, 1024), BF16)...  71.1 us
    pallas_call x1, Pallas kernels, unfold(): pl.pallas_call(unfold_kernel, out_shape=jax.ShapeDtypeStruct((1024, 3072)...  6.44 us

profile of v3, /device:TPU:1, one launch (start us, length us, event | category | flops | bytes accessed | tf_op | source)
XLA Modules:
  0.0 287.4 jit_solution(9167272875801110890)
XLA Ops:
  0.7 0.1 pad.2.clone
  0.7 1.4 add_convert_fusion.pairs_ref
  2.1 71.1 %shard_map.195 = (bf16[8,80,1024]{2,1,0:T(8,128)(2,1)}, f32[128,1024]{1,0:T(8,128)}, f32[128,8]{1,0:T(8,128)}, bf16[1024,128]{1,0:T(8,128)(2,1)}, bf16[3,64,2048...) custom-call(bf16[128,1024]{1,0:T(8,128)(2,1)} %x_ref.3, ...), custom_call_target="tpu_custom_call" | custom-call | tf_op jit(solution)/shard_map/pallas_call | solution.py:433
  73.2 85.2 %shard_map.196 = (bf16[16,80,1024]{2,1,0:T(8,128)(2,1)}, bf16[4,2,704,256]{3,2,1,0:T(8,128)(2,1)}, bf16[4,704,256]{2,1,0:T(8,128)(2,1)}) custom-call(bf16[8,80,1024]{2,1,0:T(8,128)(2,1)} %get-tuple-element.32.send_ref, bf16[2,704,1024]{2,1,0:T(8,128)(2,1)} %get-tuple-element.33.w_ref, bf16[704,256]{1,0:T(8,128)(2,1)} %get-tuple-element.34.down_ref), custom_call_target="tpu_custom_call" | custom-call | tf_op jit(solution)/shard_map/pallas_call | solution.py:702
  158.4 112.1 %shard_map.197 = (bf16[128,1024]{1,0:T(8,128)(2,1)}, f32[128,1024]{1,0:T(8,128)}, f32[1,1024]{1,0:T(1,128)}, bf16[3,2,4,4,4,64,128]{6,5,4,3,2,1,0:T(8,128)(2,1)}...) custom-call(bf16[16,80,1024]{2,1,0:T(8,128)(2,1)} %get-tuple-element.35.ret_ref, ...), custom_call_target="tpu_custom_call" | custom-call | tf_op jit(solution)/shard_map/pallas_call | solution.py:1250
  270.5 1.4 slice.15
  271.9 1.4 slice_bitcast_fusion.3
  273.3 0.0 copy-start
  273.3 0.0 slice-start
  273.3 1.6 convert_element_type.15
  274.8 0.0 slice-start.1
  274.9 1.4 slice_bitcast_fusion
  276.2 0.0 copy-done
  276.2 2.6 bitcast_convert_fusion
  278.9 0.0 slice-done
  278.9 0.0 slice-done.1
  278.9 0.0 copy-start.2
  278.9 0.0 copy-start.1
  278.9 0.0 copy-start.3
  278.9 6.4 %shard_map.198 = f32[1024,3072]{1,0:T(8,128)} custom-call(bf16[3,2,4,4,4,64,128]{6,5,4,3,2,1,0:T(8,128)(2,1)S(1)} %bitcast.26), custom_call_target="tpu_custom_call" | custom-call | tf_op jit(solution)/shard_map/pallas_call | solution.py:1335
  285.3 0.0 copy-done.2
  285.3 0.7 copy.25
  286.0 0.0 copy-done.1
  286.0 0.8 copy.26
  286.8 0.0 copy-done.3
  286.8 0.6 copy.27
  (2 shorter events, 0.0 us)
Async XLA Ops:
  273.3 3.0 %copy-start = (bf16[2,16,32,1024]{3,2,1,0:T(8,128)(2,1)S(1)}, bf16[2,16,32,1024]{3,2,1,0:T(8,128)(2,1)}, u32[]{:S(2)}) copy-start(bf16[2,16,32,1024]{3,2,1,0:T(8,128)(2,1)} %get-tuple-element.51) | copy-start | bytes 6291460
  273.3 5.6 %slice-start = ((s8[6291456]{0:T(1024)(128)(4,1)}), s8[4194304]{0:T(1024)(128)(4,1)S(1)}, s32[]{:S(2)}) async-start(s8[6291456]{0:T(1024)(128)(4,1)} %bitcast.25), calls=%async_computation | async-start | bytes 8388608
  274.8 4.0 %slice-start.1 = ((s8[6291456]{0:T(1024)(128)(4,1)}), s8[2097152]{0:T(1024)(128)(4,1)S(1)}, s32[]{:S(2)}) async-start(s8[6291456]{0:T(1024)(128)(4,1)} %bitcast.25), calls=%async_computation.1 | async-start | bytes 4194304
  278.9 6.5 %copy-start.2 = (bf16[128,1024]{1,0:T(8,128)(2,1)S(1)}, bf16[128,1024]{1,0:T(8,128)(2,1)}, u32[]{:S(2)}) copy-start(bf16[128,1024]{1,0:T(8,128)(2,1)} %get-tuple-element.67) | copy-start | bytes 786436
  278.9 7.2 %copy-start.1 = (f32[128,1024]{1,0:T(8,128)S(1)}, f32[128,1024]{1,0:T(8,128)}, u32[]{:S(2)}) copy-start(f32[128,1024]{1,0:T(8,128)} %get-tuple-element.68) | copy-start | bytes 1572868
  278.9 8.0 %copy-start.3 = (f32[1,1024]{1,0:T(1,128)S(1)}, f32[1,1024]{1,0:T(1,128)}, u32[]{:S(2)}) copy-start(f32[1,1024]{1,0:T(1,128)} %get-tuple-element.49) | copy-start | bytes 12292

commit v4 on v3

v4 whole, which is shorter than its diff:
```python
import jax
import jax.numpy as jnp
from jax import lax
from jax.experimental import pallas as pl
from jax.experimental.pallas import tpu as pltpu
from jax.sharding import PartitionSpec as P

EPSILON = 1e-06
HIGHEST = lax.Precision.HIGHEST
MESH = pl.DeviceIdType.MESH
F32 = jnp.float32
BF16 = jnp.bfloat16
VMEM = pltpu.VMEM
ROWS = 40
FFB = 176
FFQ = 704
DB = 256
NT = (((1,), (1,)), ((), ()))
TN = (((0,), (0,)), ((), ()))


def dot(a, b):
    return jnp.dot(a, b, preferred_element_type=F32)


def dot_nt(a, b):
    return lax.dot_general(a, b, NT, preferred_element_type=F32)


def dot_tn(a, b):
    return lax.dot_general(a, b, TN, preferred_element_type=F32)


def spot():
    m = lax.axis_index("mp")
    return lax.axis_index("dp"), lax.axis_index("expert"), m, m // 4, m % 4


def params(cid, mb=60):
    return pltpu.CompilerParams(
        collective_id=cid, has_side_effects=True, vmem_limit_bytes=mb * 1024 * 1024
    )


def swapped(c, z):
    return z % 2, 2 * (z // 2) + c


def mp_at(m, k):
    return {"mp": (m + k) % 16}


def y_at(z, y, d):
    return {"mp": z * 4 + (y + d) % 4}


def z_at(z, y, d):
    return {"mp": ((z + d) % 4) * 4 + y}


def push(src, dst, send, recv, device):
    return pltpu.make_async_remote_copy(
        src_ref=src, dst_ref=dst, send_sem=send, recv_sem=recv, device_id=device, device_id_type=MESH
    )


def lanes(at, size):
    return pl.ds(pl.multiple_of(at * size, size), size)


def greet_mp(barrier, m):
    def one(k, carry):
        pl.semaphore_signal(barrier, inc=1, device_id=mp_at(m, k), device_id_type=MESH)
        return carry

    lax.fori_loop(1, 16, one, 0)


def places(routes, slots):
    return jnp.where(slots < ROWS, routes * (2 * ROWS) + slots, -1.0)


def picks(columns):
    lane = lax.broadcasted_iota(jnp.int32, (128, 8), 1).astype(F32)
    return [(columns[:, j : j + 1] == lane).astype(F32) for j in range(2)]


def gates_of(probs, hot):
    chosen = [jnp.sum(probs * h, axis=1, keepdims=True) for h in hot]
    total = chosen[0] + chosen[1]
    return [v / total for v in chosen], total


def exact(a, b, dims):
    return lax.dot_general(a, b, dims, precision=HIGHEST, preferred_element_type=F32)


def unit(v):
    scale = lax.rsqrt(jnp.mean(v * v, axis=-1, keepdims=True) + EPSILON)
    return v * scale, scale


def attend_kernel(
    x_ref,
    gain_ref,
    gate_ref,
    up_ref,
    downs_ref,
    moe_gain_ref,
    router_ref,
    pairs_ref,
    cot_ref,
    wq_hbm,
    wo_hbm,
    send_ref,
    mid_ref,
    probs_ref,
    ctx_ref,
    qkv_ref,
    ctx_here_ref,
    lse_ref,
    down_ref,
    nall_ref,
    w_out_ref,
    wq_out_ref,
    wo_out_ref,
    wq_wide,
    wo_wide,
    wq_ref,
    wo_ref,
    normed,
    heads,
    blocks,
    stage,
    key_rows,
    ctx_low,
    here,
    s_send,
    s_recv,
    x_send,
    x_recv,
    a_send,
    a_recv,
    n_send,
    n_recv,
    c_send,
    c_recv,
):
    x, c, m, z, y = spot()
    pc, pz = swapped(c, z)
    away = (pc - c) * (pc - c)
    barrier = pltpu.get_barrier_semaphore()

    def remote(el):
        return (away == 1) | (el != y)

    def partner(el):
        return {"expert": pc, "mp": pz * 4 + el}

    greet_mp(barrier, m)
    for el in range(4):

        @pl.when(remote(el))
        def _():
            pl.semaphore_signal(barrier, inc=1, device_id=partner(el), device_id_type=MESH)

    for d in range(1, 4):
        pl.semaphore_signal(barrier, inc=1, device_id={"dp": (x + d) % 4}, device_id_type=MESH)

    wide = 512

    def load(i):
        cols = pl.ds(i * wide, wide)
        return pltpu.make_async_copy(wq_hbm.at[:, cols], wq_wide.at[:, cols], here.at[4 + i])

    def save(i):
        cols = pl.ds(i * wide, wide)
        return pltpu.make_async_copy(wq_ref.at[:, cols], wq_out_ref.at[:, cols], here.at[4 + i])

    load_o = pltpu.make_async_copy(wo_hbm, wo_wide, here.at[10])
    save_o = pltpu.make_async_copy(wo_ref, wo_out_ref, here.at[10])
    for i in range(6):
        load(i).start()
    load_o.start()
    for el in range(4):
        blocks[el, 0] = gate_ref[el].astype(BF16)
        blocks[el, 1] = up_ref[el].astype(BF16)
        blocks[el, 2] = downs_ref[el].astype(BF16)
    pl.semaphore_wait(barrier, 15 + 6 + away)

    def units(at):
        return stage.at[:, pl.ds(pl.multiple_of(at * FFB, 16), FFB), :]

    def block(i, el, at):
        return push(
            blocks.at[el, i],
            stage.at[i, pl.ds(pl.multiple_of(at * FFB, 16), FFB), :],
            s_send.at[i, el],
            s_recv.at[i, at],
            partner(el),
        )

    def each_block(f):
        for el in range(4):

            @pl.when(remote(el))
            def _(el=el):
                f(el)

    def blocks_out(i):
        each_block(lambda el: block(i, el, y).start())

    def blocks_in(i):
        each_block(lambda el: block(i, el, el).wait_recv())

    blocks_out(0)

    @pl.when(away == 0)
    def _():
        kept = pltpu.make_async_copy(blocks.at[y], units(y), here.at[2])
        kept.start()
        kept.wait()

    normed[...] = (unit(x_ref[...].astype(F32))[0] * gain_ref[...]).astype(BF16)
    half = 512

    def near(part, d):
        cols = pl.ds(part * half, half)
        device = y_at(z, y, d) if part == 0 else z_at(z, y, d)
        return lambda at: push(
            normed.at[:, cols],
            nall_ref.at[at // 4, at % 4, :, cols],
            n_send.at[part, 0, d],
            n_recv.at[part, 0, d],
            device,
        )

    y_from = [z * 4 + (y + 4 - d) % 4 for d in range(4)]
    z_from = [((z + 4 - d) % 4) * 4 + y for d in range(4)]

    for i in range(6):
        load(i).wait()
        cols = slice(i * wide, (i + 1) * wide)
        wq_ref[:, cols] = wq_wide[:, cols].astype(BF16)
        save(i).start()
        part = dot(normed[...], wq_ref[:, cols])
        heads[i // 2, (i % 2) * 8 : (i % 2) * 8 + 8] = part.T.astype(BF16).reshape(8, 64, 128)

    def head_out(k):
        t = (m + k) % 16
        return push(
            heads.at[:, t],
            qkv_ref.at[:, :, lanes(m, 128)],
            a_send.at[k],
            a_recv.at[k],
            mp_at(m, k),
        )

    def head_in(k):
        return push(
            heads.at[:, 0],
            qkv_ref.at[:, :, lanes((m + 16 - k) % 16, 128)],
            a_send.at[k],
            a_recv.at[k],
            mp_at(m, k),
        )

    def each(lo, hi, f):
        def one(k, carry):
            f(k)
            return carry

        lax.fori_loop(lo, hi, one, 0)

    each(1, 16, lambda k: head_out(k).start())
    own = pltpu.make_async_copy(heads.at[:, m], qkv_ref.at[:, :, lanes(m, 128)], here.at[0])
    own.start()
    mine = pltpu.make_async_copy(normed, nall_ref.at[z, y], here.at[1])
    mine.start()


    def fan(i, d, step, at):
        rows = pl.ds(0, FFQ) if step == 0 else pl.ds(0 if d == 1 else FFQ // 2, FFQ // 2)
        cols = w_out_ref.at[i, rows, lanes(at, DB)]
        return push(
            stage.at[i] if step == 0 else cols,
            cols,
            x_send.at[i, step, d],
            x_recv.at[i, step, d],
            {"dp": (x + d) % 4},
        )

    def fan_wait(i, step):
        for d in (1, 3):
            fan(i, d, step, (x + 8 - d * (1 + step)) % 4).wait_recv()

    def fan_start(i, step):
        for d in (1, 3):
            fan(i, d, step, x if step == 0 else (x + 4 - d) % 4).start()

    def fan_own(i):
        return pltpu.make_async_copy(stage.at[i], w_out_ref.at[i, :, lanes(x, DB)], here.at[2 + i])

    blocks_in(0)
    fan_start(0, 0)
    fan_own(0).start()
    load_o.wait()
    wo_ref[...] = wo_wide[...].astype(BF16)
    save_o.start()

    own.wait()
    each(1, 16, lambda k: head_in(k).wait_recv())
    blocks_out(1)
    blocks_out(2)
    for d in (2, 1, 3):
        near(0, d)(m).start()
        near(1, d)(m).start()

    key_rows[...] = qkv_ref[1].astype(F32).T.astype(BF16)

    def ctx_out(t):
        return push(
            ctx_low.at[:, lanes(t, 128)],
            ctx_ref.at[pl.ds(pl.multiple_of(m * 64, 64), 64), :],
            c_send.at[(t + 16 - m) % 16],
            c_recv.at[(t + 16 - m) % 16],
            {"mp": t},
        )

    def ctx_in(k):
        s = (m + 16 - k) % 16
        return push(
            ctx_low.at[:, pl.ds(0, 128)],
            ctx_ref.at[pl.ds(pl.multiple_of(s * 64, 64), 64), :],
            c_send.at[k],
            c_recv.at[k],
            {"mp": s},
        )

    def queries(i):
        b = (m // 2 + i) % 8
        cols = lanes(b, 256)
        q = (qkv_ref[0, :, cols].astype(F32) * 0.125).astype(BF16)
        s = dot(key_rows[...], q)
        top = jnp.max(s, axis=0, keepdims=True)
        p = jnp.exp(s - top)
        total = jnp.sum(p, axis=0, keepdims=True)
        ctx = dot(qkv_ref[2], p.astype(BF16)) / total
        lse_ref[:, cols] = top + jnp.log(total)
        ctx_here_ref[:, cols] = ctx
        ctx_low[:, cols] = ctx.astype(BF16)

    def pair(i, carry):
        queries(2 * i)
        queries(2 * i + 1)
        for u in range(2):
            b = (m // 2 + 2 * i + u) % 8
            for v in range(2):
                t = 2 * b + v

                @pl.when(t != m)
                def _():
                    ctx_out(t).start()

        @pl.when(i == 0)
        def _():
            blocks_in(1)
            fan_start(1, 0)
            fan_own(1).start()

        @pl.when(i == 1)
        def _():
            fan_wait(0, 0)
            fan_start(0, 1)
            blocks_in(2)

        return carry

    lax.fori_loop(0, 4, pair, 0)
    ctx_ref[pl.ds(pl.multiple_of(m * 64, 64), 64), :] = ctx_low[:, lanes(m, 128)]
    each(1, 16, lambda k: ctx_in(k).wait_recv())

    fan_wait(1, 0)
    fan_start(1, 1)
    down_ref[...] = stage[2]

    mid = x_ref[...].astype(F32) + dot_tn(ctx_ref[...], wo_ref[...])
    mid_ref[...] = mid
    moe_in = unit(mid)[0] * moe_gain_ref[...]
    logits = exact(moe_in, router_ref[...], NT)
    grown = jnp.exp(logits - jnp.max(logits, axis=1, keepdims=True))
    probs = grown / jnp.sum(grown, axis=1, keepdims=True)
    probs_ref[...] = probs
    gates, _ = gates_of(probs, picks(pairs_ref[...].T))
    upstream = cot_ref[...].astype(F32)
    rows = [moe_in.astype(BF16)] + [(g * upstream).astype(BF16) for g in gates]
    row = lax.broadcasted_iota(jnp.int32, (16 * ROWS, 128), 0).astype(F32)
    at = [places(pairs_ref[j : j + 1], pairs_ref[2 + j : 3 + j]) for j in range(2)]
    hot = [((row == at[0]) | (row == at[1]))] + [row == jnp.where(a < 0, a, a + ROWS) for a in at]
    hot = jnp.concatenate([h.astype(F32) for h in hot], axis=1).astype(BF16)
    sent = dot(hot, jnp.concatenate(rows, axis=0))
    send_ref[...] = sent.astype(BF16).reshape(8, 2 * ROWS, 1024)

    for i in range(6):
        save(i).wait()
    save_o.wait()
    fan_wait(0, 1)
    fan_wait(1, 1)
    for d in (1, 2, 3):
        near(0, d)(y_from[d]).wait_recv()
        near(1, d)(z_from[d]).wait_recv()
    for d in (1, 2, 3):
        near(0, d)(m).wait_send()
        near(1, d)(m).wait_send()
    mine.wait()
    for i in range(2):
        fan_own(i).wait()
        for d in (1, 3):
            for step in range(2):
                fan(i, d, step, x).wait_send()
    each(1, 16, lambda k: head_out(k).wait_send())
    each(1, 16, lambda k: ctx_in(k).wait_send())
    for i in range(3):
        each_block(lambda el, i=i: block(i, el, y).wait_send())


def attend(
    block_input,
    gain,
    gate_weight,
    up_weight,
    down_weight,
    moe_gain,
    router,
    pairs,
    cotangent,
    qkv_weight,
    out_weight,
):
    dma = pltpu.SemaphoreType.DMA
    vm = pl.BlockSpec(memory_space=VMEM)
    hbm = pl.BlockSpec(memory_space=pl.ANY)
    shape = jax.ShapeDtypeStruct
    return pl.pallas_call(
        attend_kernel,
        out_shape=(
            shape((8, 2 * ROWS, 1024), BF16),
            shape((128, 1024), F32),
            shape((128, 8), F32),
            shape((1024, 128), BF16),
            shape((3, 64, 2048), BF16),
            shape((64, 2048), F32),
            shape((1, 2048), F32),
            shape((FFQ, DB), BF16),
            shape((4, 4, 128, 1024), BF16),
            shape((2, FFQ, 4 * DB), BF16),
            shape((1024, 3072), BF16),
            shape((1024, 1024), BF16),
        ),
        in_specs=[vm] * 9 + [hbm] * 2,
        out_specs=(vm,) * 8 + (hbm,) * 4,
        scratch_shapes=[
            VMEM((1024, 3072), F32),
            VMEM((1024, 1024), F32),
            VMEM((1024, 3072), BF16),
            VMEM((1024, 1024), BF16),
            VMEM((128, 1024), BF16),
            VMEM((3, 16, 64, 128), BF16),
            VMEM((4, 3, FFB, DB), BF16),
            VMEM((3, FFQ, DB), BF16),
            VMEM((2048, 64), BF16),
            VMEM((64, 2048), BF16),
            dma((11,)),
            dma((3, 4)),
            dma((3, 4)),
            dma((2, 2, 4)),
            dma((2, 2, 4)),
            dma((16,)),
            dma((16,)),
            dma((2, 1, 4)),
            dma((2, 1, 4)),
            dma((16,)),
            dma((16,)),
        ],
        compiler_params=params(1, 62),
    )(
        block_input,
        gain.reshape(1, -1),
        jnp.swapaxes(gate_weight, 1, 2),
        jnp.swapaxes(up_weight, 1, 2),
        down_weight,
        moe_gain.reshape(1, -1),
        router.T,
        pairs,
        cotangent,
        qkv_weight,
        out_weight,
    )


GELU_A = 0.7978845608
GELU_B = 0.044715


def experts_back_kernel(
    mid_ref,
    probs_ref,
    pairs_ref,
    cot_ref,
    moe_gain_ref,
    router_ref,
    tok_ref,
    qkv_ref,
    ctx_ref,
    lse_ref,
    x_ref,
    gain_ref,
    down_ref,
    send_hbm,
    w_hbm,
    near_hbm,
    wq_hbm,
    wo_hbm,
    y_ref,
    in_ref,
    gain_out_ref,
    g_out_ref,
    few_out_ref,
    full_ref,
    ret_ref,
    nall_ref,
    weights,
    recv,
    rows,
    back,
    sib_recv,
    sib_send,
    own_part,
    hid,
    gcs,
    ucs,
    g_relay,
    g_near,
    dctx,
    mid_cot,
    few,
    o_sib,
    o_x,
    o_q,
    o_mp,
    o_fin,
    few_mp,
    few_sum,
    few_done,
    few_rest,
    cot,
    key_rows,
    value_rows,
    row_dot,
    dk,
    dv,
    pc_here,
    pc_tok,
    slices,
    own_share,
    parts,
    gain_row,
    gain_mp,
    gain_rest,
    here,
    d_send,
    d_recv,
    f_send,
    f_recv,
    p_send,
    p_recv,
    r_send,
    r_recv,
    w_send,
    w_recv,
    x_send,
    x_recv,
    s_send,
    s_recv,
    n_send,
    n_recv,
    a_send,
    a_recv,
    b_send,
    b_recv,
    q_send,
    q_recv,
    g_send,
    g_recv,
    t_send,
    t_recv,
    u_send,
    u_recv,
    v_send,
    v_recv,
    o_send,
    o_recv,
    ox_send,
    ox_recv,
    om_send,
    om_recv,
    fm_send,
    fm_recv,
    fr_send,
    fr_recv,
):
    x, c, m, z, y = spot()
    pc, pz = swapped(c, z)
    away = (pc - c) * (pc - c)
    barrier = pltpu.get_barrier_semaphore()

    def remote(el):
        return (away == 1) | (el != y)

    def partner(el):
        return {"expert": pc, "mp": pz * 4 + el}

    def rest(r):
        return {"dp": (x + r % 4) % 4, "expert": (c + r // 4) % 2}

    def each(lo, hi, f):
        def one(k, carry):
            f(k)
            return carry

        lax.fori_loop(lo, hi, one, 0)

    def local(src, dst, i):
        return pltpu.make_async_copy(src, dst, here.at[i])

    twin = {"expert": 1 - c}
    size = 2 * ROWS

    greet_mp(barrier, m)
    for el in range(4):

        @pl.when(remote(el))
        def _():
            pl.semaphore_signal(barrier, inc=1, device_id=partner(el), device_id_type=MESH)

    for r in range(1, 8):
        pl.semaphore_signal(barrier, inc=1, device_id=rest(r), device_id_type=MESH)
    load_w = [local(w_hbm.at[i], weights.at[pl.ds(i * FFQ, FFQ)], i) for i in range(2)]
    for copy in load_w:
        copy.start()
    near = [
        local(near_hbm.at[z, :, :, pl.ds(0, 512)], nall_ref.at[z, :, :, pl.ds(0, 512)], 2),
        local(near_hbm.at[:, y, :, pl.ds(512, 512)], nall_ref.at[:, y, :, pl.ds(512, 512)], 3),
    ]
    for copy in near:
        copy.start()
    pl.semaphore_wait(barrier, 15 + 3 + away + 7)

    def expert_of(t):
        return ((t // 4) % 2) * 4 + t % 4

    def slot(core, k, n=1):
        return pl.ds(pl.multiple_of((core * 16 + k) * size, size), n * size)

    def dispatch(k):
        t = (m + k) % 16
        return push(
            send_hbm.at[expert_of(t)],
            recv.at[slot(0, k)],
            d_send.at[k],
            d_recv.at[k],
            {"mp": t},
        )

    def forward(k):
        return push(recv.at[slot(0, k)], recv.at[slot(1, k)], f_send.at[k], f_recv.at[k], twin)

    def partials(j):
        return push(
            sib_send.at[j % 2],
            sib_recv.at[pl.ds(pl.multiple_of(j * 4 * size, size), 4 * size)],
            p_send.at[j],
            p_recv.at[j],
            twin,
        )

    def spot_of(k, n=1):
        return pl.ds(pl.multiple_of(k * size, size), n * size)

    def giving(k, at):
        return push(
            back.at[spot_of(k)], ret_ref.at[at], r_send.at[k], r_recv.at[k], mp_at(m, 16 - k)
        )

    def down_fan(d, at):
        return push(
            down_ref,
            weights.at[pl.ds(2 * FFQ, FFQ), lanes(at, DB)],
            w_send.at[d],
            w_recv.at[d],
            {"dp": (x + d) % 4},
        )

    each(1, 16, lambda k: dispatch(k).start())
    own = local(send_hbm.at[expert_of(m)], recv.at[slot(0, 0)], 4)
    own.start()
    for d in (2, 1, 3):
        down_fan(d, x).start()
    weights[2 * FFQ :, lanes(x, DB)] = down_ref[...]
    own.wait()

    def finish(j):
        partials(j).wait_recv()
        span = spot_of(4 * j, 4)
        back[span] = (own_part[...] + sib_recv[span].astype(F32)).astype(BF16)
        for i in range(4):
            k = 4 * j + i

            @pl.when(k > 0)
            def _():
                giving(k, m).start()

            @pl.when(k == 0)
            def _():
                local(back.at[spot_of(0)], ret_ref.at[m], 4).start()

    gate_w, up_w, down_w = (slice(i * FFQ, (i + 1) * FFQ) for i in range(3))
    cot_rows = 32 * ROWS

    def chunk(j, carry):
        for i in range(4):
            k = 4 * j + i

            @pl.when(k > 0)
            def _():
                dispatch(k).wait_recv()

            forward(k).start()

        @pl.when(j > 0)
        def _():
            finish(j - 1)

        @pl.when(j == 0)
        def _():
            for copy in load_w:
                copy.wait()
            for d in (1, 2, 3):
                down_fan(d, (x + 4 - d) % 4).wait_recv()

        for i in range(4):
            forward(4 * j + i).wait_recv()
        xs = pl.ds(pl.multiple_of(j * 8 * ROWS, 16), 8 * ROWS)
        cs = pl.ds(pl.multiple_of(cot_rows + j * 8 * ROWS, 16), 8 * ROWS)
        for r in range(2):
            blk = recv[slot(r, 4 * j, 4)].astype(F32).reshape(4, size, 4 * DB)
            for at, part in ((0, blk[:, :ROWS]), (cot_rows, blk[:, ROWS:])):
                span = pl.ds(pl.multiple_of(at + (2 * j + r) * 4 * ROWS, 16), 4 * ROWS)
                rows[span] = part.reshape(4 * ROWS, 4 * DB).astype(BF16)
        gate = dot_nt(rows[xs], weights[gate_w])
        up = dot_nt(rows[xs], weights[up_w])
        hid_cot = dot_nt(rows[cs], weights[down_w])
        sq = gate * gate
        th = jnp.tanh(GELU_A * (gate + GELU_B * (gate * sq)))
        half = 0.5 * (1.0 + th)
        act = gate * half
        slope = half + 0.5 * gate * (1.0 - th * th) * (GELU_A * (1.0 + 3.0 * GELU_B * sq))
        hid[xs] = (act * up).astype(BF16)
        gcs[xs] = (hid_cot * up * slope).astype(BF16)
        ucs[xs] = (hid_cot * act).astype(BF16)
        out = dot(hid[xs], weights[down_w]).reshape(2, 4, ROWS, 4 * DB)
        low = dot(gcs[xs], weights[gate_w]) + dot(ucs[xs], weights[up_w])
        low = low.reshape(2, 4, ROWS, 4 * DB)
        own_part[...] = jnp.concatenate([out[0], low[0]], axis=1).reshape(4 * size, 4 * DB)

        @pl.when(j > 1)
        def _():
            partials(j - 2).wait_send()

        sib_send[j % 2] = (
            jnp.concatenate([out[1], low[1]], axis=1).reshape(4 * size, 4 * DB).astype(BF16)
        )
        partials(j).start()
        return carry

    lax.fori_loop(0, 4, chunk, 0)
    finish(3)
    each(0, 16, lambda k: forward(k).wait_send())
    load_o = local(wo_hbm, weights.at[pl.ds(0, 1024)], 0)
    load_o.start()

    unit_half = FFQ // 2

    def unit_rows(i, d):
        return pl.ds(i * FFQ + (0 if d == 1 else unit_half), unit_half)

    def relay(i, d):
        return push(
            recv.at[unit_rows(i, d), lanes((x + 2) % 4, DB)],
            g_relay.at[d // 2, i],
            x_send.at[0, i, d],
            x_recv.at[0, i, d],
            {"dp": (x + d) % 4},
        )

    def settle(i, d):
        return push(
            recv.at[pl.ds(i * FFQ, FFQ), lanes((x + d) % 4, DB)],
            g_near.at[d // 2, i],
            x_send.at[1, i, d],
            x_recv.at[1, i, d],
            {"dp": (x + d) % 4},
        )

    for i, (a, at) in enumerate(((gcs, 0), (ucs, 0), (hid, cot_rows))):
        g = dot_tn(a[...], rows[at : at + cot_rows])
        recv[i * FFQ : (i + 1) * FFQ] = g.astype(BF16)
        for d in (1, 3):
            relay(i, d).start()
    load_q = [
        local(wq_hbm.at[:, pl.ds(i * 1024, 1024)], rows.at[pl.ds(i * 1024, 1024)], 5 + i)
        for i in range(3)
    ]
    for copy in load_q:
        copy.start()
    for i in range(3):
        for d in (1, 3):
            relay(i, d).wait_recv()
            span, cols = unit_rows(i, d), lanes((x + d) % 4, DB)
            recv[span, cols] = (
                recv[span, cols].astype(F32) + g_relay[d // 2, i].astype(F32)
            ).astype(BF16)
            settle(i, d).start()

    def home(i, at, to):
        return push(
            recv.at[pl.ds(i * FFQ + at * FFB, FFB), lanes(x, DB)],
            g_out_ref.at[to, i],
            s_send.at[i, at],
            s_recv.at[i, to],
            partner(at),
        )

    def each_home(f):
        for at in range(4):

            @pl.when(remote(at))
            def _(at=at):
                f(at)

    def go_home(i):
        for d in (1, 3):
            settle(i, d).wait_recv()
        span, cols = pl.ds(i * FFQ, FFQ), lanes(x, DB)
        recv[span, cols] = (
            recv[span, cols].astype(F32) + g_near[0, i].astype(F32) + g_near[1, i].astype(F32)
        ).astype(BF16)
        each_home(lambda at: home(i, at, y).start())

        @pl.when(away == 0)
        def _():
            kept = local(
                recv.at[pl.ds(pl.multiple_of(i * FFQ + y * FFB, 16), FFB), cols], g_out_ref.at[y, i], 1
            )
            kept.start()
            kept.wait()

    local(back.at[spot_of(0)], ret_ref.at[m], 4).wait()
    each(1, 16, lambda k: giving(k, (m + k) % 16).wait())
    load_r = local(ret_ref, back.reshape(16, size, 4 * DB), 4)
    load_r.start()
    load_r.wait()

    for copy in near:
        copy.wait()
    y_from = [z * 4 + (y + 4 - d) % 4 for d in range(4)]
    z_from = [((z + 4 - d) % 4) * 4 + y for d in range(4)]

    def far(part, d, step, origin):
        cols = pl.ds(part * 512, 512)
        some = pl.ds(0, 4) if step == 0 else pl.ds(0 if d == 1 else 2, 2)
        if part == 0:
            ref, device = nall_ref.at[origin // 4, some, :, cols], z_at(z, y, d)
        else:
            ref, device = nall_ref.at[some, origin % 4, :, cols], y_at(z, y, d)
        return push(ref, ref, n_send.at[part, step, d], n_recv.at[part, step, d], device)

    def far_wait(step):
        for part, origins in enumerate((z_from, y_from)):
            for d in (1, 3):
                far(part, d, step, origins[(d * (1 + step)) % 4]).wait_recv()

    def far_start(step):
        for part, origins in enumerate((z_from, y_from)):
            for d in (1, 3):
                far(part, d, step, origins[d * step]).start()

    columns = pairs_ref[...].T
    hot = picks(columns)
    probs = probs_ref[...]
    gates, total = gates_of(probs, hot)
    at = places(columns[:, 0:2], columns[:, 2:4])
    lane = lax.broadcasted_iota(jnp.int32, (128, 16 * ROWS), 1).astype(F32)
    at = [at[:, j : j + 1] for j in range(2)]
    given = (back[: 8 * size].astype(F32) + back[8 * size :].astype(F32)).astype(BF16)
    fetched = [dot((lane == a).astype(F32).astype(BF16), given) for a in at]
    low = [lane == jnp.where(a < 0, a, a + ROWS) for a in at]
    moe_cot = dot((low[0] | low[1]).astype(F32).astype(BF16), given)
    mid = mid_ref[...]
    upstream = cot_ref[...].astype(F32)
    y_ref[...] = (mid + gates[0] * fetched[0] + gates[1] * fetched[1]).astype(BF16)
    gate_cot = [jnp.sum(upstream * f, axis=1, keepdims=True) for f in fetched]
    inner = gate_cot[0] * gates[0] + gate_cot[1] * gates[1]
    probs_cot = sum(h * ((g - inner) / total) for h, g in zip(hot, gate_cot))
    logit_cot = probs * (probs_cot - jnp.sum(probs * probs_cot, axis=1, keepdims=True))
    hat, scale = unit(mid)
    moe_cot += exact(logit_cot, router_ref[...], (((1,), (0,)), ((), ())))
    few[:8] = exact(logit_cot, hat * moe_gain_ref[...], TN)
    few[8:] = jnp.concatenate(
        [jnp.sum(moe_cot * hat, axis=0, keepdims=True), jnp.zeros((7, 1024), F32)], axis=0
    )
    gained = moe_cot * moe_gain_ref[...]
    mid_cot[...] = upstream + scale * (gained - hat * jnp.mean(gained * hat, axis=-1, keepdims=True))
    branch_cot = mid_cot[...].astype(BF16)
    load_o.wait()
    dctx[...] = dot_nt(weights[:1024], branch_cot).astype(BF16).reshape(16, 64, 128)

    def cot_out(k):
        t = (m + k) % 16
        return push(dctx.at[t], cot.at[:, lanes(m, 128)], a_send.at[k], a_recv.at[k], {"mp": t})

    def cot_in(k):
        s = (m + 16 - k) % 16
        return push(dctx.at[0], cot.at[:, lanes(s, 128)], a_send.at[k], a_recv.at[k], {"mp": s})

    each(1, 16, lambda k: cot_out(k).start())
    far_start(0)
    cot[:, lanes(m, 128)] = dctx[m]

    weights[1024:2048] = dot(tok_ref[...], branch_cot).astype(BF16)

    def halves():
        rows_at = pl.ds(pl.multiple_of(1024 + (1 - c) * 512, 512), 512)
        return push(weights.at[rows_at], o_sib, o_send.at[0], o_recv.at[0], twin)

    def quarters(d):
        t = (x + d) % 4
        return push(
            weights.at[pl.ds(0, 512), lanes(t, DB)], o_x.at[d], ox_send.at[d], ox_recv.at[d], {"dp": t}
        )

    def thirty(k):
        t = (m + k) % 16
        return push(
            o_q.at[pl.ds(pl.multiple_of(t * 32, 32), 32)],
            o_mp.at[k],
            om_send.at[k],
            om_recv.at[k],
            {"mp": t},
        )

    def few_share(r):
        t = 2 * ((x + r % 4) % 4) + (c + r // 4) % 2
        return push(
            few.at[:, lanes(t, 128)], few_rest.at[r], fr_send.at[0, r], fr_recv.at[0, r], rest(r)
        )

    def few_near(k):
        return push(few_sum, few_mp.at[k], fm_send.at[k], fm_recv.at[k], mp_at(m, k))

    def few_back(r, back_from):
        t = 2 * ((x + 4 - r % 4) % 4) + (c + r // 4) % 2 if back_from else 2 * x + c
        return push(
            few_done, few_out_ref.at[:, lanes(t, 128)], fr_send.at[1, r], fr_recv.at[1, r], rest(r)
        )

    halves().start()
    for r in range(1, 8):
        few_share(r).start()

    def along(axis, d):
        if axis == 0:
            return {"dp": (x + d) % 4}
        return z_at(z, y, d) if axis == 1 else y_at(z, y, d)

    orders = ((0, 2, 1), (2, 1, 0), (1, 0, 2), (1, 2, 0))

    def spread(p, s, d, incoming):
        at = [x, z, y]
        axis = orders[p][s]
        if incoming:
            at[axis] = (at[axis] + 4 - d) % 4
        src = [x, z, y]
        for done in orders[p][:s]:
            at[done] = slice(None)
            src[done] = slice(None)
        return push(
            full_ref.at[(p, c, *src)],
            full_ref.at[(p, c, *at)],
            g_send.at[p, s, d],
            g_recv.at[p, s, d],
            along(axis, d),
        )

    def spread_start(p, s):
        for d in (2, 1, 3):
            spread(p, s, d, False).start()

    def spread_wait(p, s):
        for d in (1, 2, 3):
            spread(p, s, d, True).wait_recv()

    def share_twin(p, core):
        return push(full_ref.at[p, core], full_ref.at[p, core], t_send.at[p], t_recv.at[p], twin)

    key_rows[...] = qkv_ref[1].astype(F32).T.astype(BF16)
    value_rows[...] = qkv_ref[2].astype(F32).T.astype(BF16)
    dk[...] = jnp.zeros_like(dk)
    dv[...] = jnp.zeros_like(dv)
    halves().wait_recv()
    weights[:512] = (
        weights[pl.ds(pl.multiple_of(1024 + c * 512, 512), 512)].astype(F32) + o_sib[...].astype(F32)
    ).astype(BF16)
    for d in (2, 1, 3):
        quarters(d).start()
    go_home(0)
    each(1, 16, lambda k: cot_in(k).wait_recv())
    row_dot[...] = jnp.sum(cot[...].astype(F32) * ctx_ref[...], axis=0, keepdims=True)

    def queries(b):
        cols = lanes(b, 256)
        q = (qkv_ref[0, :, cols].astype(F32) * 0.125).astype(BF16)
        p = jnp.exp(dot(key_rows[...], q) - lse_ref[:, cols])
        dp = dot(value_rows[...], cot[:, cols])
        ds = (p * (dp - row_dot[:, cols])).astype(BF16)
        pc_here[0, :, cols] = (dot(qkv_ref[1], ds) * 0.125).astype(BF16)
        dk[...] += dot_nt(ds, q)
        dv[...] += dot_nt(p.astype(BF16), cot[:, cols])

    def pair(i, carry):
        queries(2 * i)
        queries(2 * i + 1)

        @pl.when(i == 0)
        def _():
            for d in (1, 2, 3):
                quarters(d).wait_recv()
            o_sum = weights[:512, lanes(x, DB)].astype(F32)
            for d in (1, 2, 3):
                o_sum += o_x[d].astype(F32)
            o_q[...] = o_sum.astype(BF16)
            each(1, 16, lambda k: thirty(k).start())
            few_all = few[:, lanes(2 * x + c, 128)]
            for r in range(1, 8):
                few_share(r).wait_recv()
                few_all += few_rest[r]
            few_sum[...] = few_all
            each(1, 16, lambda k: few_near(k).start())

        @pl.when(i == 1)
        def _():
            far_wait(0)
            far_start(1)

        @pl.when(i == 2)
        def _():
            each(1, 16, lambda k: thirty(k).wait_recv())
            o_sum = o_q[pl.ds(pl.multiple_of(m * 32, 32), 32)].astype(F32)
            for k in range(1, 16):
                o_sum += o_mp[k].astype(F32)
            o_low = o_sum.astype(BF16)
            o_fin[:32] = o_low[:, :128]
            o_fin[32:] = o_low[:, 128:]
            lay = local(o_fin, full_ref.at[3, c, x, z, y], 2)
            lay.start()
            lay.wait()
            spread_start(3, 0)

        return carry

    lax.fori_loop(0, 4, pair, 0)
    pc_here[1] = dk[...].T.astype(BF16)
    pc_here[2] = dv[...].T.astype(BF16)

    def pc_out(k):
        t = (m + k) % 16
        return push(
            pc_here.at[:, :, lanes(t, 128)], pc_tok.at[:, m], b_send.at[k], b_recv.at[k], {"mp": t}
        )

    def pc_in(k):
        s = (m + 16 - k) % 16
        return push(
            pc_here.at[:, :, pl.ds(0, 128)], pc_tok.at[:, s], b_send.at[k], b_recv.at[k], {"mp": s}
        )

    each(1, 16, lambda k: pc_out(k).start())
    pc_tok[:, m] = pc_here[:, :, lanes(m, 128)]

    far_wait(1)
    load_n = [
        local(nall_ref.at[pl.ds(2 * i, 2)], ref.at[pl.ds(0, 1024)].reshape(2, 4, 128, 1024), 2 + i)
        for i, ref in enumerate((back, sib_recv))
    ]
    for copy in load_n:
        copy.start()
    for copy in load_n:
        copy.wait()
    long = pc_here[...].reshape(192, 2048)
    slices[...] = (dot(long[:, :1024], back[:1024]) + dot(long[:, 1024:], sib_recv[:1024])).astype(BF16)

    def share_out(r):
        t = 2 * ((x + r % 4) % 4) + (c + r // 4) % 2
        return push(slices.at[:, lanes(t, 128)], parts.at[r], q_send.at[r], q_recv.at[r], rest(r))

    for r in range(1, 8):
        share_out(r).start()
    spread_wait(3, 0)
    spread_start(3, 1)
    whole = slices[:, lanes(2 * x + c, 128)].astype(F32)
    for r in range(1, 8):
        share_out(r).wait_recv()
    for r in range(1, 8):
        whole += parts[r].astype(F32)
    own_share[...] = whole.astype(BF16).reshape(3, 64, 128)
    lay = local(own_share, full_ref.at[pl.ds(0, 3), c, x, z, y], 2)
    lay.start()
    lay.wait()
    for p in range(3):
        spread_start(p, 0)
    go_home(1)

    each(1, 16, lambda k: pc_in(k).wait_recv())
    for copy in load_q:
        copy.wait()
    dn = sum(dot(rows[i * 1024 : (i + 1) * 1024], pc_tok[i].reshape(1024, 128)) for i in range(3)).T
    hat, scale = unit(x_ref[...].astype(F32))
    gained = dn * gain_ref[...]
    in_ref[...] = mid_cot[...] + scale * (
        gained - hat * jnp.mean(gained * hat, axis=-1, keepdims=True)
    )
    gain_row[...] = jnp.sum(dn * hat, axis=0, keepdims=True)

    def gain_out(k):
        return push(gain_row, gain_mp.at[k], u_send.at[k], u_recv.at[k], mp_at(m, k))

    def gain_far(r):
        return push(gain_mp.at[0], gain_rest.at[r], v_send.at[r], v_recv.at[r], rest(r))

    each(1, 16, lambda k: gain_out(k).start())
    for p in range(3):
        spread_wait(p, 0)
        spread_start(p, 1)
    spread_wait(3, 1)
    spread_start(3, 2)
    go_home(2)

    each(1, 16, lambda k: few_near(k).wait_recv())
    few_all = few_sum[...]
    for k in range(1, 16):
        few_all += few_mp[k]
    few_done[...] = few_all
    few_out_ref[:, lanes(2 * x + c, 128)] = few_all
    for r in range(1, 8):
        few_back(r, False).start()
    for p in range(3):
        spread_wait(p, 1)
        spread_start(p, 2)
    each(1, 16, lambda k: gain_out(k).wait_recv())
    got = gain_row[...]
    for k in range(1, 16):
        got += gain_mp[k]
    gain_mp[0] = got
    for r in range(1, 8):
        gain_far(r).start()
    for r in range(1, 8):
        gain_far(r).wait_recv()
    for r in range(1, 8):
        got += gain_rest[r]
    gain_out_ref[...] = got

    for p in (3, 0, 1, 2):
        spread_wait(p, 2)
        share_twin(p, c).start()
    for i in range(3):
        each_home(lambda at, i=i: home(i, at, at).wait_recv())
    for r in range(1, 8):
        few_back(r, True).wait_recv()
    for p in range(4):
        share_twin(p, 1 - c).wait_recv()

    for p in range(4):
        share_twin(p, c).wait_send()
        for s in range(3):
            for d in (1, 2, 3):
                spread(p, s, d, False).wait_send()
    each(1, 16, lambda k: dispatch(k).wait_send())
    each(1, 16, lambda k: cot_out(k).wait_send())
    each(1, 16, lambda k: pc_out(k).wait_send())
    each(1, 16, lambda k: gain_out(k).wait_send())
    each(1, 16, lambda k: thirty(k).wait_send())
    each(1, 16, lambda k: few_near(k).wait_send())
    for j in (2, 3):
        partials(j).wait_send()
    halves().wait_send()
    for d in (1, 2, 3):
        down_fan(d, x).wait_send()
        quarters(d).wait_send()
    for d in (1, 3):
        for i in range(3):
            relay(i, d).wait_send()
            settle(i, d).wait_send()
        for step in range(2):
            far(0, d, step, m).wait_send()
            far(1, d, step, m).wait_send()
    for r in range(1, 8):
        few_share(r).wait_send()
        few_back(r, False).wait_send()
        share_out(r).wait_send()
        gain_far(r).wait_send()
    for i in range(3):
        each_home(lambda at, i=i: home(i, at, y).wait_send())


def experts_back(*operands):
    dma = pltpu.SemaphoreType.DMA
    vm = pl.BlockSpec(memory_space=VMEM)
    hbm = pl.BlockSpec(memory_space=pl.ANY)
    shape = jax.ShapeDtypeStruct
    width = 4 * DB
    pairs_of = lambda *dims: [dma(dims), dma(dims)]
    return pl.pallas_call(
        experts_back_kernel,
        out_shape=(
            shape((128, 1024), BF16),
            shape((128, 1024), F32),
            shape((1, 1024), F32),
            shape((4, 3, FFB, DB), BF16),
            shape((16, 1024), F32),
            shape((4, 2, 4, 4, 4, 64, 128), BF16),
            shape((16, 2 * ROWS, width), BF16),
            shape((4, 4, 128, 1024), BF16),
        ),
        in_specs=[vm] * 13 + [hbm] * 5,
        out_specs=(vm,) * 5 + (hbm,) * 3,
        scratch_shapes=[
            VMEM((3 * FFQ, width), BF16),
            VMEM((64 * ROWS, width), BF16),
            VMEM((3072, width), BF16),
            VMEM((32 * ROWS, width), BF16),
            VMEM((32 * ROWS, width), BF16),
            VMEM((2, 8 * ROWS, width), BF16),
            VMEM((8 * ROWS, width), F32),
            VMEM((32 * ROWS, FFQ), BF16),
            VMEM((32 * ROWS, FFQ), BF16),
            VMEM((32 * ROWS, FFQ), BF16),
            VMEM((2, 3, FFQ // 2, DB), BF16),
            VMEM((2, 3, FFQ, DB), BF16),
            VMEM((16, 64, 128), BF16),
            VMEM((128, 1024), F32),
            VMEM((16, 1024), F32),
            VMEM((512, 1024), BF16),
            VMEM((4, 512, DB), BF16),
            VMEM((512, DB), BF16),
            VMEM((16, 32, DB), BF16),
            VMEM((64, 128), BF16),
            VMEM((16, 16, 128), F32),
            VMEM((16, 128), F32),
            VMEM((16, 128), F32),
            VMEM((8, 16, 128), F32),
            VMEM((64, 2048), BF16),
            VMEM((2048, 64), BF16),
            VMEM((2048, 64), BF16),
            VMEM((1, 2048), F32),
            VMEM((2048, 64), F32),
            VMEM((2048, 64), F32),
            VMEM((3, 64, 2048), BF16),
            VMEM((3, 16, 64, 128), BF16),
            VMEM((192, 1024), BF16),
            VMEM((3, 64, 128), BF16),
            VMEM((8, 192, 128), BF16),
            VMEM((1, 1024), F32),
            VMEM((16, 1, 1024), F32),
            VMEM((8, 1, 1024), F32),
            dma((8,)),
            *pairs_of(16),
            *pairs_of(16),
            *pairs_of(4),
            *pairs_of(16),
            *pairs_of(4),
            *pairs_of(2, 3, 4),
            *pairs_of(3, 4),
            *pairs_of(2, 2, 4),
            *pairs_of(16),
            *pairs_of(16),
            *pairs_of(8),
            *pairs_of(4, 3, 4),
            *pairs_of(4),
            *pairs_of(16),
            *pairs_of(8),
            *pairs_of(1),
            *pairs_of(4),
            *pairs_of(16),
            *pairs_of(16),
            *pairs_of(2, 8),
        ],
        compiler_params=params(2, 63),
    )(*operands)


def unfold_kernel(f_ref, o_ref, g_ref, qkv_ref, out_ref, gate_ref, up_ref, down_ref):
    qkv_ref[...] = f_ref[...].reshape(3072, 128).astype(F32).T
    for i in range(4):
        for h in range(2):
            part = o_ref[i, :, 32 * h : 32 * (h + 1)].reshape(128, 128)
            out_ref[:, (2 * i + h) * 128 : (2 * i + h + 1) * 128] = part.astype(F32)
    gate_ref[...] = g_ref[0].astype(F32)
    up_ref[...] = g_ref[1].astype(F32)
    down_ref[...] = g_ref[2].astype(F32)


def unfold(full, blocks):
    shape = jax.ShapeDtypeStruct
    share = pl.BlockSpec((None, FFB, 128), lambda i, j: (i, 0, j))
    return pl.pallas_call(
        unfold_kernel,
        out_shape=(
            shape((1024, 3072), F32),
            shape((1024, 1024), F32),
            *[shape((4, FFB, DB), F32)] * 3,
        ),
        grid=(4, 2),
        in_specs=[
            pl.BlockSpec((3, None, None, 4, 4, 64, 128), lambda i, j: (0, j, i, 0, 0, 0, 0)),
            pl.BlockSpec((None, None, 4, None, 4, 64, 128), lambda i, j: (3, j, 0, i, 0, 0, 0)),
            pl.BlockSpec((None, 3, FFB, 128), lambda i, j: (i, 0, 0, j)),
        ],
        out_specs=(
            pl.BlockSpec((128, 3072), lambda i, j: (2 * i + j, 0)),
            pl.BlockSpec((128, 1024), lambda i, j: (4 * j + i, 0)),
            *[share] * 3,
        ),
        compiler_params=pltpu.CompilerParams(vmem_limit_bytes=48 * 1024 * 1024),
    )(full, full, blocks)


def body(
    block_input,
    attn_gain,
    qkv_weight,
    out_weight,
    moe_gain,
    router_weight,
    gate_weight,
    up_weight,
    down_weight,
    routes,
    slot_index,
    cotangent,
):
    pairs = jnp.concatenate([routes.T, slot_index.T, jnp.zeros((4, 128), jnp.int32)]).astype(F32)
    (
        send,
        middle,
        probs,
        ctx_tok,
        qkv,
        ctx_here,
        lse,
        down,
        near,
        weights,
        qkv_low,
        out_low,
    ) = attend(
        block_input,
        attn_gain,
        gate_weight,
        up_weight,
        down_weight,
        moe_gain,
        router_weight,
        pairs,
        cotangent,
        qkv_weight,
        out_weight,
    )
    block_output, input_grad, gain_grad, mine, few, full, _, _ = experts_back(
        middle,
        probs,
        pairs,
        cotangent,
        moe_gain.reshape(1, -1),
        router_weight.T,
        ctx_tok,
        qkv,
        ctx_here,
        lse,
        block_input,
        attn_gain.reshape(1, -1),
        down,
        send,
        weights,
        near,
        qkv_low,
        out_low,
    )
    qkv_grad, out_grad, gate_grad, up_grad, down_grad = unfold(full, mine)
    return (
        block_output,
        input_grad,
        gain_grad.reshape(-1),
        qkv_grad,
        out_grad,
        few[8],
        few[:8].T,
        jnp.swapaxes(gate_grad, 1, 2),
        jnp.swapaxes(up_grad, 1, 2),
        down_grad,
    )


def solution(mesh):
    tokens = P(("dp", "expert", "mp"), None)
    cols = P("expert", "dp", "mp")
    rows = P("expert", "mp", "dp")
    return jax.shard_map(
        body,
        mesh=mesh,
        in_specs=(tokens, P(), P(), P(), P(), P(), cols, cols, rows, tokens, tokens, tokens),
        out_specs=(tokens, tokens, P(), P(), P(), P(), P(), cols, cols, rows),
        check_vma=False,
    )
```

time: 290 us -> 258 us (0.89)
  Pallas kernels: 275 us -> 249 us
  other arithmetic: 5.55 us -> 1.36 us
    pallas_call x1, Pallas kernels: 71.1 us -> 56.7 us  [attend(): pl.pallas_call(attend_kernel, out_shape=(shape((8, 2 * ROWS, 1024), BF16)...]
    pallas_call x3 -> x2, Pallas kernels: 204 us -> 192 us  [the longest x1 181 us: experts_back(): pl.pallas_call(experts_back_kernel, out_shape=(shape((128, 1024), BF16),...]
    convert_element_type x2 -> x0, other arithmetic: 4.2 us -> none  [the longest x1 2.61 us: body(): out_grad.reshape(width, width).astype(F32)]
where the time goes in v4:
time: 258 us; the launch traced here: 257 us
  Pallas kernels  249 us (97%)
  local copies, waits for them, and re-layouts  6.14 us (2%)
    pallas_call x1, Pallas kernels, experts_back(): pl.pallas_call(experts_back_kernel, out_shape=(shape((128, 1024), BF16),...  181 us
    pallas_call x1, Pallas kernels, attend(): pl.pallas_call(attend_kernel, out_shape=(shape((8, 2 * ROWS, 1024), BF16)...  56.7 us
    pallas_call x1, Pallas kernels, unfold(): pl.pallas_call(unfold_kernel, out_shape=(shape((1024, 3072), F32), shape(...  11.2 us

profile of v4, /device:TPU:1, one launch (start us, length us, event | category | flops | bytes accessed | tf_op | source)
XLA Modules:
  0.0 257.2 jit_solution(8737045341786152571)
XLA Ops:
  0.7 0.1 pad.2.clone
  0.7 1.4 add_convert_fusion.pairs_ref
  2.1 56.7 %shard_map.195 = (bf16[8,80,1024]{2,1,0:T(8,128)(2,1)}, f32[128,1024]{1,0:T(8,128)}, f32[128,8]{1,0:T(8,128)}, bf16[1024,128]{1,0:T(8,128)(2,1)}, bf16[3,64,2048...) custom-call(bf16[128,1024]{1,0:T(8,128)(2,1)} %x_ref.3, ...), custom_call_target="tpu_custom_call" | custom-call | tf_op jit(solution)/shard_map/pallas_call | solution.py:444
  58.8 181.1 %shard_map.196 = (bf16[128,1024]{1,0:T(8,128)(2,1)}, f32[128,1024]{1,0:T(8,128)}, f32[1,1024]{1,0:T(1,128)}, bf16[4,3,176,256]{3,2,1,0:T(8,128)(2,1)}, f32[16,10...) custom-call(f32[128,1024]{1,0:T(8,128)} %get-tuple-element.33.mid_re, ...), custom_call_target="tpu_custom_call" | custom-call | tf_op jit(solution)/shard_map/pallas_call | solution.py:1232
  239.9 1.4 slice.6
  241.2 1.4 slice_bitcast_fusion
  242.6 0.0 copy-start
  242.6 1.2 copy-done
  243.9 0.0 copy-start.2
  243.9 0.0 copy-start.1
  243.9 0.0 copy-start.3
  243.9 11.2 %shard_map.197 = (f32[1024,3072]{1,0:T(8,128)}, f32[1024,1024]{1,0:T(8,128)}, f32[4,176,256]{2,1,0:T(8,128)}, f32[4,176,256]{2,1,0:T(8,128)}, f32[4,176,256]{2,1,0:T(8,128)}) custom-call(bf16[4,2,4,4,4,64,128]{6,5,4,3,2,1,0:T(8,128)(2,1)} %get-tuple-element.48.f_ref.o_ref, bf16[4,2,4,4,4,64,128]{6,5,4,3,2,1,0:T(8,128)(2,1)} %get-tuple-element.48.f_ref.o_ref, ...), custom_call_target="tpu_custom_call" | custom-call | tf_op jit(solution)/shard_map/pallas_call | solution.py:1325
  255.1 0.0 copy-done.2
  255.1 0.7 copy.25
  255.8 0.0 copy-done.1
  255.8 0.8 copy.26
  256.6 0.0 copy-done.3
  256.6 0.6 copy.27
  (1 shorter events, 0.0 us)
Async XLA Ops:
  242.6 1.2 copy-start
  243.9 11.2 %copy-start.2 = (bf16[128,1024]{1,0:T(8,128)(2,1)S(1)}, bf16[128,1024]{1,0:T(8,128)(2,1)}, u32[]{:S(2)}) copy-start(bf16[128,1024]{1,0:T(8,128)(2,1)} %get-tuple-element.66) | copy-start | bytes 786436
  243.9 12.0 %copy-start.1 = (f32[128,1024]{1,0:T(8,128)S(1)}, f32[128,1024]{1,0:T(8,128)}, u32[]{:S(2)}) copy-start(f32[128,1024]{1,0:T(8,128)} %get-tuple-element.67) | copy-start | bytes 1572868
  243.9 12.7 %copy-start.3 = (f32[1,1024]{1,0:T(1,128)S(1)}, f32[1,1024]{1,0:T(1,128)}, u32[]{:S(2)}) copy-start(f32[1,1024]{1,0:T(1,128)} %get-tuple-element.47) | copy-start | bytes 12292

commit v5 on v4

--- a/solution.py
+++ b/solution.py
@@ -119,7 +119,6 @@
     qkv_ref,
     ctx_here_ref,
     lse_ref,
-    down_ref,
     nall_ref,
     w_out_ref,
     wq_out_ref,
@@ -238,6 +237,14 @@
     y_from = [z * 4 + (y + 4 - d) % 4 for d in range(4)]
     z_from = [((z + 4 - d) % 4) * 4 + y for d in range(4)]
 
+    def far(part, d, origin):
+        cols = pl.ds(part * half, half)
+        if part == 0:
+            ref, device = nall_ref.at[origin // 4, :, :, cols], z_at(z, y, d)
+        else:
+            ref, device = nall_ref.at[:, origin % 4, :, cols], y_at(z, y, d)
+        return push(ref, ref, n_send.at[part, 1, d], n_recv.at[part, 1, d], device)
+
     for i in range(6):
         load(i).wait()
         cols = slice(i * wide, (i + 1) * wide)
@@ -277,6 +284,11 @@
     own.start()
     mine = pltpu.make_async_copy(normed, nall_ref.at[z, y], here.at[1])
     mine.start()
+    blocks_out(1)
+    blocks_out(2)
+    for d in (2, 1, 3):
+        near(0, d)(m).start()
+        near(1, d)(m).start()
 
 
     def fan(i, d, step, at):
@@ -310,11 +322,6 @@
 
     own.wait()
     each(1, 16, lambda k: head_in(k).wait_recv())
-    blocks_out(1)
-    blocks_out(2)
-    for d in (2, 1, 3):
-        near(0, d)(m).start()
-        near(1, d)(m).start()
 
     key_rows[...] = qkv_ref[1].astype(F32).T.astype(BF16)
 
@@ -373,16 +380,24 @@
             fan_wait(0, 0)
             fan_start(0, 1)
             blocks_in(2)
+            fan_start(2, 0)
+            fan_own(2).start()
 
         return carry
 
     lax.fori_loop(0, 4, pair, 0)
+    for d in (1, 2, 3):
+        near(0, d)(y_from[d]).wait_recv()
+        near(1, d)(z_from[d]).wait_recv()
+    mine.wait()
+    for d in (1, 3):
+        far(0, d, m).start()
+        far(1, d, m).start()
     ctx_ref[pl.ds(pl.multiple_of(m * 64, 64), 64), :] = ctx_low[:, lanes(m, 128)]
     each(1, 16, lambda k: ctx_in(k).wait_recv())
 
     fan_wait(1, 0)
     fan_start(1, 1)
-    down_ref[...] = stage[2]
 
     mid = x_ref[...].astype(F32) + dot_tn(ctx_ref[...], wo_ref[...])
     mid_ref[...] = mid
@@ -405,15 +420,20 @@
         save(i).wait()
     save_o.wait()
     fan_wait(0, 1)
+    fan_wait(2, 0)
+    fan_start(2, 1)
     fan_wait(1, 1)
-    for d in (1, 2, 3):
-        near(0, d)(y_from[d]).wait_recv()
-        near(1, d)(z_from[d]).wait_recv()
+    fan_wait(2, 1)
+    for d in (1, 3):
+        far(0, d, z_from[d]).wait_recv()
+        far(1, d, y_from[d]).wait_recv()
     for d in (1, 2, 3):
         near(0, d)(m).wait_send()
         near(1, d)(m).wait_send()
-    mine.wait()
-    for i in range(2):
+    for d in (1, 3):
+        far(0, d, m).wait_send()
+        far(1, d, m).wait_send()
+    for i in range(3):
         fan_own(i).wait()
         for d in (1, 3):
             for step in range(2):
@@ -451,14 +471,13 @@
             shape((3, 64, 2048), BF16),
             shape((64, 2048), F32),
             shape((1, 2048), F32),
-            shape((FFQ, DB), BF16),
             shape((4, 4, 128, 1024), BF16),
-            shape((2, FFQ, 4 * DB), BF16),
+            shape((3, FFQ, 4 * DB), BF16),
             shape((1024, 3072), BF16),
             shape((1024, 1024), BF16),
         ),
         in_specs=[vm] * 9 + [hbm] * 2,
-        out_specs=(vm,) * 8 + (hbm,) * 4,
+        out_specs=(vm,) * 7 + (hbm,) * 4,
         scratch_shapes=[
             VMEM((1024, 3072), F32),
             VMEM((1024, 1024), F32),
@@ -473,12 +492,12 @@
             dma((11,)),
             dma((3, 4)),
             dma((3, 4)),
+            dma((3, 2, 4)),
+            dma((3, 2, 4)),
+            dma((16,)),
+            dma((16,)),
             dma((2, 2, 4)),
             dma((2, 2, 4)),
-            dma((16,)),
-            dma((16,)),
-            dma((2, 1, 4)),
-            dma((2, 1, 4)),
             dma((16,)),
             dma((16,)),
         ],
@@ -515,7 +534,6 @@
     lse_ref,
     x_ref,
     gain_ref,
-    down_ref,
     send_hbm,
     w_hbm,
     near_hbm,
@@ -542,27 +560,23 @@
     g_relay,
     g_near,
     dctx,
-    mid_cot,
     few,
     o_sib,
     o_x,
     o_q,
     o_mp,
-    o_fin,
     few_mp,
     few_sum,
     few_done,
     few_rest,
     cot,
-    key_rows,
-    value_rows,
+    key_values,
     row_dot,
-    dk,
-    dv,
+    dkv,
     pc_here,
     pc_tok,
     slices,
-    own_share,
+    share,
     parts,
     gain_row,
     gain_mp,
@@ -576,8 +590,6 @@
     p_recv,
     r_send,
     r_recv,
-    w_send,
-    w_recv,
     x_send,
     x_recv,
     s_send,
@@ -645,13 +657,15 @@
 
     for r in range(1, 8):
         pl.semaphore_signal(barrier, inc=1, device_id=rest(r), device_id_type=MESH)
-    load_w = [local(w_hbm.at[i], weights.at[pl.ds(i * FFQ, FFQ)], i) for i in range(2)]
+    load_w = [local(w_hbm.at[i], weights.at[pl.ds(i * FFQ, FFQ)], i) for i in range(3)]
     for copy in load_w:
         copy.start()
-    near = [
-        local(near_hbm.at[z, :, :, pl.ds(0, 512)], nall_ref.at[z, :, :, pl.ds(0, 512)], 2),
-        local(near_hbm.at[:, y, :, pl.ds(512, 512)], nall_ref.at[:, y, :, pl.ds(512, 512)], 3),
-    ]
+    near = []
+    for i, d in enumerate((0, 1, 3)):
+        at = (z + d) % 4, slice(None), slice(None), pl.ds(0, 512)
+        near.append(local(near_hbm.at[at], nall_ref.at[at], 8 + i))
+        at = slice(None), (y + d) % 4, slice(None), pl.ds(512, 512)
+        near.append(local(near_hbm.at[at], nall_ref.at[at], 11 + i))
     for copy in near:
         copy.start()
     pl.semaphore_wait(barrier, 15 + 3 + away + 7)
@@ -692,21 +706,9 @@
             back.at[spot_of(k)], ret_ref.at[at], r_send.at[k], r_recv.at[k], mp_at(m, 16 - k)
         )
 
-    def down_fan(d, at):
-        return push(
-            down_ref,
-            weights.at[pl.ds(2 * FFQ, FFQ), lanes(at, DB)],
-            w_send.at[d],
-            w_recv.at[d],
-            {"dp": (x + d) % 4},
-        )
-
     each(1, 16, lambda k: dispatch(k).start())
     own = local(send_hbm.at[expert_of(m)], recv.at[slot(0, 0)], 4)
     own.start()
-    for d in (2, 1, 3):
-        down_fan(d, x).start()
-    weights[2 * FFQ :, lanes(x, DB)] = down_ref[...]
     own.wait()
 
     def finish(j):
@@ -745,8 +747,6 @@
         def _():
             for copy in load_w:
                 copy.wait()
-            for d in (1, 2, 3):
-                down_fan(d, (x + 4 - d) % 4).wait_recv()
 
         for i in range(4):
             forward(4 * j + i).wait_recv()
@@ -873,27 +873,14 @@
 
     for copy in near:
         copy.wait()
-    y_from = [z * 4 + (y + 4 - d) % 4 for d in range(4)]
-    z_from = [((z + 4 - d) % 4) * 4 + y for d in range(4)]
-
-    def far(part, d, step, origin):
-        cols = pl.ds(part * 512, 512)
-        some = pl.ds(0, 4) if step == 0 else pl.ds(0 if d == 1 else 2, 2)
+
+    def far(part, d, hops):
+        cols, some = pl.ds(part * 512, 512), pl.ds(0 if d == 1 else 2, 2)
         if part == 0:
-            ref, device = nall_ref.at[origin // 4, some, :, cols], z_at(z, y, d)
+            ref, device = nall_ref.at[(z + 8 - hops * d) % 4, some, :, cols], z_at(z, y, d)
         else:
-            ref, device = nall_ref.at[some, origin % 4, :, cols], y_at(z, y, d)
-        return push(ref, ref, n_send.at[part, step, d], n_recv.at[part, step, d], device)
-
-    def far_wait(step):
-        for part, origins in enumerate((z_from, y_from)):
-            for d in (1, 3):
-                far(part, d, step, origins[(d * (1 + step)) % 4]).wait_recv()
-
-    def far_start(step):
-        for part, origins in enumerate((z_from, y_from)):
-            for d in (1, 3):
-                far(part, d, step, origins[d * step]).start()
+            ref, device = nall_ref.at[some, (y + 8 - hops * d) % 4, :, cols], y_at(z, y, d)
+        return push(ref, ref, n_send.at[part, d], n_recv.at[part, d], device)
 
     columns = pairs_ref[...].T
     hot = picks(columns)
@@ -920,8 +907,8 @@
         [jnp.sum(moe_cot * hat, axis=0, keepdims=True), jnp.zeros((7, 1024), F32)], axis=0
     )
     gained = moe_cot * moe_gain_ref[...]
-    mid_cot[...] = upstream + scale * (gained - hat * jnp.mean(gained * hat, axis=-1, keepdims=True))
-    branch_cot = mid_cot[...].astype(BF16)
+    in_ref[...] = upstream + scale * (gained - hat * jnp.mean(gained * hat, axis=-1, keepdims=True))
+    branch_cot = in_ref[...].astype(BF16)
     load_o.wait()
     dctx[...] = dot_nt(weights[:1024], branch_cot).astype(BF16).reshape(16, 64, 128)
 
@@ -934,7 +921,9 @@
         return push(dctx.at[0], cot.at[:, lanes(s, 128)], a_send.at[k], a_recv.at[k], {"mp": s})
 
     each(1, 16, lambda k: cot_out(k).start())
-    far_start(0)
+    for d in (1, 3):
+        far(0, d, 1).start()
+        far(1, d, 1).start()
     cot[:, lanes(m, 128)] = dctx[m]
 
     weights[1024:2048] = dot(tok_ref[...], branch_cot).astype(BF16)
@@ -946,7 +935,7 @@
     def quarters(d):
         t = (x + d) % 4
         return push(
-            weights.at[pl.ds(0, 512), lanes(t, DB)], o_x.at[d], ox_send.at[d], ox_recv.at[d], {"dp": t}
+            weights.at[pl.ds(0, 512), lanes(t, DB)], o_x.at[d - 1], ox_send.at[d], ox_recv.at[d], {"dp": t}
         )
 
     def thirty(k):
@@ -983,7 +972,8 @@
             return {"dp": (x + d) % 4}
         return z_at(z, y, d) if axis == 1 else y_at(z, y, d)
 
-    orders = ((0, 2, 1), (2, 1, 0), (1, 0, 2), (1, 2, 0))
+    orders = ((0, 2, 1), (1, 0, 2), (2, 1, 0), (0, 2, 1), (0, 1, 2))
+    spans = [pl.ds(0, 64), pl.ds(64, 64), pl.ds(128, 64), pl.ds(192, 32), pl.ds(224, 32)]
 
     def spread(p, s, d, incoming):
         at = [x, z, y]
@@ -995,8 +985,8 @@
             at[done] = slice(None)
             src[done] = slice(None)
         return push(
-            full_ref.at[(p, c, *src)],
-            full_ref.at[(p, c, *at)],
+            full_ref.at[(c, *src, spans[p])],
+            full_ref.at[(c, *at, spans[p])],
             g_send.at[p, s, d],
             g_recv.at[p, s, d],
             along(axis, d),
@@ -1006,17 +996,33 @@
         for d in (2, 1, 3):
             spread(p, s, d, False).start()
 
+    def last(p, d, hops):
+        at = [slice(None)] * 3
+        axis = orders[p][2]
+        at[axis] = ((x, z, y)[axis] + 8 - hops * d) % 4
+        return at
+
+    def circle(p, d, step, incoming):
+        at = last(p, d, step + incoming)
+        if step:
+            at[orders[p][0]] = pl.ds(0 if d == 1 else 2, 2)
+        ref = full_ref.at[(c, *at, spans[p])]
+        return push(ref, ref, g_send.at[p, 2 + step, d], g_recv.at[p, 2 + step, d], along(orders[p][2], d))
+
     def spread_wait(p, s):
         for d in (1, 2, 3):
             spread(p, s, d, True).wait_recv()
 
-    def share_twin(p, core):
-        return push(full_ref.at[p, core], full_ref.at[p, core], t_send.at[p], t_recv.at[p], twin)
-
-    key_rows[...] = qkv_ref[1].astype(F32).T.astype(BF16)
-    value_rows[...] = qkv_ref[2].astype(F32).T.astype(BF16)
-    dk[...] = jnp.zeros_like(dk)
-    dv[...] = jnp.zeros_like(dv)
+    def share_twin(p, i, core):
+        d, hops = ((1, 0), (1, 1), (3, 1), (1, 2), (3, 2))[i]
+        at = last(p, d, hops)
+        if hops == 2:
+            at[orders[p][0]] = pl.ds(0 if d == 1 else 2, 2)
+        ref = full_ref.at[(core, *at, spans[p])]
+        return push(ref, ref, t_send.at[p, i], t_recv.at[p, i], twin)
+
+    key_values[...] = qkv_ref[1:].reshape(128, 2048).astype(F32).T.astype(BF16)
+    dkv[...] = jnp.zeros_like(dkv)
     halves().wait_recv()
     weights[:512] = (
         weights[pl.ds(pl.multiple_of(1024 + c * 512, 512), 512)].astype(F32) + o_sib[...].astype(F32)
@@ -1030,24 +1036,30 @@
     def queries(b):
         cols = lanes(b, 256)
         q = (qkv_ref[0, :, cols].astype(F32) * 0.125).astype(BF16)
-        p = jnp.exp(dot(key_rows[...], q) - lse_ref[:, cols])
-        dp = dot(value_rows[...], cot[:, cols])
+        none = jnp.zeros((64, 256), BF16)
+        q = jnp.concatenate([q, none], axis=0)
+        g = jnp.concatenate([none, cot[:, cols]], axis=0)
+        p = jnp.exp(dot(key_values[...], q) - lse_ref[:, cols])
+        dp = dot(key_values[...], g)
         ds = (p * (dp - row_dot[:, cols])).astype(BF16)
         pc_here[0, :, cols] = (dot(qkv_ref[1], ds) * 0.125).astype(BF16)
-        dk[...] += dot_nt(ds, q)
-        dv[...] += dot_nt(p.astype(BF16), cot[:, cols])
+        dkv[...] += dot_nt(ds, q) + dot_nt(p.astype(BF16), g)
 
     def pair(i, carry):
         queries(2 * i)
         queries(2 * i + 1)
 
-        @pl.when(i == 0)
+        @pl.when(i == 1)
+        def _():
+            go_home(1)
+
+        @pl.when(i == 2)
         def _():
             for d in (1, 2, 3):
                 quarters(d).wait_recv()
             o_sum = weights[:512, lanes(x, DB)].astype(F32)
             for d in (1, 2, 3):
-                o_sum += o_x[d].astype(F32)
+                o_sum += o_x[d - 1].astype(F32)
             o_q[...] = o_sum.astype(BF16)
             each(1, 16, lambda k: thirty(k).start())
             few_all = few[:, lanes(2 * x + c, 128)]
@@ -1056,31 +1068,12 @@
                 few_all += few_rest[r]
             few_sum[...] = few_all
             each(1, 16, lambda k: few_near(k).start())
-
-        @pl.when(i == 1)
-        def _():
-            far_wait(0)
-            far_start(1)
-
-        @pl.when(i == 2)
-        def _():
-            each(1, 16, lambda k: thirty(k).wait_recv())
-            o_sum = o_q[pl.ds(pl.multiple_of(m * 32, 32), 32)].astype(F32)
-            for k in range(1, 16):
-                o_sum += o_mp[k].astype(F32)
-            o_low = o_sum.astype(BF16)
-            o_fin[:32] = o_low[:, :128]
-            o_fin[32:] = o_low[:, 128:]
-            lay = local(o_fin, full_ref.at[3, c, x, z, y], 2)
-            lay.start()
-            lay.wait()
-            spread_start(3, 0)
+            go_home(2)
 
         return carry
 
     lax.fori_loop(0, 4, pair, 0)
-    pc_here[1] = dk[...].T.astype(BF16)
-    pc_here[2] = dv[...].T.astype(BF16)
+    pc_here[1:] = dkv[...].T.astype(BF16).reshape(2, 64, 2048)
 
     def pc_out(k):
         t = (m + k) % 16
@@ -1097,17 +1090,11 @@
     each(1, 16, lambda k: pc_out(k).start())
     pc_tok[:, m] = pc_here[:, :, lanes(m, 128)]
 
-    far_wait(1)
-    load_n = [
-        local(nall_ref.at[pl.ds(2 * i, 2)], ref.at[pl.ds(0, 1024)].reshape(2, 4, 128, 1024), 2 + i)
-        for i, ref in enumerate((back, sib_recv))
-    ]
-    for copy in load_n:
-        copy.start()
-    for copy in load_n:
-        copy.wait()
+    for d in (1, 3):
+        far(0, d, 2).wait_recv()
+        far(1, d, 2).wait_recv()
     long = pc_here[...].reshape(192, 2048)
-    slices[...] = (dot(long[:, :1024], back[:1024]) + dot(long[:, 1024:], sib_recv[:1024])).astype(BF16)
+    slices[...] = dot(long, nall_ref[...].reshape(2048, 1024)).astype(BF16)
 
     def share_out(r):
         t = 2 * ((x + r % 4) % 4) + (c + r // 4) % 2
@@ -1115,20 +1102,44 @@
 
     for r in range(1, 8):
         share_out(r).start()
-    spread_wait(3, 0)
-    spread_start(3, 1)
     whole = slices[:, lanes(2 * x + c, 128)].astype(F32)
     for r in range(1, 8):
         share_out(r).wait_recv()
     for r in range(1, 8):
         whole += parts[r].astype(F32)
-    own_share[...] = whole.astype(BF16).reshape(3, 64, 128)
-    lay = local(own_share, full_ref.at[pl.ds(0, 3), c, x, z, y], 2)
+    share[:192] = whole.astype(BF16)
+    lay = local(share.at[pl.ds(0, 192)], full_ref.at[c, x, z, y, pl.ds(0, 192)], 2)
     lay.start()
     lay.wait()
     for p in range(3):
         spread_start(p, 0)
-    go_home(1)
+    each(1, 16, lambda k: thirty(k).wait_recv())
+    o_sum = o_q[pl.ds(pl.multiple_of(m * 32, 32), 32)].astype(F32)
+    for k in range(1, 16):
+        o_sum += o_mp[k].astype(F32)
+    o_low = o_sum.astype(BF16)
+    share[192:224] = o_low[:, :128]
+    share[224:] = o_low[:, 128:]
+    lay = local(share.at[pl.ds(192, 64)], full_ref.at[c, x, z, y, pl.ds(192, 64)], 2)
+    lay.start()
+    lay.wait()
+    for p in (3, 4):
+        spread_start(p, 0)
+
+    def circles(p):
+        spread_wait(p, 1)
+        for d in (1, 3):
+            circle(p, d, 0, 0).start()
+        share_twin(p, 0, c).start()
+
+    for p in range(3):
+        spread_wait(p, 0)
+        spread_start(p, 1)
+    for p in range(3):
+        circles(p)
+    for p in (3, 4):
+        spread_wait(p, 0)
+        spread_start(p, 1)
 
     each(1, 16, lambda k: pc_in(k).wait_recv())
     for copy in load_q:
@@ -1136,7 +1147,7 @@
     dn = sum(dot(rows[i * 1024 : (i + 1) * 1024], pc_tok[i].reshape(1024, 128)) for i in range(3)).T
     hat, scale = unit(x_ref[...].astype(F32))
     gained = dn * gain_ref[...]
-    in_ref[...] = mid_cot[...] + scale * (
+    in_ref[...] = in_ref[...] + scale * (
         gained - hat * jnp.mean(gained * hat, axis=-1, keepdims=True)
     )
     gain_row[...] = jnp.sum(dn * hat, axis=0, keepdims=True)
@@ -1148,13 +1159,26 @@
         return push(gain_mp.at[0], gain_rest.at[r], v_send.at[r], v_recv.at[r], rest(r))
 
     each(1, 16, lambda k: gain_out(k).start())
+    for p in (3, 4):
+        circles(p)
+
+    def onward(p):
+        for i, d in ((1, 1), (2, 3)):
+            circle(p, d, 0, 1).wait_recv()
+            circle(p, d, 1, 0).start()
+            share_twin(p, i, c).start()
+
     for p in range(3):
-        spread_wait(p, 0)
-        spread_start(p, 1)
-    spread_wait(3, 1)
-    spread_start(3, 2)
-    go_home(2)
-
+        onward(p)
+    each(1, 16, lambda k: gain_out(k).wait_recv())
+    got = gain_row[...]
+    for k in range(1, 16):
+        got += gain_mp[k]
+    gain_mp[0] = got
+    for r in range(1, 8):
+        gain_far(r).start()
+    for p in (3, 4):
+        onward(p)
     each(1, 16, lambda k: few_near(k).wait_recv())
     few_all = few_sum[...]
     for k in range(1, 16):
@@ -1163,37 +1187,32 @@
     few_out_ref[:, lanes(2 * x + c, 128)] = few_all
     for r in range(1, 8):
         few_back(r, False).start()
-    for p in range(3):
-        spread_wait(p, 1)
-        spread_start(p, 2)
-    each(1, 16, lambda k: gain_out(k).wait_recv())
-    got = gain_row[...]
-    for k in range(1, 16):
-        got += gain_mp[k]
-    gain_mp[0] = got
-    for r in range(1, 8):
-        gain_far(r).start()
+    for p in range(5):
+        for i, d in ((3, 1), (4, 3)):
+            circle(p, d, 1, 1).wait_recv()
+            share_twin(p, i, c).start()
     for r in range(1, 8):
         gain_far(r).wait_recv()
     for r in range(1, 8):
         got += gain_rest[r]
     gain_out_ref[...] = got
-
-    for p in (3, 0, 1, 2):
-        spread_wait(p, 2)
-        share_twin(p, c).start()
     for i in range(3):
         each_home(lambda at, i=i: home(i, at, at).wait_recv())
     for r in range(1, 8):
         few_back(r, True).wait_recv()
-    for p in range(4):
-        share_twin(p, 1 - c).wait_recv()
-
-    for p in range(4):
-        share_twin(p, c).wait_send()
-        for s in range(3):
-            for d in (1, 2, 3):
-                spread(p, s, d, False).wait_send()
+    for p in range(5):
+        for i in range(5):
+            share_twin(p, i, 1 - c).wait_recv()
+
+    for p in range(5):
+        for i in range(5):
+            share_twin(p, i, c).wait_send()
+        for d in (1, 2, 3):
+            spread(p, 0, d, False).wait_send()
+            spread(p, 1, d, False).wait_send()
+        for d in (1, 3):
+            circle(p, d, 0, 0).wait_send()
+            circle(p, d, 1, 0).wait_send()
     each(1, 16, lambda k: dispatch(k).wait_send())
     each(1, 16, lambda k: cot_out(k).wait_send())
     each(1, 16, lambda k: pc_out(k).wait_send())
@@ -1204,15 +1223,13 @@
         partials(j).wait_send()
     halves().wait_send()
     for d in (1, 2, 3):
-        down_fan(d, x).wait_send()
         quarters(d).wait_send()
     for d in (1, 3):
         for i in range(3):
             relay(i, d).wait_send()
             settle(i, d).wait_send()
-        for step in range(2):
-            far(0, d, step, m).wait_send()
-            far(1, d, step, m).wait_send()
+        far(0, d, 1).wait_send()
+        far(1, d, 1).wait_send()
     for r in range(1, 8):
         few_share(r).wait_send()
         few_back(r, False).wait_send()
@@ -1237,13 +1254,13 @@
             shape((1, 1024), F32),
             shape((4, 3, FFB, DB), BF16),
             shape((16, 1024), F32),
-            shape((4, 2, 4, 4, 4, 64, 128), BF16),
+            shape((2, 4, 4, 4, 256, 128), BF16),
             shape((16, 2 * ROWS, width), BF16),
-            shape((4, 4, 128, 1024), BF16),
         ),
-        in_specs=[vm] * 13 + [hbm] * 5,
-        out_specs=(vm,) * 5 + (hbm,) * 3,
+        in_specs=[vm] * 12 + [hbm] * 5,
+        out_specs=(vm,) * 3 + (hbm, vm, vm, hbm),
         scratch_shapes=[
+            VMEM((4, 4, 128, 1024), BF16),
             VMEM((3 * FFQ, width), BF16),
             VMEM((64 * ROWS, width), BF16),
             VMEM((3072, width), BF16),
@@ -1257,45 +1274,40 @@
             VMEM((2, 3, FFQ // 2, DB), BF16),
             VMEM((2, 3, FFQ, DB), BF16),
             VMEM((16, 64, 128), BF16),
-            VMEM((128, 1024), F32),
             VMEM((16, 1024), F32),
             VMEM((512, 1024), BF16),
-            VMEM((4, 512, DB), BF16),
+            VMEM((3, 512, DB), BF16),
             VMEM((512, DB), BF16),
             VMEM((16, 32, DB), BF16),
-            VMEM((64, 128), BF16),
             VMEM((16, 16, 128), F32),
             VMEM((16, 128), F32),
             VMEM((16, 128), F32),
             VMEM((8, 16, 128), F32),
             VMEM((64, 2048), BF16),
-            VMEM((2048, 64), BF16),
-            VMEM((2048, 64), BF16),
+            VMEM((2048, 128), BF16),
             VMEM((1, 2048), F32),
-            VMEM((2048, 64), F32),
-            VMEM((2048, 64), F32),
+            VMEM((2048, 128), F32),
             VMEM((3, 64, 2048), BF16),
             VMEM((3, 16, 64, 128), BF16),
             VMEM((192, 1024), BF16),
-            VMEM((3, 64, 128), BF16),
+            VMEM((256, 128), BF16),
             VMEM((8, 192, 128), BF16),
             VMEM((1, 1024), F32),
             VMEM((16, 1, 1024), F32),
             VMEM((8, 1, 1024), F32),
-            dma((8,)),
+            dma((14,)),
             *pairs_of(16),
             *pairs_of(16),
             *pairs_of(4),
             *pairs_of(16),
-            *pairs_of(4),
             *pairs_of(2, 3, 4),
             *pairs_of(3, 4),
-            *pairs_of(2, 2, 4),
+            *pairs_of(2, 4),
             *pairs_of(16),
             *pairs_of(16),
             *pairs_of(8),
-            *pairs_of(4, 3, 4),
-            *pairs_of(4),
+            *pairs_of(5, 4, 4),
+            *pairs_of(5, 5),
             *pairs_of(16),
             *pairs_of(8),
             *pairs_of(1),
@@ -1308,8 +1320,14 @@
     )(*operands)
 
 
-def unfold_kernel(f_ref, o_ref, g_ref, qkv_ref, out_ref, gate_ref, up_ref, down_ref):
-    qkv_ref[...] = f_ref[...].reshape(3072, 128).astype(F32).T
+def unfold_kernel(
+    f_ref, o_ref, g_ref, few_ref, qkv_ref, out_ref, gate_ref, up_ref, down_ref, router_ref, gain_ref
+):
+    router_ref[...] = few_ref[:8]
+    gain_ref[...] = few_ref[8:9]
+    for i in range(3):
+        part = f_ref[:, :, 64 * i : 64 * (i + 1)].reshape(1024, 128)
+        qkv_ref[:, 1024 * i : 1024 * (i + 1)] = part.T.astype(F32)
     for i in range(4):
         for h in range(2):
             part = o_ref[i, :, 32 * h : 32 * (h + 1)].reshape(128, 128)
@@ -1319,7 +1337,7 @@
     down_ref[...] = g_ref[2].astype(F32)
 
 
-def unfold(full, blocks):
+def unfold(full, blocks, few):
     shape = jax.ShapeDtypeStruct
     share = pl.BlockSpec((None, FFB, 128), lambda i, j: (i, 0, j))
     return pl.pallas_call(
@@ -1328,20 +1346,25 @@
             shape((1024, 3072), F32),
             shape((1024, 1024), F32),
             *[shape((4, FFB, DB), F32)] * 3,
+            shape((8, 1024), F32),
+            shape((1, 1024), F32),
         ),
         grid=(4, 2),
         in_specs=[
-            pl.BlockSpec((3, None, None, 4, 4, 64, 128), lambda i, j: (0, j, i, 0, 0, 0, 0)),
-            pl.BlockSpec((None, None, 4, None, 4, 64, 128), lambda i, j: (3, j, 0, i, 0, 0, 0)),
+            pl.BlockSpec((None, None, 4, 4, 192, 128), lambda i, j: (j, i, 0, 0, 0, 0)),
+            pl.BlockSpec((None, 4, None, 4, 64, 128), lambda i, j: (j, 0, i, 0, 3, 0)),
             pl.BlockSpec((None, 3, FFB, 128), lambda i, j: (i, 0, 0, j)),
+            pl.BlockSpec((16, 1024), lambda i, j: (0, 0)),
         ],
         out_specs=(
             pl.BlockSpec((128, 3072), lambda i, j: (2 * i + j, 0)),
             pl.BlockSpec((128, 1024), lambda i, j: (4 * j + i, 0)),
             *[share] * 3,
+            pl.BlockSpec((8, 1024), lambda i, j: (0, 0)),
+            pl.BlockSpec((1, 1024), lambda i, j: (0, 0)),
         ),
         compiler_params=pltpu.CompilerParams(vmem_limit_bytes=48 * 1024 * 1024),
-    )(full, full, blocks)
+    )(full, full, blocks, few)
 
 
 def body(
@@ -1367,7 +1390,6 @@
         qkv,
         ctx_here,
         lse,
-        down,
         near,
         weights,
         qkv_low,
@@ -1385,7 +1407,7 @@
         qkv_weight,
         out_weight,
     )
-    block_output, input_grad, gain_grad, mine, few, full, _, _ = experts_back(
+    block_output, input_grad, gain_grad, mine, few, full, _ = experts_back(
         middle,
         probs,
         pairs,
@@ -1398,22 +1420,23 @@
         lse,
         block_input,
         attn_gain.reshape(1, -1),
-        down,
         send,
         weights,
         near,
         qkv_low,
         out_low,
     )
-    qkv_grad, out_grad, gate_grad, up_grad, down_grad = unfold(full, mine)
+    qkv_grad, out_grad, gate_grad, up_grad, down_grad, router_grad, moe_gain_grad = unfold(
+        full, mine, few
+    )
     return (
         block_output,
         input_grad,
         gain_grad.reshape(-1),
         qkv_grad,
         out_grad,
-        few[8],
-        few[:8].T,
+        moe_gain_grad.reshape(-1),
+        router_grad.T,
         jnp.swapaxes(gate_grad, 1, 2),
         jnp.swapaxes(up_grad, 1, 2),
         down_grad,

time: 258 us -> 248 us (0.961)
  Pallas kernels: 249 us -> 241 us
    pallas_call x1, Pallas kernels: 181 us -> 165 us  [experts_back(): pl.pallas_call(experts_back_kernel, out_shape=(shape((128, 1024), BF16),...]
    pallas_call x1, Pallas kernels: 56.7 us -> 64.7 us  [attend(): pl.pallas_call(attend_kernel, out_shape=(shape((8, 2 * ROWS, 1024), BF16)...]
where the time goes in v5:
time: 248 us; the launch traced here: 247 us
  Pallas kernels  241 us (97%)
  local copies, waits for them, and re-layouts  4.25 us (2%)
    pallas_call x1, Pallas kernels, experts_back(): pl.pallas_call(experts_back_kernel, out_shape=(shape((128, 1024), BF16),...  165 us
    pallas_call x1, Pallas kernels, attend(): pl.pallas_call(attend_kernel, out_shape=(shape((8, 2 * ROWS, 1024), BF16)...  64.7 us
    pallas_call x1, Pallas kernels, unfold(): pl.pallas_call(unfold_kernel, out_shape=(shape((1024, 3072), F32), shape(...  11.1 us

profile of v5, /device:TPU:1, one launch (start us, length us, event | category | flops | bytes accessed | tf_op | source)
XLA Modules:
  0.0 247.3 jit_solution(4499240923798507095)
XLA Ops:
  0.7 0.1 pad.2.clone
  0.7 1.4 add_convert_fusion.pairs_ref
  2.1 64.7 %shard_map.195 = (bf16[8,80,1024]{2,1,0:T(8,128)(2,1)}, f32[128,1024]{1,0:T(8,128)}, f32[128,8]{1,0:T(8,128)}, bf16[1024,128]{1,0:T(8,128)(2,1)}, bf16[3,64,2048...) custom-call(bf16[128,1024]{1,0:T(8,128)(2,1)} %x_ref.3, ...), custom_call_target="tpu_custom_call" | custom-call | tf_op jit(solution)/shard_map/pallas_call | solution.py:464
  66.8 165.2 %shard_map.196 = (bf16[128,1024]{1,0:T(8,128)(2,1)}, f32[128,1024]{1,0:T(8,128)}, f32[1,1024]{1,0:T(1,128)}, bf16[4,3,176,256]{3,2,1,0:T(8,128)(2,1)}, f32[16,10...) custom-call(f32[128,1024]{1,0:T(8,128)} %get-tuple-element.34.mid_ref, ...), custom_call_target="tpu_custom_call" | custom-call | tf_op jit(solution)/shard_map/pallas_call | solution.py:1249
  232.0 0.0 copy-start
  232.0 1.2 copy-done
  233.2 0.0 copy-start.1
  233.2 0.8 copy-done.1
  234.1 0.0 copy-start.3
  234.1 0.0 copy-start.2
  234.1 0.0 copy-start.4
  234.1 11.1 %shard_map.197 = (f32[1024,3072]{1,0:T(8,128)}, f32[1024,1024]{1,0:T(8,128)}, f32[4,176,256]{2,1,0:T(8,128)}, f32[4,176,256]{2,1,0:T(8,128)}, f32[4,176,256]{2,1...) custom-call(bf16[2,4,4,4,256,128]{5,4,3,2,1,0:T(8,128)(2,1)} %get-tuple-element.48.f_ref.o_ref, ...), custom_call_target="tpu_custom_call" | custom-call | tf_op jit(solution)/shard_map/pallas_call | solution.py:1343
  245.2 0.0 copy-done.3
  245.2 0.7 copy.25
  245.9 0.0 copy-done.2
  245.9 0.8 copy.26
  246.7 0.0 copy-done.4
  246.7 0.6 copy.27
  (1 shorter events, 0.0 us)
Async XLA Ops:
  232.0 1.2 copy-start
  233.2 0.8 copy-start.1
  234.1 11.1 %copy-start.3 = (bf16[128,1024]{1,0:T(8,128)(2,1)S(1)}, bf16[128,1024]{1,0:T(8,128)(2,1)}, u32[]{:S(2)}) copy-start(bf16[128,1024]{1,0:T(8,128)(2,1)} %get-tuple-element.68) | copy-start | bytes 786436
  234.1 11.9 %copy-start.2 = (f32[128,1024]{1,0:T(8,128)S(1)}, f32[128,1024]{1,0:T(8,128)}, u32[]{:S(2)}) copy-start(f32[128,1024]{1,0:T(8,128)} %get-tuple-element.69) | copy-start | bytes 1572868
  234.1 12.6 %copy-start.4 = (f32[1,1024]{1,0:T(1,128)S(1)}, f32[1,1024]{1,0:T(1,128)}, u32[]{:S(2)}) copy-start(f32[1,1024]{1,0:T(1,128)} %get-tuple-element.47) | copy-start | bytes 12292

commit v6 on v5

--- a/solution.py
+++ b/solution.py
@@ -64,6 +64,10 @@
     )
 
 
+def tally(ref, send, recv):
+    return push(ref, ref, send, recv, {"expert": 1 - lax.axis_index("expert")})
+
+
 def lanes(at, size):
     return pl.ds(pl.multiple_of(at * size, size), size)
 
@@ -112,6 +116,18 @@
     cot_ref,
     wq_hbm,
     wo_hbm,
+    send_out,
+    mid_out,
+    probs_out,
+    ctx_out_ref,
+    qkv_out,
+    ctx_here_out,
+    lse_out,
+    down_out,
+    nall_ref,
+    w_out_ref,
+    wq_out_ref,
+    wo_out_ref,
     send_ref,
     mid_ref,
     probs_ref,
@@ -119,10 +135,7 @@
     qkv_ref,
     ctx_here_ref,
     lse_ref,
-    nall_ref,
-    w_out_ref,
-    wq_out_ref,
-    wo_out_ref,
+    down_ref,
     wq_wide,
     wo_wide,
     wq_ref,
@@ -258,17 +271,8 @@
         return push(
             heads.at[:, t],
             qkv_ref.at[:, :, lanes(m, 128)],
-            a_send.at[k],
-            a_recv.at[k],
-            mp_at(m, k),
-        )
-
-    def head_in(k):
-        return push(
-            heads.at[:, 0],
-            qkv_ref.at[:, :, lanes((m + 16 - k) % 16, 128)],
-            a_send.at[k],
-            a_recv.at[k],
+            a_send.at[0],
+            a_recv.at[0],
             mp_at(m, k),
         )
 
@@ -321,7 +325,8 @@
     save_o.start()
 
     own.wait()
-    each(1, 16, lambda k: head_in(k).wait_recv())
+    some = qkv_ref.at[:, :, pl.ds(0, 15 * 128)]
+    tally(some, a_send.at[0], a_recv.at[0]).wait_recv()
 
     key_rows[...] = qkv_ref[1].astype(F32).T.astype(BF16)
 
@@ -329,19 +334,9 @@
         return push(
             ctx_low.at[:, lanes(t, 128)],
             ctx_ref.at[pl.ds(pl.multiple_of(m * 64, 64), 64), :],
-            c_send.at[(t + 16 - m) % 16],
-            c_recv.at[(t + 16 - m) % 16],
+            c_send.at[0],
+            c_recv.at[0],
             {"mp": t},
-        )
-
-    def ctx_in(k):
-        s = (m + 16 - k) % 16
-        return push(
-            ctx_low.at[:, pl.ds(0, 128)],
-            ctx_ref.at[pl.ds(pl.multiple_of(s * 64, 64), 64), :],
-            c_send.at[k],
-            c_recv.at[k],
-            {"mp": s},
         )
 
     def queries(i):
@@ -380,8 +375,7 @@
             fan_wait(0, 0)
             fan_start(0, 1)
             blocks_in(2)
-            fan_start(2, 0)
-            fan_own(2).start()
+            down_ref[...] = stage[2]
 
         return carry
 
@@ -394,7 +388,8 @@
         far(0, d, m).start()
         far(1, d, m).start()
     ctx_ref[pl.ds(pl.multiple_of(m * 64, 64), 64), :] = ctx_low[:, lanes(m, 128)]
-    each(1, 16, lambda k: ctx_in(k).wait_recv())
+    lot = ctx_ref.at[pl.ds(0, 15 * 64)]
+    tally(lot, c_send.at[0], c_recv.at[0]).wait_recv()
 
     fan_wait(1, 0)
     fan_start(1, 1)
@@ -415,15 +410,27 @@
     hot = jnp.concatenate([h.astype(F32) for h in hot], axis=1).astype(BF16)
     sent = dot(hot, jnp.concatenate(rows, axis=0))
     send_ref[...] = sent.astype(BF16).reshape(8, 2 * ROWS, 1024)
+    results = (
+        (send_ref, send_out),
+        (mid_ref, mid_out),
+        (probs_ref, probs_out),
+        (ctx_ref, ctx_out_ref),
+        (qkv_ref, qkv_out),
+        (ctx_here_ref, ctx_here_out),
+        (lse_ref, lse_out),
+        (down_ref, down_out),
+    )
+    results = [
+        pltpu.make_async_copy(src, dst, here.at[11 + i]) for i, (src, dst) in enumerate(results)
+    ]
+    for copy in results:
+        copy.start()
 
     for i in range(6):
         save(i).wait()
     save_o.wait()
     fan_wait(0, 1)
-    fan_wait(2, 0)
-    fan_start(2, 1)
     fan_wait(1, 1)
-    fan_wait(2, 1)
     for d in (1, 3):
         far(0, d, z_from[d]).wait_recv()
         far(1, d, y_from[d]).wait_recv()
@@ -433,15 +440,17 @@
     for d in (1, 3):
         far(0, d, m).wait_send()
         far(1, d, m).wait_send()
-    for i in range(3):
+    for i in range(2):
         fan_own(i).wait()
         for d in (1, 3):
             for step in range(2):
                 fan(i, d, step, x).wait_send()
-    each(1, 16, lambda k: head_out(k).wait_send())
-    each(1, 16, lambda k: ctx_in(k).wait_send())
+    tally(some, a_send.at[0], a_recv.at[0]).wait_send()
+    tally(lot, c_send.at[0], c_recv.at[0]).wait_send()
     for i in range(3):
         each_block(lambda el, i=i: block(i, el, y).wait_send())
+    for copy in results:
+        copy.wait()
 
 
 def attend(
@@ -471,14 +480,23 @@
             shape((3, 64, 2048), BF16),
             shape((64, 2048), F32),
             shape((1, 2048), F32),
+            shape((FFQ, DB), BF16),
             shape((4, 4, 128, 1024), BF16),
-            shape((3, FFQ, 4 * DB), BF16),
+            shape((2, FFQ, 4 * DB), BF16),
             shape((1024, 3072), BF16),
             shape((1024, 1024), BF16),
         ),
         in_specs=[vm] * 9 + [hbm] * 2,
-        out_specs=(vm,) * 7 + (hbm,) * 4,
+        out_specs=(hbm,) * 12,
         scratch_shapes=[
+            VMEM((8, 2 * ROWS, 1024), BF16),
+            VMEM((128, 1024), F32),
+            VMEM((128, 8), F32),
+            VMEM((1024, 128), BF16),
+            VMEM((3, 64, 2048), BF16),
+            VMEM((64, 2048), F32),
+            VMEM((1, 2048), F32),
+            VMEM((FFQ, DB), BF16),
             VMEM((1024, 3072), F32),
             VMEM((1024, 1024), F32),
             VMEM((1024, 3072), BF16),
@@ -489,17 +507,17 @@
             VMEM((3, FFQ, DB), BF16),
             VMEM((2048, 64), BF16),
             VMEM((64, 2048), BF16),
-            dma((11,)),
+            dma((19,)),
             dma((3, 4)),
             dma((3, 4)),
-            dma((3, 2, 4)),
-            dma((3, 2, 4)),
-            dma((16,)),
-            dma((16,)),
             dma((2, 2, 4)),
             dma((2, 2, 4)),
-            dma((16,)),
-            dma((16,)),
+            dma((1,)),
+            dma((1,)),
+            dma((2, 2, 4)),
+            dma((2, 2, 4)),
+            dma((1,)),
+            dma((1,)),
         ],
         compiler_params=params(1, 62),
     )(
@@ -522,6 +540,31 @@
 
 
 def experts_back_kernel(
+    mid_hbm,
+    probs_hbm,
+    pairs_hbm,
+    cot_hbm,
+    moe_gain_hbm,
+    router_hbm,
+    tok_hbm,
+    qkv_hbm,
+    ctx_hbm,
+    lse_hbm,
+    x_hbm,
+    gain_hbm,
+    down_hbm,
+    send_hbm,
+    w_hbm,
+    near_hbm,
+    wq_hbm,
+    wo_hbm,
+    y_ref,
+    in_ref,
+    gain_out_ref,
+    g_out_ref,
+    few_out_ref,
+    full_out,
+    ret_ref,
     mid_ref,
     probs_ref,
     pairs_ref,
@@ -534,18 +577,8 @@
     lse_ref,
     x_ref,
     gain_ref,
-    send_hbm,
-    w_hbm,
-    near_hbm,
-    wq_hbm,
-    wo_hbm,
-    y_ref,
-    in_ref,
-    gain_out_ref,
-    g_out_ref,
-    few_out_ref,
+    down_ref,
     full_ref,
-    ret_ref,
     nall_ref,
     weights,
     recv,
@@ -582,6 +615,7 @@
     gain_mp,
     gain_rest,
     here,
+    leave,
     d_send,
     d_recv,
     f_send,
@@ -590,6 +624,8 @@
     p_recv,
     r_send,
     r_recv,
+    w_send,
+    w_recv,
     x_send,
     x_recv,
     s_send,
@@ -657,7 +693,29 @@
 
     for r in range(1, 8):
         pl.semaphore_signal(barrier, inc=1, device_id=rest(r), device_id_type=MESH)
-    load_w = [local(w_hbm.at[i], weights.at[pl.ds(i * FFQ, FFQ)], i) for i in range(3)]
+    operands = [
+        local(src, dst, 14 + i)
+        for i, (src, dst) in enumerate(
+            (
+                (down_hbm, down_ref),
+                (mid_hbm, mid_ref),
+                (probs_hbm, probs_ref),
+                (pairs_hbm, pairs_ref),
+                (cot_hbm, cot_ref),
+                (moe_gain_hbm, moe_gain_ref),
+                (router_hbm, router_ref),
+                (tok_hbm, tok_ref),
+                (qkv_hbm, qkv_ref),
+                (ctx_hbm, ctx_ref),
+                (lse_hbm, lse_ref),
+                (x_hbm, x_ref),
+                (gain_hbm, gain_ref),
+            )
+        )
+    ]
+    for copy in operands:
+        copy.start()
+    load_w = [local(w_hbm.at[i], weights.at[pl.ds(i * FFQ, FFQ)], i) for i in range(2)]
     for copy in load_w:
         copy.start()
     near = []
@@ -681,13 +739,15 @@
         return push(
             send_hbm.at[expert_of(t)],
             recv.at[slot(0, k)],
-            d_send.at[k],
+            d_send.at[0],
             d_recv.at[k],
             {"mp": t},
         )
 
     def forward(k):
-        return push(recv.at[slot(0, k)], recv.at[slot(1, k)], f_send.at[k], f_recv.at[k], twin)
+        return push(
+            recv.at[slot(0, k)], recv.at[slot(1, k)], f_send.at[0], f_recv.at[k // 4], twin
+        )
 
     def partials(j):
         return push(
@@ -703,12 +763,28 @@
 
     def giving(k, at):
         return push(
-            back.at[spot_of(k)], ret_ref.at[at], r_send.at[k], r_recv.at[k], mp_at(m, 16 - k)
-        )
-
+            back.at[spot_of(k)], ret_ref.at[at], r_send.at[0], r_recv.at[0], mp_at(m, 16 - k)
+        )
+
+    def down_fan(d, step, at):
+        part = pl.ds(0, FFQ) if step == 0 else pl.ds(0 if d == 1 else FFQ // 2, FFQ // 2)
+        units = pl.ds(2 * FFQ + part.start, part.size)
+        there = weights.at[units, lanes(at, DB)]
+        return push(
+            down_ref if step == 0 else there,
+            there,
+            w_send.at[step, d // 2],
+            w_recv.at[step, d // 2],
+            {"dp": (x + d) % 4},
+        )
+
+    operands[0].wait()
+    for d in (1, 3):
+        down_fan(d, 0, x).start()
     each(1, 16, lambda k: dispatch(k).start())
     own = local(send_hbm.at[expert_of(m)], recv.at[slot(0, 0)], 4)
     own.start()
+    weights[2 * FFQ :, lanes(x, DB)] = down_ref[...]
     own.wait()
 
     def finish(j):
@@ -747,9 +823,10 @@
         def _():
             for copy in load_w:
                 copy.wait()
-
-        for i in range(4):
-            forward(4 * j + i).wait_recv()
+            for d in (1, 3):
+                down_fan(d, 1, (x + 2) % 4).wait_recv()
+
+        tally(recv.at[slot(1, 4 * j, 4)], f_send.at[0], f_recv.at[j]).wait_recv()
         xs = pl.ds(pl.multiple_of(j * 8 * ROWS, 16), 8 * ROWS)
         cs = pl.ds(pl.multiple_of(cot_rows + j * 8 * ROWS, 16), 8 * ROWS)
         for r in range(2):
@@ -783,9 +860,15 @@
         partials(j).start()
         return carry
 
+    for d in (1, 3):
+        down_fan(d, 0, (x + 4 - d) % 4).wait_recv()
+        down_fan(d, 1, (x + 4 - d) % 4).start()
     lax.fori_loop(0, 4, chunk, 0)
     finish(3)
-    each(0, 16, lambda k: forward(k).wait_send())
+    tally(recv.at[slot(0, 0, 16)], f_send.at[0], f_recv.at[0]).wait_send()
+    for d in (1, 3):
+        down_fan(d, 0, x).wait_send()
+        down_fan(d, 1, x).wait_send()
     load_o = local(wo_hbm, weights.at[pl.ds(0, 1024)], 0)
     load_o.start()
 
@@ -798,8 +881,8 @@
         return push(
             recv.at[unit_rows(i, d), lanes((x + 2) % 4, DB)],
             g_relay.at[d // 2, i],
-            x_send.at[0, i, d],
-            x_recv.at[0, i, d],
+            x_send.at[0, i, d // 2],
+            x_recv.at[0, i, d // 2],
             {"dp": (x + d) % 4},
         )
 
@@ -807,8 +890,8 @@
         return push(
             recv.at[pl.ds(i * FFQ, FFQ), lanes((x + d) % 4, DB)],
             g_near.at[d // 2, i],
-            x_send.at[1, i, d],
-            x_recv.at[1, i, d],
+            x_send.at[1, i, d // 2],
+            x_recv.at[1, i, d // 2],
             {"dp": (x + d) % 4},
         )
 
@@ -866,12 +949,13 @@
             kept.wait()
 
     local(back.at[spot_of(0)], ret_ref.at[m], 4).wait()
-    each(1, 16, lambda k: giving(k, (m + k) % 16).wait())
+    tally(back.at[spot_of(1, 15)], r_send.at[0], r_recv.at[0]).wait_send()
+    tally(ret_ref.at[pl.ds(0, 15)], r_send.at[0], r_recv.at[0]).wait_recv()
     load_r = local(ret_ref, back.reshape(16, size, 4 * DB), 4)
     load_r.start()
     load_r.wait()
 
-    for copy in near:
+    for copy in (*near, *operands[1:]):
         copy.wait()
 
     def far(part, d, hops):
@@ -880,7 +964,7 @@
             ref, device = nall_ref.at[(z + 8 - hops * d) % 4, some, :, cols], z_at(z, y, d)
         else:
             ref, device = nall_ref.at[some, (y + 8 - hops * d) % 4, :, cols], y_at(z, y, d)
-        return push(ref, ref, n_send.at[part, d], n_recv.at[part, d], device)
+        return push(ref, ref, n_send.at[part, d // 2], n_recv.at[part, d // 2], device)
 
     columns = pairs_ref[...].T
     hot = picks(columns)
@@ -914,11 +998,7 @@
 
     def cot_out(k):
         t = (m + k) % 16
-        return push(dctx.at[t], cot.at[:, lanes(m, 128)], a_send.at[k], a_recv.at[k], {"mp": t})
-
-    def cot_in(k):
-        s = (m + 16 - k) % 16
-        return push(dctx.at[0], cot.at[:, lanes(s, 128)], a_send.at[k], a_recv.at[k], {"mp": s})
+        return push(dctx.at[t], cot.at[:, lanes(m, 128)], a_send.at[0], a_recv.at[0], {"mp": t})
 
     each(1, 16, lambda k: cot_out(k).start())
     for d in (1, 3):
@@ -935,7 +1015,7 @@
     def quarters(d):
         t = (x + d) % 4
         return push(
-            weights.at[pl.ds(0, 512), lanes(t, DB)], o_x.at[d - 1], ox_send.at[d], ox_recv.at[d], {"dp": t}
+            weights.at[pl.ds(0, 512), lanes(t, DB)], o_x.at[d - 1], ox_send.at[0], ox_recv.at[0], {"dp": t}
         )
 
     def thirty(k):
@@ -943,24 +1023,24 @@
         return push(
             o_q.at[pl.ds(pl.multiple_of(t * 32, 32), 32)],
             o_mp.at[k],
-            om_send.at[k],
-            om_recv.at[k],
+            om_send.at[0],
+            om_recv.at[0],
             {"mp": t},
         )
 
     def few_share(r):
         t = 2 * ((x + r % 4) % 4) + (c + r // 4) % 2
         return push(
-            few.at[:, lanes(t, 128)], few_rest.at[r], fr_send.at[0, r], fr_recv.at[0, r], rest(r)
+            few.at[:, lanes(t, 128)], few_rest.at[r], fr_send.at[0], fr_recv.at[0], rest(r)
         )
 
     def few_near(k):
-        return push(few_sum, few_mp.at[k], fm_send.at[k], fm_recv.at[k], mp_at(m, k))
+        return push(few_sum, few_mp.at[k], fm_send.at[0], fm_recv.at[0], mp_at(m, k))
 
     def few_back(r, back_from):
         t = 2 * ((x + 4 - r % 4) % 4) + (c + r // 4) % 2 if back_from else 2 * x + c
         return push(
-            few_done, few_out_ref.at[:, lanes(t, 128)], fr_send.at[1, r], fr_recv.at[1, r], rest(r)
+            few_done, few_out_ref.at[:, lanes(t, 128)], fr_send.at[1], fr_recv.at[1], rest(r)
         )
 
     halves().start()
@@ -987,8 +1067,8 @@
         return push(
             full_ref.at[(c, *src, spans[p])],
             full_ref.at[(c, *at, spans[p])],
-            g_send.at[p, s, d],
-            g_recv.at[p, s, d],
+            g_send.at[p, s],
+            g_recv.at[p, s],
             along(axis, d),
         )
 
@@ -1007,19 +1087,34 @@
         if step:
             at[orders[p][0]] = pl.ds(0 if d == 1 else 2, 2)
         ref = full_ref.at[(c, *at, spans[p])]
-        return push(ref, ref, g_send.at[p, 2 + step, d], g_recv.at[p, 2 + step, d], along(orders[p][2], d))
+        return push(ref, ref, g_send.at[p, 2 + step], g_recv.at[p, 2 + 2 * step + d // 2], along(orders[p][2], d))
+
+    def blocks_of(p, s):
+        at = ((0, 0, pl.ds(0, 3)), (0, pl.ds(0, 3), slice(None)), (pl.ds(0, 2),), (pl.ds(0, 1),))[s]
+        at = (*at, *[slice(None)] * (3 - len(at)))
+        return full_ref.at[(c, *at, spans[p])]
 
     def spread_wait(p, s):
-        for d in (1, 2, 3):
-            spread(p, s, d, True).wait_recv()
-
-    def share_twin(p, i, core):
+        tally(blocks_of(p, s), g_send.at[p, s], g_recv.at[p, s]).wait_recv()
+
+    def piece(p, i, core):
         d, hops = ((1, 0), (1, 1), (3, 1), (1, 2), (3, 2))[i]
         at = last(p, d, hops)
         if hops == 2:
             at[orders[p][0]] = pl.ds(0 if d == 1 else 2, 2)
-        ref = full_ref.at[(core, *at, spans[p])]
-        return push(ref, ref, t_send.at[p, i], t_recv.at[p, i], twin)
+        return (core, *at, spans[p])
+
+    def share_twin(p, i, core):
+        ref = full_ref.at[piece(p, i, core)]
+        return push(ref, ref, t_send.at[0], t_recv.at[p, i], twin)
+
+    def write(p, i, other):
+        at = piece(p, i, 1 - c if other else c)
+        return pltpu.make_async_copy(full_ref.at[at], full_out.at[at], leave.at[other])
+
+    def hand_on(p, i):
+        share_twin(p, i, c).start()
+        write(p, i, 0).start()
 
     key_values[...] = qkv_ref[1:].reshape(128, 2048).astype(F32).T.astype(BF16)
     dkv[...] = jnp.zeros_like(dkv)
@@ -1030,7 +1125,8 @@
     for d in (2, 1, 3):
         quarters(d).start()
     go_home(0)
-    each(1, 16, lambda k: cot_in(k).wait_recv())
+    cots = cot.at[:, pl.ds(0, 15 * 128)]
+    tally(cots, a_send.at[0], a_recv.at[0]).wait_recv()
     row_dot[...] = jnp.sum(cot[...].astype(F32) * ctx_ref[...], axis=0, keepdims=True)
 
     def queries(b):
@@ -1055,16 +1151,9 @@
 
         @pl.when(i == 2)
         def _():
-            for d in (1, 2, 3):
-                quarters(d).wait_recv()
-            o_sum = weights[:512, lanes(x, DB)].astype(F32)
-            for d in (1, 2, 3):
-                o_sum += o_x[d - 1].astype(F32)
-            o_q[...] = o_sum.astype(BF16)
-            each(1, 16, lambda k: thirty(k).start())
             few_all = few[:, lanes(2 * x + c, 128)]
+            tally(few_rest.at[pl.ds(1, 7)], fr_send.at[0], fr_recv.at[0]).wait_recv()
             for r in range(1, 8):
-                few_share(r).wait_recv()
                 few_all += few_rest[r]
             few_sum[...] = few_all
             each(1, 16, lambda k: few_near(k).start())
@@ -1078,17 +1167,8 @@
     def pc_out(k):
         t = (m + k) % 16
         return push(
-            pc_here.at[:, :, lanes(t, 128)], pc_tok.at[:, m], b_send.at[k], b_recv.at[k], {"mp": t}
-        )
-
-    def pc_in(k):
-        s = (m + 16 - k) % 16
-        return push(
-            pc_here.at[:, :, pl.ds(0, 128)], pc_tok.at[:, s], b_send.at[k], b_recv.at[k], {"mp": s}
-        )
-
-    each(1, 16, lambda k: pc_out(k).start())
-    pc_tok[:, m] = pc_here[:, :, lanes(m, 128)]
+            pc_here.at[:, :, lanes(t, 128)], pc_tok.at[:, m], b_send.at[0], b_recv.at[0], {"mp": t}
+        )
 
     for d in (1, 3):
         far(0, d, 2).wait_recv()
@@ -1098,13 +1178,22 @@
 
     def share_out(r):
         t = 2 * ((x + r % 4) % 4) + (c + r // 4) % 2
-        return push(slices.at[:, lanes(t, 128)], parts.at[r], q_send.at[r], q_recv.at[r], rest(r))
+        return push(slices.at[:, lanes(t, 128)], parts.at[r], q_send.at[0], q_recv.at[0], rest(r))
 
     for r in range(1, 8):
         share_out(r).start()
+    each(1, 16, lambda k: pc_out(k).start())
+    pc_tok[:, m] = pc_here[:, :, lanes(m, 128)]
+
+    tally(o_x, ox_send.at[0], ox_recv.at[0]).wait_recv()
+    o_sum = weights[:512, lanes(x, DB)].astype(F32)
+    for d in (1, 2, 3):
+        o_sum += o_x[d - 1].astype(F32)
+    o_q[...] = o_sum.astype(BF16)
+    each(1, 16, lambda k: thirty(k).start())
     whole = slices[:, lanes(2 * x + c, 128)].astype(F32)
-    for r in range(1, 8):
-        share_out(r).wait_recv()
+    seven = parts.at[pl.ds(1, 7)]
+    tally(seven, q_send.at[0], q_recv.at[0]).wait_recv()
     for r in range(1, 8):
         whole += parts[r].astype(F32)
     share[:192] = whole.astype(BF16)
@@ -1113,7 +1202,17 @@
     lay.wait()
     for p in range(3):
         spread_start(p, 0)
-    each(1, 16, lambda k: thirty(k).wait_recv())
+    def circles(p):
+        spread_wait(p, 1)
+        for d in (1, 3):
+            circle(p, d, 0, 0).start()
+        hand_on(p, 0)
+
+    for p in range(3):
+        spread_wait(p, 0)
+        spread_start(p, 1)
+    fifteen = o_mp.at[pl.ds(1, 15)]
+    tally(fifteen, om_send.at[0], om_recv.at[0]).wait_recv()
     o_sum = o_q[pl.ds(pl.multiple_of(m * 32, 32), 32)].astype(F32)
     for k in range(1, 16):
         o_sum += o_mp[k].astype(F32)
@@ -1126,22 +1225,14 @@
     for p in (3, 4):
         spread_start(p, 0)
 
-    def circles(p):
-        spread_wait(p, 1)
-        for d in (1, 3):
-            circle(p, d, 0, 0).start()
-        share_twin(p, 0, c).start()
-
-    for p in range(3):
-        spread_wait(p, 0)
-        spread_start(p, 1)
     for p in range(3):
         circles(p)
     for p in (3, 4):
         spread_wait(p, 0)
         spread_start(p, 1)
 
-    each(1, 16, lambda k: pc_in(k).wait_recv())
+    packs = pc_here.at[:, :, pl.ds(0, 15 * 128)]
+    tally(packs, b_send.at[0], b_recv.at[0]).wait_recv()
     for copy in load_q:
         copy.wait()
     dn = sum(dot(rows[i * 1024 : (i + 1) * 1024], pc_tok[i].reshape(1024, 128)) for i in range(3)).T
@@ -1153,10 +1244,10 @@
     gain_row[...] = jnp.sum(dn * hat, axis=0, keepdims=True)
 
     def gain_out(k):
-        return push(gain_row, gain_mp.at[k], u_send.at[k], u_recv.at[k], mp_at(m, k))
+        return push(gain_row, gain_mp.at[k], u_send.at[0], u_recv.at[0], mp_at(m, k))
 
     def gain_far(r):
-        return push(gain_mp.at[0], gain_rest.at[r], v_send.at[r], v_recv.at[r], rest(r))
+        return push(gain_mp.at[0], gain_rest.at[r], v_send.at[0], v_recv.at[0], rest(r))
 
     each(1, 16, lambda k: gain_out(k).start())
     for p in (3, 4):
@@ -1166,11 +1257,12 @@
         for i, d in ((1, 1), (2, 3)):
             circle(p, d, 0, 1).wait_recv()
             circle(p, d, 1, 0).start()
-            share_twin(p, i, c).start()
+            hand_on(p, i)
 
     for p in range(3):
         onward(p)
-    each(1, 16, lambda k: gain_out(k).wait_recv())
+    gains = gain_mp.at[pl.ds(1, 15)]
+    tally(gains, u_send.at[0], u_recv.at[0]).wait_recv()
     got = gain_row[...]
     for k in range(1, 16):
         got += gain_mp[k]
@@ -1179,7 +1271,8 @@
         gain_far(r).start()
     for p in (3, 4):
         onward(p)
-    each(1, 16, lambda k: few_near(k).wait_recv())
+    fews = few_mp.at[pl.ds(1, 15)]
+    tally(fews, fm_send.at[0], fm_recv.at[0]).wait_recv()
     few_all = few_sum[...]
     for k in range(1, 16):
         few_all += few_mp[k]
@@ -1190,51 +1283,47 @@
     for p in range(5):
         for i, d in ((3, 1), (4, 3)):
             circle(p, d, 1, 1).wait_recv()
-            share_twin(p, i, c).start()
-    for r in range(1, 8):
-        gain_far(r).wait_recv()
+            hand_on(p, i)
+    rests = gain_rest.at[pl.ds(1, 7)]
+    tally(rests, v_send.at[0], v_recv.at[0]).wait_recv()
     for r in range(1, 8):
         got += gain_rest[r]
     gain_out_ref[...] = got
     for i in range(3):
         each_home(lambda at, i=i: home(i, at, at).wait_recv())
-    for r in range(1, 8):
-        few_back(r, True).wait_recv()
+    few_seven = few_rest.at[pl.ds(1, 7)]
+    tally(few_seven, fr_send.at[1], fr_recv.at[1]).wait_recv()
     for p in range(5):
         for i in range(5):
             share_twin(p, i, 1 - c).wait_recv()
-
+            write(p, i, 1).start()
+
+    tally(full_ref.at[c], t_send.at[0], t_recv.at[0, 0]).wait_send()
+    for i in range(2):
+        pltpu.make_async_copy(full_ref.at[i], full_out.at[i], leave.at[i]).wait()
     for p in range(5):
-        for i in range(5):
-            share_twin(p, i, c).wait_send()
-        for d in (1, 2, 3):
-            spread(p, 0, d, False).wait_send()
-            spread(p, 1, d, False).wait_send()
-        for d in (1, 3):
-            circle(p, d, 0, 0).wait_send()
-            circle(p, d, 1, 0).wait_send()
-    each(1, 16, lambda k: dispatch(k).wait_send())
-    each(1, 16, lambda k: cot_out(k).wait_send())
-    each(1, 16, lambda k: pc_out(k).wait_send())
-    each(1, 16, lambda k: gain_out(k).wait_send())
-    each(1, 16, lambda k: thirty(k).wait_send())
-    each(1, 16, lambda k: few_near(k).wait_send())
+        for s in range(4):
+            tally(blocks_of(p, s), g_send.at[p, s], g_recv.at[p, s]).wait_send()
+    tally(recv.at[pl.ds(0, 15 * size)], d_send.at[0], d_recv.at[0]).wait_send()
+    tally(cots, a_send.at[0], a_recv.at[0]).wait_send()
+    tally(packs, b_send.at[0], b_recv.at[0]).wait_send()
+    tally(gains, u_send.at[0], u_recv.at[0]).wait_send()
+    tally(fifteen, om_send.at[0], om_recv.at[0]).wait_send()
+    tally(fews, fm_send.at[0], fm_recv.at[0]).wait_send()
     for j in (2, 3):
         partials(j).wait_send()
     halves().wait_send()
-    for d in (1, 2, 3):
-        quarters(d).wait_send()
+    tally(o_x, ox_send.at[0], ox_recv.at[0]).wait_send()
     for d in (1, 3):
         for i in range(3):
             relay(i, d).wait_send()
             settle(i, d).wait_send()
         far(0, d, 1).wait_send()
         far(1, d, 1).wait_send()
-    for r in range(1, 8):
-        few_share(r).wait_send()
-        few_back(r, False).wait_send()
-        share_out(r).wait_send()
-        gain_far(r).wait_send()
+    tally(few_seven, fr_send.at[0], fr_recv.at[0]).wait_send()
+    tally(few_seven, fr_send.at[1], fr_recv.at[1]).wait_send()
+    tally(seven, q_send.at[0], q_recv.at[0]).wait_send()
+    tally(rests, v_send.at[0], v_recv.at[0]).wait_send()
     for i in range(3):
         each_home(lambda at, i=i: home(i, at, y).wait_send())
 
@@ -1257,9 +1346,23 @@
             shape((2, 4, 4, 4, 256, 128), BF16),
             shape((16, 2 * ROWS, width), BF16),
         ),
-        in_specs=[vm] * 12 + [hbm] * 5,
-        out_specs=(vm,) * 3 + (hbm, vm, vm, hbm),
+        in_specs=[hbm] * 18,
+        out_specs=(vm,) * 3 + (hbm, vm, hbm, hbm),
         scratch_shapes=[
+            VMEM((128, 1024), F32),
+            VMEM((128, 8), F32),
+            VMEM((8, 128), F32),
+            VMEM((128, 1024), BF16),
+            VMEM((1, 1024), F32),
+            VMEM((8, 1024), F32),
+            VMEM((1024, 128), BF16),
+            VMEM((3, 64, 2048), BF16),
+            VMEM((64, 2048), F32),
+            VMEM((1, 2048), F32),
+            VMEM((128, 1024), BF16),
+            VMEM((1, 1024), F32),
+            VMEM((FFQ, DB), BF16),
+            VMEM((2, 4, 4, 4, 256, 128), BF16),
             VMEM((4, 4, 128, 1024), BF16),
             VMEM((3 * FFQ, width), BF16),
             VMEM((64 * ROWS, width), BF16),
@@ -1295,34 +1398,59 @@
             VMEM((1, 1024), F32),
             VMEM((16, 1, 1024), F32),
             VMEM((8, 1, 1024), F32),
-            dma((14,)),
-            *pairs_of(16),
-            *pairs_of(16),
+            dma((27,)),
+            dma((2,)),
+            dma((1,)),
+            dma((16,)),
+            dma((1,)),
+            dma((4,)),
             *pairs_of(4),
-            *pairs_of(16),
-            *pairs_of(2, 3, 4),
+            *pairs_of(1),
+            *pairs_of(2, 2),
+            *pairs_of(2, 3, 2),
             *pairs_of(3, 4),
-            *pairs_of(2, 4),
-            *pairs_of(16),
-            *pairs_of(16),
-            *pairs_of(8),
-            *pairs_of(5, 4, 4),
-            *pairs_of(5, 5),
-            *pairs_of(16),
-            *pairs_of(8),
+            *pairs_of(2, 2),
             *pairs_of(1),
-            *pairs_of(4),
-            *pairs_of(16),
-            *pairs_of(16),
-            *pairs_of(2, 8),
+            *pairs_of(1),
+            *pairs_of(1),
+            dma((5, 4)),
+            dma((5, 6)),
+            dma((1,)),
+            dma((5, 5)),
+            *pairs_of(1),
+            *pairs_of(1),
+            *pairs_of(1),
+            *pairs_of(1),
+            *pairs_of(1),
+            *pairs_of(1),
+            *pairs_of(2),
         ],
         compiler_params=params(2, 63),
     )(*operands)
 
 
 def unfold_kernel(
-    f_ref, o_ref, g_ref, few_ref, qkv_ref, out_ref, gate_ref, up_ref, down_ref, router_ref, gain_ref
+    f_ref,
+    o_ref,
+    g_ref,
+    few_ref,
+    y_ref,
+    in_ref,
+    norm_ref,
+    qkv_ref,
+    out_ref,
+    gate_ref,
+    up_ref,
+    down_ref,
+    router_ref,
+    gain_ref,
+    y_out_ref,
+    in_out_ref,
+    norm_out_ref,
 ):
+    y_out_ref[...] = y_ref[...]
+    in_out_ref[...] = in_ref[...]
+    norm_out_ref[...] = norm_ref[...]
     router_ref[...] = few_ref[:8]
     gain_ref[...] = few_ref[8:9]
     for i in range(3):
@@ -1337,7 +1465,7 @@
     down_ref[...] = g_ref[2].astype(F32)
 
 
-def unfold(full, blocks, few):
+def unfold(full, blocks, few, block_output, input_grad, gain_grad):
     shape = jax.ShapeDtypeStruct
     share = pl.BlockSpec((None, FFB, 128), lambda i, j: (i, 0, j))
     return pl.pallas_call(
@@ -1348,6 +1476,9 @@
             *[shape((4, FFB, DB), F32)] * 3,
             shape((8, 1024), F32),
             shape((1, 1024), F32),
+            shape((128, 1024), BF16),
+            shape((128, 1024), F32),
+            shape((1, 1024), F32),
         ),
         grid=(4, 2),
         in_specs=[
@@ -1355,6 +1486,9 @@
             pl.BlockSpec((None, 4, None, 4, 64, 128), lambda i, j: (j, 0, i, 0, 3, 0)),
             pl.BlockSpec((None, 3, FFB, 128), lambda i, j: (i, 0, 0, j)),
             pl.BlockSpec((16, 1024), lambda i, j: (0, 0)),
+            pl.BlockSpec((16, 1024), lambda i, j: (2 * i + j, 0)),
+            pl.BlockSpec((16, 1024), lambda i, j: (2 * i + j, 0)),
+            pl.BlockSpec((1, 1024), lambda i, j: (0, 0)),
         ],
         out_specs=(
             pl.BlockSpec((128, 3072), lambda i, j: (2 * i + j, 0)),
@@ -1362,9 +1496,12 @@
             *[share] * 3,
             pl.BlockSpec((8, 1024), lambda i, j: (0, 0)),
             pl.BlockSpec((1, 1024), lambda i, j: (0, 0)),
+            pl.BlockSpec((16, 1024), lambda i, j: (2 * i + j, 0)),
+            pl.BlockSpec((16, 1024), lambda i, j: (2 * i + j, 0)),
+            pl.BlockSpec((1, 1024), lambda i, j: (0, 0)),
         ),
-        compiler_params=pltpu.CompilerParams(vmem_limit_bytes=48 * 1024 * 1024),
-    )(full, full, blocks, few)
+        compiler_params=pltpu.CompilerParams(vmem_limit_bytes=62 * 1024 * 1024),
+    )(full, full, blocks, few, block_output, input_grad, gain_grad)
 
 
 def body(
@@ -1390,6 +1527,7 @@
         qkv,
         ctx_here,
         lse,
+        down,
         near,
         weights,
         qkv_low,
@@ -1420,15 +1558,25 @@
         lse,
         block_input,
         attn_gain.reshape(1, -1),
+        down,
         send,
         weights,
         near,
         qkv_low,
         out_low,
     )
-    qkv_grad, out_grad, gate_grad, up_grad, down_grad, router_grad, moe_gain_grad = unfold(
-        full, mine, few
-    )
+    (
+        qkv_grad,
+        out_grad,
+        gate_grad,
+        up_grad,
+        down_grad,
+        router_grad,
+        moe_gain_grad,
+        block_output,
+        input_grad,
+        gain_grad,
+    ) = unfold(full, mine, few, block_output, input_grad, gain_grad)
     return (
         block_output,
         input_grad,

time: 248 us -> 224 us (0.903)
  Pallas kernels: 241 us -> 222 us
  local copies, waits for them, and re-layouts: 4.25 us -> 0.08 us
    pallas_call x1, Pallas kernels: 165 us -> 154 us  [experts_back(): pl.pallas_call(experts_back_kernel, out_shape=(shape((128, 1024), BF16),...]
    pallas_call x1, Pallas kernels: 64.7 us -> 55.4 us  [attend(): pl.pallas_call(attend_kernel, out_shape=(shape((8, 2 * ROWS, 1024), BF16)...]
    unnamed x13 -> x0, local copies, waits for them, and re-layouts: 4.17 us -> none
where the time goes in v6:
time: 224 us
  Pallas kernels  222 us (99%)
    pallas_call x1, Pallas kernels, experts_back(): pl.pallas_call(experts_back_kernel, out_shape=(shape((128, 1024), BF16),...  154 us
    pallas_call x1, Pallas kernels, attend(): pl.pallas_call(attend_kernel, out_shape=(shape((8, 2 * ROWS, 1024), BF16)...  55.4 us
    pallas_call x1, Pallas kernels, unfold(): pl.pallas_call(unfold_kernel, out_shape=(shape((1024, 3072), F32), shape(...  11.8 us

profile of v6, /device:TPU:1, one launch (start us, length us, event | category | flops | bytes accessed | tf_op | source)
XLA Modules:
  0.0 223.8 jit_solution(10911467412368537686)
XLA Ops:
  0.7 0.1 pad.2.clone
  0.7 1.4 add_convert_fusion.pairs_ref.pairs_hbm
  2.1 55.4 %shard_map.195 = (bf16[8,80,1024]{2,1,0:T(8,128)(2,1)}, f32[128,1024]{1,0:T(8,128)}, f32[128,8]{1,0:T(8,128)}, bf16[1024,128]{1,0:T(8,128)(2,1)}, bf16[3,64,2048...) custom-call(bf16[128,1024]{1,0:T(8,128)(2,1)} %x_hbm.1, ...), custom_call_target="tpu_custom_call" | custom-call | tf_op jit(solution)/shard_map/pallas_call | solution.py:473
  57.5 154.4 %shard_map.196 = (bf16[128,1024]{1,0:T(8,128)(2,1)}, f32[128,1024]{1,0:T(8,128)}, f32[1,1024]{1,0:T(1,128)}, bf16[4,3,176,256]{3,2,1,0:T(8,128)(2,1)}, f32[16,10...) custom-call(f32[128,1024]{1,0:T(8,128)} %get-tuple-element.38.mid_hbm, ...), custom_call_target="tpu_custom_call" | custom-call | tf_op jit(solution)/shard_map/pallas_call | solution.py:1338
  211.9 11.8 %shard_map.197 = (f32[1024,3072]{1,0:T(8,128)}, f32[1024,1024]{1,0:T(8,128)}, f32[4,176,256]{2,1,0:T(8,128)}, f32[4,176,256]{2,1,0:T(8,128)}, f32[4,176,256]{2,1...) custom-call(bf16[2,4,4,4,256,128]{5,4,3,2,1,0:T(8,128)(2,1)} %get-tu, ...), custom_call_target="tpu_custom_call" | custom-call | tf_op jit(solution)/shard_map/pallas_call | solution.py:1471
  (1 shorter events, 0.0 us)

commit v7 on v6

--- a/solution.py
+++ b/solution.py
@@ -50,6 +50,14 @@
     return {"mp": (m + k) % 16}
 
 
+def ahead(z, y, k):
+    return ((z + k % 4 + k // 4) % 4) * 4 + (y + k % 4) % 4
+
+
+def behind(z, y, k):
+    return ((z + 8 - k % 4 - k // 4) % 4) * 4 + (y + 4 - k % 4) % 4
+
+
 def y_at(z, y, d):
     return {"mp": z * 4 + (y + d) % 4}
 
@@ -112,11 +120,13 @@
     downs_ref,
     moe_gain_ref,
     router_ref,
-    pairs_ref,
+    routes_ref,
+    slots_ref,
     cot_ref,
     wq_hbm,
     wo_hbm,
     send_out,
+    pairs_out,
     mid_out,
     probs_out,
     ctx_out_ref,
@@ -129,6 +139,7 @@
     wq_out_ref,
     wo_out_ref,
     send_ref,
+    pairs_ref,
     mid_ref,
     probs_ref,
     ctx_ref,
@@ -170,6 +181,9 @@
         return {"expert": pc, "mp": pz * 4 + el}
 
     greet_mp(barrier, m)
+    pairs_ref[0:2] = routes_ref[...].astype(F32)
+    pairs_ref[2:4] = slots_ref[...].astype(F32)
+    pairs_ref[4:8] = jnp.zeros((4, 128), F32)
     for el in range(4):
 
         @pl.when(remote(el))
@@ -267,13 +281,13 @@
         heads[i // 2, (i % 2) * 8 : (i % 2) * 8 + 8] = part.T.astype(BF16).reshape(8, 64, 128)
 
     def head_out(k):
-        t = (m + k) % 16
+        t = ahead(z, y, k)
         return push(
             heads.at[:, t],
             qkv_ref.at[:, :, lanes(m, 128)],
             a_send.at[0],
             a_recv.at[0],
-            mp_at(m, k),
+            {"mp": t},
         )
 
     def each(lo, hi, f):
@@ -412,6 +426,7 @@
     send_ref[...] = sent.astype(BF16).reshape(8, 2 * ROWS, 1024)
     results = (
         (send_ref, send_out),
+        (pairs_ref, pairs_out),
         (mid_ref, mid_out),
         (probs_ref, probs_out),
         (ctx_ref, ctx_out_ref),
@@ -461,7 +476,8 @@
     down_weight,
     moe_gain,
     router,
-    pairs,
+    routes,
+    slots,
     cotangent,
     qkv_weight,
     out_weight,
@@ -474,6 +490,7 @@
         attend_kernel,
         out_shape=(
             shape((8, 2 * ROWS, 1024), BF16),
+            shape((8, 128), F32),
             shape((128, 1024), F32),
             shape((128, 8), F32),
             shape((1024, 128), BF16),
@@ -486,10 +503,11 @@
             shape((1024, 3072), BF16),
             shape((1024, 1024), BF16),
         ),
-        in_specs=[vm] * 9 + [hbm] * 2,
-        out_specs=(hbm,) * 12,
+        in_specs=[vm] * 10 + [hbm] * 2,
+        out_specs=(hbm,) * 13,
         scratch_shapes=[
             VMEM((8, 2 * ROWS, 1024), BF16),
+            VMEM((8, 128), F32),
             VMEM((128, 1024), F32),
             VMEM((128, 8), F32),
             VMEM((1024, 128), BF16),
@@ -507,7 +525,7 @@
             VMEM((3, FFQ, DB), BF16),
             VMEM((2048, 64), BF16),
             VMEM((64, 2048), BF16),
-            dma((19,)),
+            dma((20,)),
             dma((3, 4)),
             dma((3, 4)),
             dma((2, 2, 4)),
@@ -528,7 +546,8 @@
         down_weight,
         moe_gain.reshape(1, -1),
         router.T,
-        pairs,
+        routes.T,
+        slots.T,
         cotangent,
         qkv_weight,
         out_weight,
@@ -735,7 +754,7 @@
         return pl.ds(pl.multiple_of((core * 16 + k) * size, size), n * size)
 
     def dispatch(k):
-        t = (m + k) % 16
+        t = ahead(z, y, k)
         return push(
             send_hbm.at[expert_of(t)],
             recv.at[slot(0, k)],
@@ -763,7 +782,7 @@
 
     def giving(k, at):
         return push(
-            back.at[spot_of(k)], ret_ref.at[at], r_send.at[0], r_recv.at[0], mp_at(m, 16 - k)
+            back.at[spot_of(k)], ret_ref.at[at], r_send.at[0], r_recv.at[0], {"mp": behind(z, y, k)}
         )
 
     def down_fan(d, step, at):
@@ -997,7 +1016,7 @@
     dctx[...] = dot_nt(weights[:1024], branch_cot).astype(BF16).reshape(16, 64, 128)
 
     def cot_out(k):
-        t = (m + k) % 16
+        t = ahead(z, y, k)
         return push(dctx.at[t], cot.at[:, lanes(m, 128)], a_send.at[0], a_recv.at[0], {"mp": t})
 
     each(1, 16, lambda k: cot_out(k).start())
@@ -1019,7 +1038,7 @@
         )
 
     def thirty(k):
-        t = (m + k) % 16
+        t = ahead(z, y, k)
         return push(
             o_q.at[pl.ds(pl.multiple_of(t * 32, 32), 32)],
             o_mp.at[k],
@@ -1052,7 +1071,7 @@
             return {"dp": (x + d) % 4}
         return z_at(z, y, d) if axis == 1 else y_at(z, y, d)
 
-    orders = ((0, 2, 1), (1, 0, 2), (2, 1, 0), (0, 2, 1), (0, 1, 2))
+    orders = ((0, 2, 1), (0, 1, 2), (2, 1, 0), (0, 2, 1), (2, 1, 0))
     spans = [pl.ds(0, 64), pl.ds(64, 64), pl.ds(128, 64), pl.ds(192, 32), pl.ds(224, 32)]
 
     def spread(p, s, d, incoming):
@@ -1165,7 +1184,7 @@
     pc_here[1:] = dkv[...].T.astype(BF16).reshape(2, 64, 2048)
 
     def pc_out(k):
-        t = (m + k) % 16
+        t = ahead(z, y, k)
         return push(
             pc_here.at[:, :, lanes(t, 128)], pc_tok.at[:, m], b_send.at[0], b_recv.at[0], {"mp": t}
         )
@@ -1208,7 +1227,7 @@
             circle(p, d, 0, 0).start()
         hand_on(p, 0)
 
-    for p in range(3):
+    for p in range(2):
         spread_wait(p, 0)
         spread_start(p, 1)
     fifteen = o_mp.at[pl.ds(1, 15)]
@@ -1225,6 +1244,8 @@
     for p in (3, 4):
         spread_start(p, 0)
 
+    spread_wait(2, 0)
+    spread_start(2, 1)
     for p in range(3):
         circles(p)
     for p in (3, 4):
@@ -1518,9 +1539,9 @@
     slot_index,
     cotangent,
 ):
-    pairs = jnp.concatenate([routes.T, slot_index.T, jnp.zeros((4, 128), jnp.int32)]).astype(F32)
     (
         send,
+        pairs,
         middle,
         probs,
         ctx_tok,
@@ -1540,7 +1561,8 @@
         down_weight,
         moe_gain,
         router_weight,
-        pairs,
+        routes,
+        slot_index,
         cotangent,
         qkv_weight,
         out_weight,

time: 224 us -> 215 us (0.960)
  Pallas kernels: 222 us -> 214 us
    pallas_call x1, Pallas kernels: 154 us -> 148 us  [experts_back(): pl.pallas_call(experts_back_kernel, out_shape=(shape((128, 1024), BF16),...]
where the time goes in v7:
time: 215 us
  Pallas kernels  214 us (100%)
    pallas_call x1, Pallas kernels, experts_back(): pl.pallas_call(experts_back_kernel, out_shape=(shape((128, 1024), BF16),...  148 us
    pallas_call x1, Pallas kernels, attend(): pl.pallas_call(attend_kernel, out_shape=(shape((8, 2 * ROWS, 1024), BF16)...  54.7 us
    pallas_call x1, Pallas kernels, unfold(): pl.pallas_call(unfold_kernel, out_shape=(shape((1024, 3072), F32), shape(...  11.8 us

profile of v7, /device:TPU:1, one launch (start us, length us, event | category | flops | bytes accessed | tf_op | source)
XLA Modules:
  0.0 215.0 jit_solution(1404040475067186082)
XLA Ops:
  0.6 54.7 %shard_map.195 = (bf16[8,80,1024]{2,1,0:T(8,128)(2,1)}, f32[8,128]{1,0:T(8,128)}, f32[128,1024]{1,0:T(8,128)}, f32[128,8]{1,0:T(8,128)}, bf16[1024,128]{1,0:T(8,...) custom-call(bf16[128,1024]{1,0:T(8,128)(2,1)} %x_hbm.1, ...), custom_call_target="tpu_custom_call" | custom-call | tf_op jit(solution)/shard_map/pallas_call | solution.py:489
  55.3 147.7 %shard_map.196 = (bf16[128,1024]{1,0:T(8,128)(2,1)}, f32[128,1024]{1,0:T(8,128)}, f32[1,1024]{1,0:T(1,128)}, bf16[4,3,176,256]{3,2,1,0:T(8,128)(2,1)}, f32[16,10...) custom-call(f32[128,1024]{1,0:T(8,128)} %get-tuple-element.39.mid_hbm, ...), custom_call_target="tpu_custom_call" | custom-call | tf_op jit(solution)/shard_map/pallas_call | solution.py:1359
  203.0 11.8 %shard_map.197 = (f32[1024,3072]{1,0:T(8,128)}, f32[1024,1024]{1,0:T(8,128)}, f32[4,176,256]{2,1,0:T(8,128)}, f32[4,176,256]{2,1,0:T(8,128)}, f32[4,176,256]{2,1...) custom-call(bf16[2,4,4,4,256,128]{5,4,3,2,1,0:T(8,128)(2,1)} %get-tu, ...), custom_call_target="tpu_custom_call" | custom-call | tf_op jit(solution)/shard_map/pallas_call | solution.py:1492

commit v8 on v7

--- a/solution.py
+++ b/solution.py
@@ -797,14 +797,13 @@
             {"dp": (x + d) % 4},
         )
 
+    each(1, 16, lambda k: dispatch(k).start())
     operands[0].wait()
     for d in (1, 3):
         down_fan(d, 0, x).start()
-    each(1, 16, lambda k: dispatch(k).start())
     own = local(send_hbm.at[expert_of(m)], recv.at[slot(0, 0)], 4)
     own.start()
     weights[2 * FFQ :, lanes(x, DB)] = down_ref[...]
-    own.wait()
 
     def finish(j):
         partials(j).wait_recv()
@@ -831,6 +830,10 @@
             @pl.when(k > 0)
             def _():
                 dispatch(k).wait_recv()
+
+            @pl.when(k == 0)
+            def _():
+                own.wait()
 
             forward(k).start()
 

time: 215 us -> 215 us (level)
  no operation moved by 1% of the time
where the time goes in v8:
time: 215 us
  Pallas kernels  214 us (100%)
    pallas_call x1, Pallas kernels, experts_back(): pl.pallas_call(experts_back_kernel, out_shape=(shape((128, 1024), BF16),...  148 us
    pallas_call x1, Pallas kernels, attend(): pl.pallas_call(attend_kernel, out_shape=(shape((8, 2 * ROWS, 1024), BF16)...  54.7 us
    pallas_call x1, Pallas kernels, unfold(): pl.pallas_call(unfold_kernel, out_shape=(shape((1024, 3072), F32), shape(...  11.8 us

profile of v8, /device:TPU:1, one launch (start us, length us, event | category | flops | bytes accessed | tf_op | source)
XLA Modules:
  0.0 215.0 jit_solution(17880100993277512869)
XLA Ops:
  0.6 54.7 %shard_map.195 = (bf16[8,80,1024]{2,1,0:T(8,128)(2,1)}, f32[8,128]{1,0:T(8,128)}, f32[128,1024]{1,0:T(8,128)}, f32[128,8]{1,0:T(8,128)}, bf16[1024,128]{1,0:T(8,...) custom-call(bf16[128,1024]{1,0:T(8,128)(2,1)} %x_hbm.1, ...), custom_call_target="tpu_custom_call" | custom-call | tf_op jit(solution)/shard_map/pallas_call | solution.py:489
  55.3 147.7 %shard_map.196 = (bf16[128,1024]{1,0:T(8,128)(2,1)}, f32[128,1024]{1,0:T(8,128)}, f32[1,1024]{1,0:T(1,128)}, bf16[4,3,176,256]{3,2,1,0:T(8,128)(2,1)}, f32[16,10...) custom-call(f32[128,1024]{1,0:T(8,128)} %get-tuple-element.39.mid_hbm, ...), custom_call_target="tpu_custom_call" | custom-call | tf_op jit(solution)/shard_map/pallas_call | solution.py:1362
  203.1 11.8 %shard_map.197 = (f32[1024,3072]{1,0:T(8,128)}, f32[1024,1024]{1,0:T(8,128)}, f32[4,176,256]{2,1,0:T(8,128)}, f32[4,176,256]{2,1,0:T(8,128)}, f32[4,176,256]{2,1...) custom-call(bf16[2,4,4,4,256,128]{5,4,3,2,1,0:T(8,128)(2,1)} %get-tu, ...), custom_call_target="tpu_custom_call" | custom-call | tf_op jit(solution)/shard_map/pallas_call | solution.py:1495
